TPU v7x, 32 devices: a whole 2x2x4 slice. The times are simulated.
32 devices in a mesh: pair: 8 (over z, x), aux: 4 (over y, core).
Axes of the slice: x: 2, y: 2, z: 4, core: 2. Of those that a mesh axis runs over, the one named last changes fastest.
Arguments:
- integrals: bfloat16 [3072, 8192], P(('aux', 'pair')), may hold values from -0.796875 to 0.796875
- metric: bfloat16 [3072, 3072], P('aux'), may hold values from -0.109375 to 0.109375
- occ_energy: float32 [8], replicated, may hold values from -1.5 to -0.3
- virt_energy: float32 [1024], replicated, may hold values from 0.3 to 3
- pair_table: int32 [16, 2], P('pair'), may hold values from 0 to 7, as said below
- pair_count: int32 [8], P('pair'), may hold values from 1 to 2, as said below
Outputs:
- grad_blocks: float32 [3072, 8192], P('aux', 'pair')
Inputs may be any that keep to these rules, and one draw needn't show every extreme that they name: `pair_table`: occupied indices of the batch; slots beyond an owner's count hold valid but unused indices. `pair_count`: some owner holds exactly 2 listed pairs.
All inputs are finite; a program needn't handle non-finite values.
Results may differ from a plain program's by a relative error of at most 0.0028.
Values may be sent and summed in bfloat16 or wider, within the bound.
No kernel may reach another device: no remote copies, remote signals or barrier semaphores. Data moves between devices by JAX's collectives and lax.ppermute only.
A program may use at most 128 MiB of HBM per device.

v0:
```python
import jax
import jax.numpy as jnp
from jax import lax
from jax.sharding import PartitionSpec as P


def add_row(gradient, row_values, index):
    current = lax.dynamic_index_in_dim(gradient, index, 1, keepdims=False)
    return lax.dynamic_update_index_in_dim(gradient, current + row_values, index, 1)


def on_device(integrals, metric, occ_energy, virt_energy, pair_table, pair_count):
    occ_total = occ_energy.shape[0]
    virt_total = virt_energy.shape[0]
    regrouped = lax.all_to_all(integrals, "pair", split_axis=1, concat_axis=0, tiled=True)
    slab = regrouped.shape[0]
    fitted = lax.psum_scatter(
        lax.dot_general(
            metric, regrouped, (((0,), (0,)), ((), ())), preferred_element_type=jnp.float32
        ),
        "aux",
        scatter_dimension=0,
        tiled=True,
    ).astype(jnp.bfloat16)
    gathered = lax.all_gather(fitted, "pair", axis=1, tiled=True)
    blocks = gathered.reshape(slab, occ_total, virt_total)
    rounds = pair_table.shape[0]
    own_count = pair_count[0]

    def pick(slot):
        valid = (slot < own_count).astype(jnp.float32)
        return (pair_table[slot, 0], pair_table[slot, 1], valid)

    def visit(slot, gradient):
        occ_left, occ_right, valid = pick(slot)
        left = lax.dynamic_index_in_dim(blocks, occ_left, 1, keepdims=False)
        right = lax.dynamic_index_in_dim(blocks, occ_right, 1, keepdims=False)
        partial_ints = lax.dot_general(
            left, right, (((0,), (0,)), ((), ())), preferred_element_type=jnp.float32
        )
        shift_occ = occ_energy[occ_left] + occ_energy[occ_right]
        row_ints = lax.psum_scatter(partial_ints, "aux", scatter_dimension=0, tiled=True)
        row_total = row_ints.shape[0]
        row_energy = lax.dynamic_slice_in_dim(
            virt_energy, lax.axis_index("aux") * row_total, row_total
        )
        denominator = row_energy[:, None] + virt_energy[None, :] - shift_occ
        amp_part = (row_ints / denominator).astype(jnp.bfloat16)
        amplitude = lax.all_gather(amp_part, "aux", axis=0, tiled=True)
        to_left = (
            lax.dot_general(
                right, amplitude, (((1,), (1,)), ((), ())), preferred_element_type=jnp.float32
            )
            * valid
        )
        to_right = jnp.dot(left, amplitude, preferred_element_type=jnp.float32) * valid
        gradient = add_row(gradient, to_left, occ_left)
        return add_row(gradient, to_right, occ_right)

    gradient = lax.fori_loop(
        0, rounds, visit, jnp.zeros((slab, occ_total, virt_total), jnp.float32)
    )
    return lax.psum_scatter(
        gradient.reshape(slab, occ_total * virt_total), "pair", scatter_dimension=1, tiled=True
    )


def solution(mesh):
    placed = (P(("aux", "pair"), None), P("aux", None), P(), P(), P("pair", None), P("pair"))
    return jax.shard_map(
        on_device, mesh=mesh, in_specs=placed, out_specs=P("aux", "pair"), check_vma=False
    )
```

profile of v0, /device:TPU:0, one launch (start us, length us, event | category | flops | bytes accessed | tf_op | source)
XLA Modules:
  0.0 973.7 jit_solution(17034870877690770568)
XLA Ops:
  6.5 0.0 reduce-scatter.4.cloned.1.call-start
  6.5 0.0 copy-start.3
  6.5 1.7 copy.22
  8.2 44.2 %all_to_all.19 = bf16[96,8,1024]{2,0,1:T(8,128)(2,1)S(1)} all-to-all(bf16[96,8,1024]{2,0,1:T(8,128)(2,1)S(1)} %bitcast.73), channel_id=1, replica_groups=mesh['pair'=8,'aux'=4] {'pair'}, dimensions={1} | all-to-all | bytes 3145728 | tf_op jit(solution)/shard_map/all_to_all | solution.py:15
  52.4 0.0 copy-done.3
  52.4 8.0 fusion.13
  60.5 0.0 reduce-scatter.4.cloned.1.call-update
  60.5 0.0 all-gather.3.cloned.1.call-start
  60.5 98.2 %reduce-scatter.4.cloned.1.call-done = f32[768,1024]{1,0:T(8,128)} async-done(((f32[3072,1024]{1,0:T(8,128)}), f32[768,1024]{1,0:T(8,128)}) %reduce-scatter.4.cloned.1.call-update) | async-done | bytes 3145744 | tf_op jit(solution)/shard_map/reduce_scatter | solution.py:17
  158.7 3.3 convert_element_type.17
  162.0 0.0 all-gather.3.cloned.1.call-update
  162.0 176.6 %all-gather.3.cloned.1.call-done = bf16[768,8192]{1,0:T(8,128)(2,1)} async-done(((bf16[768,1024]{1,0:T(8,128)(2,1)}), bf16[768,8192]{1,0:T(8,128)(2,1)}) %all-gather.3.cloned.1.call-update) | async-done | bytes 12582928 | tf_op jit(solution)/shard_map/all_gather | solution.py:25
  338.6 10.7 %copy.21 = bf16[96,8,8,1024]{3,2,0,1:T(8,128)(2,1)} copy(bf16[96,8,8,1024]{3,2,1,0:T(8,128)(2,1)} %bitcast.72) | data formatting | bytes 25165824 | tf_op jit(solution)/shard_map/reshape | solution.py:26
  349.4 0.0 copy-start
  349.4 0.0 copy-start.1
  349.4 0.0 copy-start.2
  349.4 11.5 %broadcast_in_dim.24 = f32[768,8,1024]{2,0,1:T(8,128)} broadcast(f32[]{:T(128)} %constant.71.clone.1), dimensions={} | broadcast | bytes 25165828 | tf_op jit(solution)/shard_map/broadcast_in_dim | solution.py:61
  360.9 0.0 copy-done
  360.9 0.0 copy-done.1
  360.9 0.0 copy-done.2
  360.9 183.8 %while.13 = (s32[]{:T(128)}, f32[768,8,1024]{2,0,1:T(8,128)}, s32[2,2]{1,0:T(2,128)S(1)}, bf16[768,8,1024]{2,0,1:T(8,128)(2,1)}, f32[1024]{0:T(1024)S(1)}, /*ind...) while((s32[]{:T(128)}, f32[768,8,1024]{2,0,1:T(8,128)}, ...), condition=%wide.region_3.4_spmd, body=%wide.region_1.3_spmd.sunk | while | flops 4836032512 | bytes 73407976 | solution.py:60
  360.9 0.0 reduce-scatter.8.cloned.1.call-start
  361.0 0.6 constant_dynamic-slice_fusion.7
  365.4 5.7 fusion.32
  371.1 0.0 reduce-scatter.8.cloned.1.call-update
  371.1 0.0 all-gather.5.cloned.1.call-start
  371.1 0.1 dynamic_slice.106
  371.2 0.6 fusion.33
  373.1 40.8 %reduce-scatter.8.cloned.1.call-done = f32[256,1024]{1,0:T(8,128)} async-done(((f32[1024,1024]{1,0:T(8,128)}), f32[256,1024]{1,0:T(8,128)}) %reduce-scatter.8.cloned.1.call-update) | async-done | bytes 1048592 | tf_op jit(solution)/shard_map/while/body/eval_jaxpr/reduce_scatter | solution.py:42
  413.9 2.2 divide_convert_fusion.2
  416.2 0.0 all-gather.5.cloned.1.call-update
  416.8 2.1 constant_dynamic-slice_fusion.8
  419.0 20.0 %all-gather.5.cloned.1.call-done = bf16[1024,1024]{1,0:T(8,128)(2,1)} async-done(((bf16[256,1024]{1,0:T(8,128)(2,1)}), bf16[1024,1024]{1,0:T(8,128)(2,1)}) %all-gather.5.cloned.1.call-update) | async-done | bytes 2097168 | tf_op jit(solution)/shard_map/while/body/eval_jaxpr/all_gather | solution.py:49
  439.0 5.6 bitcast_dynamic-update-slice_fusion.4
  444.6 0.0 copy-start.4
  444.6 2.3 constant_dynamic-slice_fusion.9
  446.9 0.3 copy-done.4
  447.1 4.9 bitcast_dynamic-update-slice_fusion.5
  452.0 0.0 reduce-scatter.8.cloned.1.call-start
  452.0 0.6 constant_dynamic-slice_fusion.7
  456.4 5.7 fusion.32
  462.1 0.0 reduce-scatter.8.cloned.1.call-update
  462.1 0.0 all-gather.5.cloned.1.call-start
  462.2 0.1 dynamic_slice.106
  462.2 0.6 fusion.33
  464.1 42.6 %reduce-scatter.8.cloned.1.call-done = f32[256,1024]{1,0:T(8,128)} async-done(((f32[1024,1024]{1,0:T(8,128)}), f32[256,1024]{1,0:T(8,128)}) %reduce-scatter.8.cloned.1.call-update) | async-done | bytes 1048592 | tf_op jit(solution)/shard_map/while/body/eval_jaxpr/reduce_scatter | solution.py:42
  506.7 2.2 divide_convert_fusion.2
  509.0 0.0 all-gather.5.cloned.1.call-update
  509.6 2.1 constant_dynamic-slice_fusion.8
  511.8 20.0 %all-gather.5.cloned.1.call-done = bf16[1024,1024]{1,0:T(8,128)(2,1)} async-done(((bf16[256,1024]{1,0:T(8,128)(2,1)}), bf16[1024,1024]{1,0:T(8,128)(2,1)}) %all-gather.5.cloned.1.call-update) | async-done | bytes 2097168 | tf_op jit(solution)/shard_map/while/body/eval_jaxpr/all_gather | solution.py:49
  531.7 5.6 bitcast_dynamic-update-slice_fusion.4
  537.3 0.0 copy-start.4
  537.3 2.3 constant_dynamic-slice_fusion.9
  539.6 0.3 copy-done.4
  539.8 4.9 bitcast_dynamic-update-slice_fusion.5
  544.7 0.0 reduce-scatter.6.cloned.1.call-start
  544.7 17.6 %copy.18 = f32[8,96,8,1024]{3,2,0,1:T(8,128)} copy(f32[8,96,8,1024]{3,2,1,0:T(8,128)} %bitcast.69) | data formatting | bytes 50331648 | tf_op jit(solution)/shard_map/reshape | solution.py:64
  562.3 0.0 reduce-scatter.6.cloned.1.call-update
  562.3 404.6 %reduce-scatter.6.cloned.1.call-done = f32[768,1024]{1,0:T(8,128)} async-done(((f32[768,8192]{1,0:T(8,128)}), f32[768,1024]{1,0:T(8,128)}) %reduce-scatter.6.cloned.1.call-update) | async-done | bytes 3145744 | tf_op jit(solution)/shard_map/reduce_scatter | solution.py:63
Async XLA Ops:
  6.5 152.2 %reduce-scatter.4.cloned.1.call-start = ((), (), s32[]{:S(2)}) async-start(), calls=%async_computation.4 | async-start | bytes 15728640 | tf_op jit(solution)/shard_map/reduce_scatter | solution.py:17
  6.5 45.9 %copy-start.3 = (bf16[768,3072]{1,0:T(8,128)(2,1)S(1)}, bf16[768,3072]{1,0:T(8,128)(2,1)}, u32[]{:S(2)}) copy-start(bf16[768,3072]{1,0:T(8,128)(2,1)} %param.9) | copy-start | bytes 14155780
  60.5 278.1 %all-gather.3.cloned.1.call-start = ((), (), s32[]{:S(2)}) async-start(), calls=%async_computation.5 | async-start | bytes 14155776 | tf_op jit(solution)/shard_map/all_gather | solution.py:25
  349.4 11.5 %copy-start = (f32[1024]{0:T(1024)S(1)}, f32[1024]{0:T(1024)}, u32[]{:S(2)}) copy-start(f32[1024]{0:T(1024)} %param.11) | copy-start | bytes 12292
  349.4 11.5 %copy-start.1 = (f32[8]{0:T(128)S(1)}, f32[8]{0:T(128)}, u32[]{:S(2)}) copy-start(f32[8]{0:T(128)} %param.10) | copy-start | bytes 100
  349.4 11.5 %copy-start.2 = (s32[2,2]{1,0:T(2,128)S(1)}, s32[2,2]{1,0:T(2,128)}, u32[]{:S(2)}) copy-start(s32[2,2]{1,0:T(2,128)} %param.12) | copy-start | bytes 52
  360.9 53.0 %reduce-scatter.8.cloned.1.call-start = ((), (), s32[]{:S(2)}) async-start(), calls=%async_computation.7 | async-start | bytes 5242880 | tf_op jit(solution)/shard_map/while/body/eval_jaxpr/reduce_scatter | solution.py:42
  371.1 67.9 %all-gather.5.cloned.1.call-start = ((), (), s32[]{:S(2)}) async-start(), calls=%async_computation.8 | async-start | bytes 2621440 | tf_op jit(solution)/shard_map/while/body/eval_jaxpr/all_gather | solution.py:49
  444.6 2.5 copy-start.4
  452.0 54.7 %reduce-scatter.8.cloned.1.call-start = ((), (), s32[]{:S(2)}) async-start(), calls=%async_computation.7 | async-start | bytes 5242880 | tf_op jit(solution)/shard_map/while/body/eval_jaxpr/reduce_scatter | solution.py:42
  462.1 69.6 %all-gather.5.cloned.1.call-start = ((), (), s32[]{:S(2)}) async-start(), calls=%async_computation.8 | async-start | bytes 2621440 | tf_op jit(solution)/shard_map/while/body/eval_jaxpr/all_gather | solution.py:49
  537.3 2.5 copy-start.4
  544.7 422.2 %reduce-scatter.6.cloned.1.call-start = ((), (), s32[]{:S(2)}) async-start(), calls=%async_computation.6 | async-start | bytes 28311552 | tf_op jit(solution)/shard_map/reduce_scatter | solution.py:63
Sparse Core Ops, SparseCore 0:
  60.6 98.0 reduce-scatter.3
  162.2 176.4 all-gather.2
  371.2 42.6 reduce-scatter.7
  416.3 22.5 all-gather.4
  462.2 44.4 reduce-scatter.7
  509.1 22.5 all-gather.4
  562.4 404.4 reduce-scatter.5
where the time goes:
time: 974 us
  waiting for transfers between devices  803 us (82%)
  local copies, waits for them, and re-layouts  53.4 us (5%)
  blocking collectives  44.2 us (5%)
  matrix products  40.3 us (4%)
  between operations  13.4 us (1%)
  loops' own time  11.6 us (1%)
    reduce_scatter x1, waiting for transfers between devices, on_device(): lax.psum_scatter(gradient.reshape(slab, occ_total * virt_total), 'pair',...  405 us
    all_gather x1, waiting for transfers between devices, on_device(): gathered = lax.all_gather(fitted, 'pair', axis=1, tiled=True)  177 us
    reduce_scatter x1, waiting for transfers between devices, on_device(): lax.psum_scatter(lax.dot_general(metric, regrouped, (((0,), (0,)), ((), (...  98.2 us
    reduce_scatter x2, waiting for transfers between devices, visit(): lax.psum_scatter(partial_ints, 'aux', scatter_dimension=0, tiled=True)  83.4 us
    all_to_all x1, blocking collectives, on_device(): lax.all_to_all(integrals, 'pair', split_axis=1, concat_axis=0, tiled=True)  44.2 us
    all_gather x2, waiting for transfers between devices, visit(): amplitude = lax.all_gather(amp_part, 'aux', axis=0, tiled=True)  40 us
  transfers between devices with their start and end apart: 7, of which 7 were waited for; matrix products, arithmetic and copies ran while one was open for 1% of the time, Pallas kernels for 0%

commit v1 on v0

v1 whole, which is shorter than its diff:
```python
import functools

import jax
import jax.numpy as jnp
import numpy as np
from jax import lax
from jax.experimental import pallas as pl
from jax.experimental.pallas import tpu as pltpu
from jax.sharding import PartitionSpec as P

CORES = 2
RING = (0, 1, 3, 2)
CHUNKS = 2
VMEM = 56 * 1024 * 1024


class Layout:
    def __init__(self, mesh):
        self.n_pair = mesh.shape["pair"]
        self.n_aux = mesh.shape["aux"]
        self.nz = len(RING)
        self.nx = self.n_pair // self.nz
        self.ny = self.n_aux // CORES

    def pair_shift(self, s, t):
        return [
            (RING[r] * self.nx + x, RING[(r + s) % self.nz] * self.nx + (x + t) % self.nx)
            for r in range(self.nz)
            for x in range(self.nx)
        ]

    def y_shift(self, k):
        return [
            (y * CORES + c, (y + k) % self.ny * CORES + c)
            for y in range(self.ny)
            for c in range(CORES)
        ]

    def core_swap(self):
        return [(a, a ^ 1) for a in range(self.n_aux)]

    def inverse(self, g):
        return (-g[0] % self.nz, -g[1] % self.nx)

    def elements(self):
        return [(s, t) for s in range(self.nz) for t in range(self.nx)]


def to_pair(x, lay, s, t):
    return lax.ppermute(x, "pair", lay.pair_shift(s % lay.nz, t % lay.nx))


def to_y(x, lay, k):
    return lax.ppermute(x, "aux", lay.y_shift(k))


def to_core(x, lay):
    return lax.ppermute(x, "aux", lay.core_swap())


def products_kernel(entries, table, own, *rest):
    blocks, out = rest[:-1], rest[-1]
    w = own.shape[-1]

    def one(c, carry):
        i, j = table[0, c], table[1, c]
        for way, (l, r) in enumerate(((i, j), (j, i))):
            for e, (b, d) in enumerate(entries):
                if d == way:
                    out[c, e] = lax.dot_general(
                        own[l], blocks[b][r], (((0,), (0,)), ((), ())), preferred_element_type=jnp.float32
                    )
        return carry

    lax.fori_loop(0, table.shape[1], one, 0)


def products(table, own, blocks, entries):
    slots = table.shape[1]
    w = own.shape[-1]
    flops = 2 * slots * len(entries) * w * w * own.shape[1]
    vm = pl.BlockSpec(memory_space=pltpu.VMEM)
    return pl.pallas_call(
        functools.partial(products_kernel, entries),
        out_shape=jax.ShapeDtypeStruct((slots, len(entries), w, w), jnp.float32),
        in_specs=[pl.BlockSpec(memory_space=pltpu.SMEM)] + [vm] * (1 + len(blocks)),
        out_specs=vm,
        compiler_params=pltpu.CompilerParams(vmem_limit_bytes=VMEM),
        cost_estimate=pl.CostEstimate(flops=2 * flops, bytes_accessed=4 * slots * len(entries) * w * w, transcendentals=0),
        name="products",
    )(table, own, *blocks)


def gradient_kernel(where, n_blocks, table, *rest):
    blocks, weights = rest[:n_blocks], rest[n_blocks:-2]
    out, acc = rest[-2:]
    w = out.shape[-1]
    acc[...] = jnp.zeros_like(acc)

    def one(c, carry):
        i, j = table[0, c], table[1, c]
        for way, (l, r) in enumerate(((i, j), (j, i))):
            parts = [(blocks[b][r], weights[g][c, e]) for b, g, e in where[way]]
            if w % 128 == 0:
                parts = [(jnp.concatenate([x for x, _ in parts], axis=1), jnp.concatenate([y for _, y in parts], axis=0))]
            total = acc[l]
            for x, y in parts:
                total = total + jnp.dot(x, y, preferred_element_type=jnp.float32)
            acc[l] = total
        return carry

    lax.fori_loop(0, table.shape[1], one, 0)
    out[...] = acc[...].astype(out.dtype)


def gradient_of(table, blocks, weights, where):
    occ, rows, w = blocks[0].shape
    tile = 256 if rows % 256 == 0 else 128
    spec = pl.BlockSpec((occ, tile, w), lambda q: (0, q, 0))
    slots = table.shape[1]
    flops = 2 * 2 * slots * rows * w * w * len(blocks)
    return pl.pallas_call(
        functools.partial(gradient_kernel, where, len(blocks)),
        grid=(rows // tile,),
        out_shape=jax.ShapeDtypeStruct((occ, rows, w), jnp.bfloat16),
        in_specs=[pl.BlockSpec(memory_space=pltpu.SMEM)]
        + [spec] * len(blocks)
        + [pl.BlockSpec(memory_space=pltpu.VMEM)] * len(weights),
        out_specs=spec,
        scratch_shapes=[pltpu.VMEM((occ, tile, w), jnp.float32)],
        compiler_params=pltpu.CompilerParams(vmem_limit_bytes=VMEM),
        cost_estimate=pl.CostEstimate(flops=2 * flops, bytes_accessed=2 * occ * rows * w * len(blocks), transcendentals=0),
        name="gradient",
    )(table, *blocks, *weights)


def reduce_slots(x, lay, share):
    half = x.shape[0] // CORES
    x = x[:half] + to_core(x[half:], lay)
    total = x[:share]
    for k in range(1, lay.ny):
        total = total + to_y(x[k * share:(k + 1) * share], lay, k)
    return total


def gather_slots(x, lay):
    x = jnp.concatenate([x] + [to_y(x, lay, k) for k in range(1, lay.ny)], axis=0)
    return jnp.concatenate([x, to_core(x, lay)], axis=0)


def on_device(lay, integrals, metric, occ_energy, virt_energy, pair_table, pair_count):
    n_pair, n_aux, ny = lay.n_pair, lay.n_aux, lay.ny
    occ = occ_energy.shape[0]
    parts = n_pair // occ
    u = integrals.shape[1] // (n_pair * n_pair)
    w = parts * u
    slab = metric.shape[0]
    aux = lax.axis_index("aux")
    y, c = aux // CORES, aux % CORES
    pair = lax.axis_index("pair")
    z, x = pair // lay.nx, pair % lay.nx

    cap = pair_table.shape[0]
    listed = jnp.concatenate([pair_table, jnp.broadcast_to(pair_count, (cap, 1))], axis=1)
    listed = lax.all_gather(listed, "pair", axis=0, tiled=True)
    slots = listed.shape[0]
    share = slots // n_aux
    valid = jnp.arange(slots) % cap < listed[:, 2]
    grouped = listed[:, :2].reshape(n_aux, share, 2)

    def ordered(sign):
        owners = jnp.stack([(y + sign * k) % ny * CORES + (c ^ cc) for cc in range(CORES) for k in range(ny)])
        return grouped[owners].reshape(slots, 2).T

    scatter_table, gather_table = ordered(1), ordered(-1)
    mine = lax.dynamic_index_in_dim(grouped, aux, 0, keepdims=False)
    mine_valid = lax.dynamic_index_in_dim(valid.reshape(n_aux, share), aux, 0, keepdims=False)
    mine_shift = occ_energy[mine[:, 0]], occ_energy[mine[:, 1]]
    virt_of = virt_energy.reshape(parts, n_pair, u).transpose(1, 0, 2).reshape(n_pair, w)

    wide = slab * CORES

    def columns(k):
        return lax.dynamic_slice_in_dim(metric, (y + k) % ny * wide, wide, 1)

    near = jnp.concatenate([columns(0)] + [to_y(columns(k), lay, k) for k in range(1, ny)], axis=0)
    far = to_core(lax.dynamic_slice_in_dim(near, (1 - c) * slab, slab, 1), lay)
    near = lax.dynamic_slice_in_dim(near, c * slab, slab, 1)
    metric_t = jnp.concatenate([near, far], axis=0).T

    def fit(piece):
        wide_d = piece.shape[1] // (n_pair * u)
        got = lax.all_to_all(
            piece.reshape(piece.shape[0], wide_d, n_pair, u), "pair", split_axis=2, concat_axis=0, tiled=True
        ).reshape(slab, wide_d * u)
        got = jnp.concatenate([got] + [to_y(got, lay, k) for k in range(1, ny)], axis=0)
        got = jnp.concatenate([got, to_core(got, lay)], axis=0)
        fitted = jnp.dot(metric_t, got, preferred_element_type=jnp.float32).astype(jnp.bfloat16)
        return fitted.reshape(slab, wide_d // parts, w).transpose(1, 0, 2)

    cut = integrals.shape[1] // CHUNKS
    own = jnp.concatenate([fit(integrals[:, h * cut:(h + 1) * cut]) for h in range(CHUNKS)], axis=0)

    block = {(0, 0): own}
    for s in range(lay.nz):
        nxt = to_pair(block[s, 0], lay, 1, 0) if s + 1 < lay.nz else None
        for t in range(1, lay.nx):
            block[s, t] = to_pair(block[s, t - 1], lay, 0, 1)
        if nxt is not None:
            last = (s, lay.nx - 1)
            nxt, block[last] = lax.optimization_barrier((nxt, block[last]))
            block[s + 1, 0] = nxt

    firsts = [g for g in lay.elements() if g <= lay.inverse(g)]
    groups = [[g for g in firsts if g <= (1, 0)], [g for g in firsts if g > (1, 0)]]
    ring_at = jnp.asarray(np.argsort(RING))[z]
    own_virt = virt_of[pair]
    all_weights, place = [], ({}, {})
    for n_group, group in enumerate(groups):
        entries = []
        for b, g in enumerate(group):
            entries.append((b, 0))
            if g != lay.inverse(g):
                entries.append((b, 1))
        partial = products(scatter_table, own, [block[g] for g in group], tuple(entries))
        summed = reduce_slots(partial, lay, share)
        stack, keys = [], []
        for b, g in enumerate(group):
            source = jnp.asarray(RING)[(ring_at - g[0]) % lay.nz] * lay.nx + (x - g[1]) % lay.nx
            energy = own_virt[:, None] + virt_of[source][None, :]
            energy = energy[None] - mine_shift[0][:, None, None] - mine_shift[1][:, None, None]

            def amplitude(e):
                return jnp.where(mine_valid[:, None, None], summed[:, e] / energy, 0.0).astype(jnp.bfloat16)

            here = [amplitude(e) for e, (bb, _) in enumerate(entries) if bb == b]
            keys.append((g, 0))
            stack.append(here[0].transpose(0, 2, 1))
            back = lay.inverse(g)
            if g == (0, 0):
                keys.append((g, 1))
                stack.append(here[0])
            elif back == g:
                keys.append((g, 1))
                stack.append(to_pair(here[0], lay, -g[0], -g[1]))
            else:
                keys.append((g, 1))
                stack.append(here[1].transpose(0, 2, 1))
                got = to_pair(jnp.stack(here, axis=1), lay, -g[0], -g[1])
                keys += [(back, 1), (back, 0)]
                stack += [got[:, 0], got[:, 1]]
        all_weights.append(gather_slots(jnp.stack(stack, axis=1), lay))
        for e, (g, way) in enumerate(keys):
            place[way][g] = (n_group, e)

    order = lay.elements()
    where = tuple(tuple((b, *place[way][g]) for b, g in enumerate(order)) for way in (0, 1))
    gradient = gradient_of(gather_table, [block[g] for g in order], all_weights, where)
    gradient = gradient.reshape(occ, slab, parts, u).transpose(0, 2, 1, 3).reshape(n_pair, slab, u)
    home = lax.all_to_all(gradient, "pair", split_axis=0, concat_axis=0, tiled=True)
    return home.transpose(1, 0, 2).reshape(slab, n_pair * u).astype(jnp.float32)


def solution(mesh):
    placed = (P(("aux", "pair"), None), P("aux", None), P(), P(), P("pair", None), P("pair"))
    return jax.shard_map(
        functools.partial(on_device, Layout(mesh)), mesh=mesh, in_specs=placed, out_specs=P("aux", "pair"), check_vma=False
    )
```

time: 974 us -> 522 us (0.54)
  waiting for transfers between devices: 803 us -> 229 us
  Pallas kernels: 0 us -> 49.2 us
  blocking collectives: 44.2 us -> 86.7 us
  starting transfers between devices: 0.18 us -> 37.7 us
  other arithmetic: 7.76 us -> 36.8 us
  matrix products: 40.3 us -> 11.5 us
  loops' own time: 11.6 us -> 0 us
  local copies, waits for them, and re-layouts: 53.4 us -> 64.1 us
    reduce_scatter x4 -> x0, waiting for transfers between devices: 586 us -> none  [the longest x1 405 us: on_device(): lax.psum_scatter(gradient.reshape(slab, occ_total * virt_total), 'pair',...]
    all_gather x3 -> x0, waiting for transfers between devices: 217 us -> none  [the longest x1 177 us: on_device(): gathered = lax.all_gather(fitted, 'pair', axis=1, tiled=True)]
    ppermute x0 -> x26, waiting for transfers between devices: none -> 211 us  [the longest x7 112 us: to_y(): return lax.ppermute(x, 'aux', lay.y_shift(k))]
    pallas_call x0 -> x3, Pallas kernels: none -> 49.2 us  [the longest x1 26.4 us: gradient_of(): pl.pallas_call(functools.partial(gradient_kernel, where, len(blocks)), gr...]
    all_gather x0 -> x1, blocking collectives: none -> 45.4 us  [on_device(): listed = lax.all_gather(listed, 'pair', axis=0, tiled=True)]
    dot_general x7 -> x2, matrix products: 40.3 us -> 11.5 us  [fit(): jnp.dot(metric_t, got, preferred_element_type=jnp.float32)]
    ppermute x0 -> x26, starting transfers between devices: none -> 28.4 us  [the longest x12 17.9 us: to_pair(): return lax.ppermute(x, 'pair', lay.pair_shift(s % lay.nz, t % lay.nx))]
    reshape x2 -> x7, local copies, waits for them, and re-layouts: 28.3 us -> 5.73 us  [the longest x2 2.41 us: fit(): piece.reshape(piece.shape[0], wide_d, n_pair, u)]
  transfers between devices with their start and end apart: 7 -> 28, of which waited for: 7 -> 15; matrix products, arithmetic and copies ran while one was open for 1% -> 17% of each run, Pallas kernels for 0% -> 4%
where the time goes in v1:
time: 522 us; the launch traced here: 521 us
  waiting for transfers between devices  229 us (44%)
  blocking collectives  86.7 us (17%)
  local copies, waits for them, and re-layouts  64.1 us (12%)
  Pallas kernels  49.2 us (9%)
  starting transfers between devices  37.7 us (7%)
  other arithmetic  36.8 us (7%)
  matrix products  11.5 us (2%)
  between operations  6.37 us (1%)
    ppermute x7, waiting for transfers between devices, to_y(): return lax.ppermute(x, 'aux', lay.y_shift(k))  112 us
    ppermute x12, waiting for transfers between devices, to_pair(): return lax.ppermute(x, 'pair', lay.pair_shift(s % lay.nz, t % lay.nx))  99.4 us
    all_gather x1, blocking collectives, on_device(): listed = lax.all_gather(listed, 'pair', axis=0, tiled=True)  45.4 us
    all_to_all x1, blocking collectives, on_device(): lax.all_to_all(gradient, 'pair', split_axis=0, concat_axis=0, tiled=True)  41.3 us
    pallas_call x1, Pallas kernels, gradient_of(): pl.pallas_call(functools.partial(gradient_kernel, where, len(blocks)), gr...  26.4 us
    pallas_call x2, Pallas kernels, products(): pl.pallas_call(functools.partial(products_kernel, entries), out_shape=jax...  22.8 us
    unnamed x60, local copies, waits for them, and re-layouts  18.5 us
    ppermute x12, starting transfers between devices, to_pair(): return lax.ppermute(x, 'pair', lay.pair_shift(s % lay.nz, t % lay.nx))  17.9 us
  transfers between devices with their start and end apart: 28, of which 15 were waited for; matrix products, arithmetic and copies ran while one was open for 17% of the time, Pallas kernels for 4%

profile of v1, /device:TPU:0, one launch (start us, length us, event | category | flops | bytes accessed | tf_op | source)
XLA Modules:
  0.0 521.2 jit_solution(11907605381590401396)
XLA Ops:
  0.0 4.2 constant_dynamic-slice_fusion.9
  4.2 3.0 collective-permute-start
  9.5 5.8 %all-to-all-start = ((bf16[96,4,8,128]{3,1,0,2:T(4,128)(2,1)}), bf16[96,4,8,128]{3,1,0,2:T(4,128)(2,1)S(1)}, u32[]{:S(2)}, u32[]{:S(2)}) async-start(bf16[96,4,8,128]{3,1,0,2:T(4,128)(2,1)} %copy.104), calls=%async_computation | async-start | bytes 1572864 | tf_op jit(solution)/shard_map/all_to_all | solution.py:193
  17.8 17.5 %all-to-all-done = bf16[96,4,8,128]{3,1,0,2:T(4,128)(2,1)S(1)} async-done(((bf16[96,4,8,128]{3,1,0,2:T(4,128)(2,1)}), bf16[96,4,8,128]{3,1,0,2:T(4,128)(2,1)S(1)}, u32[]{:S(2)}, u32[]{:S(2)}) %all-to-all-start) | async-done | bytes 786464 | tf_op jit(solution)/shard_map/all_to_all | solution.py:193
  36.2 3.5 all-to-all-start.1
  39.8 2.1 copy.171
  42.4 17.1 %collective-permute-done = bf16[768,1536]{1,0:T(8,128)(2,1)} collective-permute-done((bf16[768,1536]{1,0:T(8,128)(2,1)}, bf16[768,1536]{1,0:T(8,128)(2,1)}, u32[]{:S(2)}, u32[]{:S(2)}) %collective-permute-start) | collective-permute-done | bytes 2359328 | tf_op jit(solution)/shard_map/ppermute | solution.py:54
  59.6 3.8 fusion.13
  63.5 2.1 collective-permute-start.4
  65.6 10.8 %collective-permute-done.2 = bf16[768,512]{1,0:T(8,128)(2,1)} collective-permute-done((bf16[768,512]{1,0:T(8,128)(2,1)}, bf16[768,512]{1,0:T(8,128)(2,1)}, u32[]{:S(2)}, u32[]{:S(2)}) %collective-permute-start.2) | collective-permute-done | bytes 786464 | tf_op jit(solution)/shard_map/ppermute | solution.py:54
  76.4 1.5 pad_maximum_fusion.7
  78.0 14.4 %collective-permute-done.4 = bf16[768,512]{1,0:T(8,128)(2,1)S(1)} collective-permute-done((bf16[768,512]{1,0:T(8,128)(2,1)S(1)}, bf16[768,512]{1,0:T(8,128)(2,1)S(1)}, u32[]{:S(2)}, u32[]{:S(2)}) %collective-permute-start.4) | collective-permute-done | bytes 786464 | tf_op jit(solution)/shard_map/ppermute | solution.py:54
  92.6 5.8 %fusion.17 = bf16[768,512]{0,1:T(8,128)(2,1)} fusion(bf16[1536,512]{1,0:T(8,128)(2,1)S(1)} %collective-permute-done.3, bf16[768,512]{1,0:T(8,128)(2,1)} %collective-permute-done.2, bf16[768,512]{1,0:T(8,128)(2,1)} %bitcast.179, bf16[1536,768]{1,0:T(8,128)(2,1)} %collective-permute-done.1, bf16[1536,768]{1,0:T(8,128)(2,1)S(1)} %copy-done.7), kind=kOutput, calls=%fused_computation.33 | convolution fusion | flops 2435186688 | bytes 8650752 | tf_op jit(solution)/shard_map/dot_general | solution.py:198
  98.4 1.5 copy.105
  99.9 5.7 %fusion.14 = bf16[768,512]{0,1:T(8,128)(2,1)S(1)} fusion(bf16[1536,512]{1,0:T(8,128)(2,1)} %collective-permute-done.5, bf16[768,512]{1,0:T(8,128)(2,1)} %copy-done.10, bf16[768,512]{1,0:T(8,128)(2,1)S(1)} %bitcast.189, bf16[1536,768]{1,0:T(8,128)(2,1)} %collective-permute-done.1, bf16[1536,768]{1,0:T(8,128)(2,1)} %get-tuple-element.19), kind=kOutput, calls=%fused_computation.32 | convolution fusion | flops 2435186688 | bytes 8650752 | tf_op jit(solution)/shard_map/dot_general | solution.py:198
  106.1 1.9 collective-permute-start.6
  108.0 1.5 collective-permute-start.7
  109.5 34.5 %collective-permute-done.6.rest_2_ = bf16[8,768,128]{2,1,0:T(8,128)(2,1)S(1)} collective-permute-done((bf16[8,768,128]{2,1,0:T(8,128)(2,1)S(1)}, bf16[8,768,128]{2,1,0:T(8,128)(2,1)S(1)}, u32[]{:S(2)}, u32[]{:S(2)}) %collective-permute-start.6) | collective-permute-done | bytes 1572896 | tf_op jit(solution)/shard_map/ppermute | solution.py:50
  144.4 2.6 collective-permute-start.8
  147.0 1.5 collective-permute-start.9
  148.5 32.6 %collective-permute-done.8.rest_1_.rest_4_ = bf16[8,768,128]{2,1,0:T(8,128)(2,1)} collective-permute-done((bf16[8,768,128]{2,1,0:T(8,128)(2,1)S(1)}, bf16[8,768,128]{2,1,0:T(8,128)(2,1)}, u32[]{:S(2)}, u32[]{:S(2)}) %collective-permute-start.8) | collective-permute-done | bytes 1572896 | tf_op jit(solution)/shard_map/ppermute | solution.py:50
  182.4 1.6 collective-permute-start.10
  183.9 1.5 collective-permute-start.11
  186.1 45.4 %all-gather = s32[8,2,3]{2,1,0:T(2,128)S(1)} all-gather(s32[1,2,3]{2,1,0:T(2,128)S(1)} %pad_bitcast_fusion), channel_id=1, replica_groups=mesh['pair'=8,'aux'=4] {'pair'}, dimensions={0}, use_global_device_ids=true | all-gather | bytes 216 | tf_op jit(solution)/shard_map/all_gather | solution.py:165
  233.5 11.4 %products.2 = f32[16,4,128,128]{3,2,1,0:T(8,128)} custom-call(s32[2,16]{1,0:T(2,128)} %bitcast.201, bf16[8,768,128]{2,1,0:T(8,128)(2,1)} %copy-done.9, bf16[8,768,128]{2,1,0:T(8,128)(2,1)} %copy-done.9, bf16[8,768,128]{2,1,0:T(8,128)(2,1)} %copy-done.19, bf16[8,768,128]{2,1,0:T(8,128)(2,1)} %copy-done.18), custom_call_target="tpu_custom_call" | custom-call | flops 3221225472 | bytes 4194304 | tf_op jit(solution)/shard_map/products/pallas_call | solution.py:83
  244.9 3.9 fusion.57
  248.8 3.0 copy.154
  251.8 11.4 %products.3 = f32[16,4,128,128]{3,2,1,0:T(8,128)} custom-call(s32[2,16]{1,0:T(2,128)} %bitcast.202, bf16[8,768,128]{2,1,0:T(8,128)(2,1)} %copy-done.9, bf16[8,768,128]{2,1,0:T(8,128)(2,1)} %copy-done.20, bf16[8,768,128]{2,1,0:T(8,128)(2,1)} %collective-permute-done.8.rest_1_.rest_4_, bf16[8,768,128]{2,1,0:T(8,128)(2,1)} %collective-permute-done.11.rest_2_.rest_5_), custom_call_target="tpu_custom_call" | custom-call | flops 3221225472 | bytes 4194304 | tf_op jit(solution)/shard_map/products/pallas_call | solution.py:83
  263.2 4.0 fusion.56
  267.2 1.5 copy.156
  276.9 1.8 copy.153
  278.7 2.5 add.315
  281.3 1.6 collective-permute-start.14
  284.1 1.7 broadcast_subtract_fusion
  285.8 2.5 copy_add_fusion
  291.8 1.8 copy.137
  296.0 11.5 %collective-permute-done.14 = f32[4,4,128,128]{2,3,0,1:T(8,128)} collective-permute-done((f32[4,4,128,128]{2,3,0,1:T(8,128)S(1)}, f32[4,4,128,128]{2,3,0,1:T(8,128)}, u32[]{:S(2)}, u32[]{:S(2)}) %collective-permute-start.14) | collective-permute-done | bytes 1048608 | tf_op jit(solution)/shard_map/ppermute | solution.py:54
  311.1 17.9 %collective-permute-done.20 = f32[4,4,128,128]{3,2,0,1:T(8,128)} collective-permute-done((f32[4,4,128,128]{3,2,0,1:T(8,128)}, f32[4,4,128,128]{3,2,0,1:T(8,128)}, u32[]{:S(2)}, u32[]{:S(2)}) %collective-permute-start.20) | collective-permute-done | bytes 1048608 | tf_op jit(solution)/shard_map/ppermute | solution.py:54
  329.0 1.7 slice_add_fusion
  333.6 2.1 fusion.22
  335.7 1.7 copy.144
  339.4 1.7 bitcast_dynamic-update-slice_fusion.5
  341.1 1.6 pad_maximum_fusion.15
  343.9 2.8 collective-permute-start.23
  346.6 1.7 copy.146
  348.3 1.7 pad_maximum_fusion.14
  350.0 1.7 collective-permute-start.16
  351.7 1.5 collective-permute-start.15
  353.3 3.7 collective-permute-done.15
  357.0 1.7 copy.125
  361.0 1.6 collective-permute-start.17
  366.1 21.1 %collective-permute-done.17 = bf16[4,8,128,128]{3,2,0,1:T(8,128)(2,1)S(1)} collective-permute-done((bf16[4,8,128,128]{3,2,0,1:T(8,128)(2,1)S(1)}, bf16[4,8,128,128]{3,2,0,1:T(8,128)(2,1)S(1)}, u32[]{:S(2)}, u32[]{:S(2)}) %collective-permute-start.17) | collective-permute-done | bytes 1048608 | tf_op jit(solution)/shard_map/ppermute | solution.py:54
  387.1 1.5 pad_maximum_fusion.5
  388.6 19.1 %collective-permute-done.24 = bf16[4,8,128,128]{3,2,1,0:T(8,128)(2,1)S(1)} collective-permute-done((bf16[4,8,128,128]{3,2,1,0:T(8,128)(2,1)S(1)}, bf16[4,8,128,128]{3,2,1,0:T(8,128)(2,1)S(1)}, u32[]{:S(2)}, u32[]{:S(2)}) %collective-permute-start.24) | collective-permute-done | bytes 1048608 | tf_op jit(solution)/shard_map/ppermute | solution.py:54
  408.7 1.5 pad_maximum_fusion.6
  410.3 1.5 collective-permute-start.12
  413.0 1.8 pad_maximum_fusion.1
  414.8 2.3 copy.147.rest_8_
  417.1 3.4 pad_maximum_fusion.2.rest_9_
  420.6 26.8 %collective-permute-done.12.rest_7_ = bf16[8,768,128]{2,1,0:T(8,128)(2,1)} collective-permute-done((bf16[8,768,128]{2,1,0:T(8,128)(2,1)}, bf16[8,768,128]{2,1,0:T(8,128)(2,1)}, u32[]{:S(2)}, u32[]{:S(2)}) %collective-permute-start.12) | collective-permute-done | bytes 1572896 | tf_op jit(solution)/shard_map/ppermute | solution.py:50
  447.4 26.4 %gradient.1 = bf16[8,768,128]{2,1,0:T(8,128)(2,1)} custom-call(s32[2,16]{1,0:T(2,128)} %bitcast.200, bf16[8,768,128]{2,1,0:T(8,128)(2,1)} %copy-done.9, bf16[8,768,128]{2,1,0:T(8,128)(2,1)} %copy-done.19, bf16[8,768,128]{2,1,0:T(8,128)(2,1)} %copy-done.18, bf16[8,768,128]{2,1,0:T(8,128)(2,1)} %copy-done.20, ...), custom_call_target="tpu_custom_call" | custom-call | flops 12884901888 | bytes 12582912 | tf_op jit(solution)/shard_map/gradient/pallas_call | solution.py:122
  473.8 41.3 %all_to_all.35 = bf16[8,768,128]{2,1,0:T(8,128)(2,1)S(1)} all-to-all(bf16[8,768,128]{2,1,0:T(8,128)(2,1)} %gradient.1), channel_id=1, replica_groups=mesh['pair'=8,'aux'=4] {'pair'}, dimensions={0} | all-to-all | bytes 3145728 | tf_op jit(solution)/shard_map/all_to_all | solution.py:260
  515.3 2.3 copy.148
  517.6 3.6 copy.149
  (132 shorter events, 39.1 us)
Async XLA Ops:
  0.0 283.5 %copy-start = (f32[8]{0:T(128)S(1)}, f32[8]{0:T(128)}, u32[]{:S(2)}) copy-start(f32[8]{0:T(128)} %param.15) | copy-start | bytes 100
  0.0 7.2 %copy-start.8 = (bf16[96,8192]{1,0:T(8,128)(2,1)S(1)}, bf16[96,8192]{1,0:T(8,128)(2,1)}, u32[]{:S(2)}) copy-start(bf16[96,8192]{1,0:T(8,128)(2,1)} %param.13) | copy-start | bytes 4718596
  4.2 55.4 %collective-permute-start = (bf16[768,1536]{1,0:T(8,128)(2,1)}, bf16[768,1536]{1,0:T(8,128)(2,1)}, u32[]{:S(2)}, u32[]{:S(2)}) collective-permute-start(bf16[768,1536]{1,0:T(8,128)(2,1)} %get-tuple-element.21), channel_id=1, source_target_pairs={{0,2},{1,3},{2,0},{3,1},{4,6},{5,7},{6,4},{7,5},{8,10},{9,11},{10,... | collective-permute-start | bytes 7077896 | tf_op jit(solution)/shard_map/ppermute | solution.py:54
  9.5 25.8 %all-to-all-start = ((bf16[96,4,8,128]{3,1,0,2:T(4,128)(2,1)}), bf16[96,4,8,128]{3,1,0,2:T(4,128)(2,1)S(1)}, u32[]{:S(2)}, u32[]{:S(2)}) async-start(bf16[96,4,8,128]{3,1,0,2:T(4,128)(2,1)} %copy.104), calls=%async_computation | async-start | bytes 1572864 | tf_op jit(solution)/shard_map/all_to_all | solution.py:193
  35.3 0.9 copy-start.6
  36.2 27.1 %all-to-all-start.1 = ((bf16[96,4,8,128]{3,1,0,2:T(4,128)(2,1)}), bf16[96,4,8,128]{3,1,0,2:T(4,128)(2,1)S(1)}, u32[]{:S(2)}, u32[]{:S(2)}) async-start(bf16[96,4,8,128]{3,1,0,2:T(4,128)(2,1)} %copy.106), calls=%async_computation.1 | async-start | bytes 1572864 | tf_op jit(solution)/shard_map/all_to_all | solution.py:193
  41.9 34.5 %collective-permute-start.2 = (bf16[768,512]{1,0:T(8,128)(2,1)}, bf16[768,512]{1,0:T(8,128)(2,1)}, u32[]{:S(2)}, u32[]{:S(2)}) collective-permute-start(bf16[768,512]{1,0:T(8,128)(2,1)} %bitcast.179), channel_id=1, source_target_pairs={{0,2},{1,3},{2,0},{3,1},{4,6},{5,7},{6,4},{7,5},{8,10},{9,11},{10,... | collective-permute-start | bytes 2359304 | tf_op jit(solution)/shard_map/ppermute | solution.py:54
  63.3 29.2 %collective-permute-start.1 = (bf16[1536,768]{1,0:T(8,128)(2,1)}, bf16[1536,768]{1,0:T(8,128)(2,1)}, u32[]{:S(2)}, u32[]{:S(2)}) collective-permute-start(bf16[1536,768]{1,0:T(8,128)(2,1)} %get-tuple-element.20), channel_id=1, source_target_pairs={{0,1},{1,0},{2,3},{3,2},{4,5},{5,4},{6,7},{7,6},{8,9},{9,8},{10,11... | collective-permute-start | bytes 7077896 | tf_op jit(solution)/shard_map/ppermute | solution.py:58
  63.5 28.9 %collective-permute-start.4 = (bf16[768,512]{1,0:T(8,128)(2,1)S(1)}, bf16[768,512]{1,0:T(8,128)(2,1)S(1)}, u32[]{:S(2)}, u32[]{:S(2)}) collective-permute-start(bf16[768,512]{1,0:T(8,128)(2,1)S(1)} %bitcast.187), channel_id=1, source_target_pairs={{0,2},{1,3},{2,0},{3,1},{4,6},{5,7},{6,4},{7,5},{8,10},{9,11},{10,... | collective-permute-start | bytes 2359304 | tf_op jit(solution)/shard_map/ppermute | solution.py:54
  77.9 14.7 %copy-start.7 = (bf16[1536,768]{1,0:T(8,128)(2,1)S(1)}, bf16[1536,768]{1,0:T(8,128)(2,1)}, u32[]{:S(2)}) copy-start(bf16[1536,768]{1,0:T(8,128)(2,1)} %get-tuple-element.19) | copy-start | bytes 7077892
  77.9 14.6 %collective-permute-start.3 = (bf16[1536,512]{1,0:T(8,128)(2,1)S(1)}, bf16[1536,512]{1,0:T(8,128)(2,1)S(1)}, u32[]{:S(2)}, u32[]{:S(2)}) collective-permute-start(bf16[1536,512]{1,0:T(8,128)(2,1)S(1)} %pad_maximum_fusion.7), channel_id=1, source_target_pairs={{0,1},{1,0},{2,3},{3,2},{4,5},{5,4},{6,7},{7,6},{8,9},{9,8},{10,11... | collective-permute-start | bytes 4718600 | tf_op jit(solution)/shard_map/ppermute | solution.py:58
  92.3 6.0 %copy-start.10 = (bf16[768,512]{1,0:T(8,128)(2,1)}, bf16[768,512]{1,0:T(8,128)(2,1)S(1)}, u32[]{:S(2)}) copy-start(bf16[768,512]{1,0:T(8,128)(2,1)S(1)} %collective-permute-done.4) | copy-start | bytes 2359300
  92.4 7.4 %collective-permute-start.5 = (bf16[1536,512]{1,0:T(8,128)(2,1)S(1)}, bf16[1536,512]{1,0:T(8,128)(2,1)}, u32[]{:S(2)}, u32[]{:S(2)}) collective-permute-start(bf16[1536,512]{1,0:T(8,128)(2,1)S(1)} %pad_maximum_fusion.8), channel_id=1, source_target_pairs={{0,1},{1,0},{2,3},{3,2},{4,5},{5,4},{6,7},{7,6},{8,9},{9,8},{10,11... | collective-permute-start | bytes 4718600 | tf_op jit(solution)/shard_map/ppermute | solution.py:58
  105.6 80.5 %copy-start.17 = (s32[2,2]{1,0:T(2,128)S(1)}, s32[2,2]{1,0:T(2,128)}, u32[]{:S(2)}) copy-start(s32[2,2]{1,0:T(2,128)} %param.17) | copy-start | bytes 52
  106.1 127.4 %copy-start.9 = (bf16[8,768,128]{2,1,0:T(8,128)(2,1)}, bf16[8,768,128]{2,1,0:T(8,128)(2,1)S(1)}, u32[]{:S(2)}) copy-start(bf16[8,768,128]{2,1,0:T(8,128)(2,1)S(1)} %pad_maximum_fusion.9.own.rest_0_) | copy-start | bytes 4718596
  106.1 37.8 %collective-permute-start.6 = (bf16[8,768,128]{2,1,0:T(8,128)(2,1)S(1)}, bf16[8,768,128]{2,1,0:T(8,128)(2,1)S(1)}, u32[]{:S(2)}, u32[]{:S(2)}) collective-permute-start(bf16[8,768,128]{2,1,0:T(8,128)(2,1)S(1)} %pad_maximum_fusion.9.own.rest_0_), channel_id=1, source_target_pairs={{0,8},{4,12},{8,24},{12,28},{24,16},{28,20},{16,0},{20,4},{1,9},{5... | collective-permute-start | bytes 4718600 | tf_op jit(solution)/shard_map/ppermute | solution.py:50
  108.0 36.4 %collective-permute-start.7 = (bf16[8,768,128]{2,1,0:T(8,128)(2,1)S(1)}, bf16[8,768,128]{2,1,0:T(8,128)(2,1)S(1)}, u32[]{:S(2)}, u32[]{:S(2)}) collective-permute-start(bf16[8,768,128]{2,1,0:T(8,128)(2,1)S(1)} %pad_maximum_fusion.9.own.rest_0_), channel_id=1, source_target_pairs={{0,4},{4,0},{8,12},{12,8},{24,28},{28,24},{16,20},{20,16},{1,5},{5... | collective-permute-start | bytes 4718600 | tf_op jit(solution)/shard_map/ppermute | solution.py:50
  144.0 89.5 %copy-start.18 = (bf16[8,768,128]{2,1,0:T(8,128)(2,1)}, bf16[8,768,128]{2,1,0:T(8,128)(2,1)S(1)}, u32[]{:S(2)}) copy-start(bf16[8,768,128]{2,1,0:T(8,128)(2,1)S(1)} %collective-permute-done.6.rest_2_) | copy-start | bytes 4718596
  144.4 37.9 %copy-start.19 = (bf16[8,768,128]{2,1,0:T(8,128)(2,1)}, bf16[8,768,128]{2,1,0:T(8,128)(2,1)S(1)}, u32[]{:S(2)}) copy-start(bf16[8,768,128]{2,1,0:T(8,128)(2,1)S(1)} %collective-permute-done.7.rest_1_) | copy-start | bytes 4718596
  144.4 36.7 %collective-permute-start.8 = (bf16[8,768,128]{2,1,0:T(8,128)(2,1)S(1)}, bf16[8,768,128]{2,1,0:T(8,128)(2,1)}, u32[]{:S(2)}, u32[]{:S(2)}) collective-permute-start(bf16[8,768,128]{2,1,0:T(8,128)(2,1)S(1)} %collective-permute-done.6.rest_2_), channel_id=1, source_target_pairs={{0,8},{4,12},{8,24},{12,28},{24,16},{28,20},{16,0},{20,4},{1,9},{5... | collective-permute-start | bytes 4718600 | tf_op jit(solution)/shard_map/ppermute | solution.py:50
  147.0 35.3 %collective-permute-start.9 = (bf16[8,768,128]{2,1,0:T(8,128)(2,1)S(1)}, bf16[8,768,128]{2,1,0:T(8,128)(2,1)S(1)}, u32[]{:S(2)}, u32[]{:S(2)}) collective-permute-start(bf16[8,768,128]{2,1,0:T(8,128)(2,1)S(1)} %collective-permute-done.6.rest_2_), channel_id=1, source_target_pairs={{0,4},{4,0},{8,12},{12,8},{24,28},{28,24},{16,20},{20,16},{1,5},{5... | collective-permute-start | bytes 4718600 | tf_op jit(solution)/shard_map/ppermute | solution.py:50
  182.4 1.6 copy-start.20
  182.4 69.4 %collective-permute-start.10 = (bf16[8,768,128]{2,1,0:T(8,128)(2,1)}, bf16[8,768,128]{2,1,0:T(8,128)(2,1)}, u32[]{:S(2)}, u32[]{:S(2)}) collective-permute-start(bf16[8,768,128]{2,1,0:T(8,128)(2,1)} %collective-permute-done.8.rest_1_.rest_4_), channel_id=1, source_target_pairs={{0,8},{4,12},{8,24},{12,28},{24,16},{28,20},{16,0},{20,4},{1,9},{5... | collective-permute-start | bytes 4718600 | tf_op jit(solution)/shard_map/ppermute | solution.py:50
  183.9 67.9 %collective-permute-start.11 = (bf16[8,768,128]{2,1,0:T(8,128)(2,1)}, bf16[8,768,128]{2,1,0:T(8,128)(2,1)}, u32[]{:S(2)}, u32[]{:S(2)}) collective-permute-start(bf16[8,768,128]{2,1,0:T(8,128)(2,1)} %collective-permute-done.8.rest_1_.rest_4_), channel_id=1, source_target_pairs={{0,4},{4,0},{8,12},{12,8},{24,28},{28,24},{16,20},{20,16},{1,5},{5... | collective-permute-start | bytes 4718600 | tf_op jit(solution)/shard_map/ppermute | solution.py:50
  251.8 26.9 %collective-permute-start.13 = (f32[8,4,128,128]{2,3,0,1:T(8,128)}, f32[8,4,128,128]{2,3,0,1:T(8,128)}, u32[]{:S(2)}, u32[]{:S(2)}) collective-permute-start(f32[8,4,128,128]{2,3,0,1:T(8,128)} %copy.154), channel_id=1, source_target_pairs={{0,1},{1,0},{2,3},{3,2},{4,5},{5,4},{6,7},{7,6},{8,9},{9,8},{10,11... | collective-permute-start | bytes 6291464 | tf_op jit(solution)/shard_map/ppermute | solution.py:58
  267.2 2.0 copy-start.14
  267.2 8.8 %copy-start.15 = (f32[1024]{0:T(1024)S(1)}, f32[1024]{0:T(1024)}, u32[]{:S(2)}) copy-start(f32[1024]{0:T(1024)} %param.16) | copy-start | bytes 12292
  268.7 17.1 %collective-permute-start.19 = (f32[8,4,128,128]{3,2,0,1:T(8,128)}, f32[8,4,128,128]{3,2,0,1:T(8,128)}, u32[]{:S(2)}, u32[]{:S(2)}) collective-permute-start(f32[8,4,128,128]{3,2,0,1:T(8,128)} %copy.156), channel_id=1, source_target_pairs={{0,1},{1,0},{2,3},{3,2},{4,5},{5,4},{6,7},{7,6},{8,9},{9,8},{10,11... | collective-permute-start | bytes 6291464 | tf_op jit(solution)/shard_map/ppermute | solution.py:58
  281.3 26.2 %collective-permute-start.14 = (f32[4,4,128,128]{2,3,0,1:T(8,128)S(1)}, f32[4,4,128,128]{2,3,0,1:T(8,128)}, u32[]{:S(2)}, u32[]{:S(2)}) collective-permute-start(f32[4,4,128,128]{2,3,0,1:T(8,128)S(1)} %slice.107), channel_id=1, source_target_pairs={{0,2},{1,3},{2,0},{3,1},{4,6},{5,7},{6,4},{7,5},{8,10},{9,11},{10,... | collective-permute-start | bytes 3145736 | tf_op jit(solution)/shard_map/ppermute | solution.py:54
  288.3 1.3 copy-start.2
  290.8 38.3 %collective-permute-start.20 = (f32[4,4,128,128]{3,2,0,1:T(8,128)}, f32[4,4,128,128]{3,2,0,1:T(8,128)}, u32[]{:S(2)}, u32[]{:S(2)}) collective-permute-start(f32[4,4,128,128]{3,2,0,1:T(8,128)} %slice.115), channel_id=1, source_target_pairs={{0,2},{1,3},{2,0},{3,1},{4,6},{5,7},{6,4},{7,5},{8,10},{9,11},{10,... | collective-permute-start | bytes 3145736 | tf_op jit(solution)/shard_map/ppermute | solution.py:54
  294.5 14.4 %copy-start.11 = (f32[128,128]{0,1:T(8,128)S(1)}, f32[128,128]{0,1:T(8,128)}, u32[]{:S(2)}) copy-start(f32[128,128]{0,1:T(8,128)} %get-tuple-element.55) | copy-start | bytes 196612
  330.7 1.0 copy-start.3
  335.7 27.9 %collective-permute-start.22 = (bf16[4,128,128]{2,1,0:T(8,128)(2,1)}, bf16[4,128,128]{2,1,0:T(8,128)(2,1)}, u32[]{:S(2)}, u32[]{:S(2)}) collective-permute-start(bf16[4,128,128]{2,1,0:T(8,128)(2,1)} %get-tuple-element.32), channel_id=1, source_target_pairs={{0,24},{4,28},{8,16},{12,20},{24,0},{28,4},{16,8},{20,12},{1,25},{... | collective-permute-start | bytes 393224 | tf_op jit(solution)/shard_map/ppermute | solution.py:50
  342.8 19.8 %collective-permute-start.21 = (bf16[4,2,128,128]{3,2,0,1:T(8,128)(2,1)}, bf16[4,2,128,128]{3,2,0,1:T(8,128)(2,1)}, u32[]{:S(2)}, u32[]{:S(2)}) collective-permute-start(bf16[4,2,128,128]{3,2,0,1:T(8,128)(2,1)} %pad_maximum_fusion.15), channel_id=1, source_target_pairs={{0,20},{4,16},{8,4},{12,0},{24,12},{28,8},{16,28},{20,24},{1,21},{... | collective-permute-start | bytes 786440 | tf_op jit(solution)/shard_map/ppermute | solution.py:50
  343.9 20.7 %collective-permute-start.23 = (bf16[4,128,128]{2,1,0:T(8,128)(2,1)}, bf16[4,128,128]{2,1,0:T(8,128)(2,1)}, u32[]{:S(2)}, u32[]{:S(2)}) collective-permute-start(bf16[4,128,128]{2,1,0:T(8,128)(2,1)} %get-tuple-element.31), channel_id=1, source_target_pairs={{0,28},{4,24},{8,20},{12,16},{24,4},{28,0},{16,12},{20,8},{1,29},{... | collective-permute-start | bytes 393224 | tf_op jit(solution)/shard_map/ppermute | solution.py:50
  350.0 10.0 %collective-permute-start.16 = (bf16[4,2,128,128]{3,2,0,1:T(8,128)(2,1)}, bf16[4,2,128,128]{3,2,0,1:T(8,128)(2,1)}, u32[]{:S(2)}, u32[]{:S(2)}) collective-permute-start(bf16[4,2,128,128]{3,2,0,1:T(8,128)(2,1)} %pad_maximum_fusion.14), channel_id=1, source_target_pairs={{0,16},{4,20},{8,0},{12,4},{24,8},{28,12},{16,24},{20,28},{1,17},{... | collective-permute-start | bytes 786440 | tf_op jit(solution)/shard_map/ppermute | solution.py:50
  351.7 5.3 %collective-permute-start.15 = (bf16[4,128,128]{1,2,0:T(8,128)(2,1)}, bf16[4,128,128]{1,2,0:T(8,128)(2,1)}, u32[]{:S(2)}, u32[]{:S(2)}) collective-permute-start(bf16[4,128,128]{1,2,0:T(8,128)(2,1)} %get-tuple-element.18), channel_id=1, source_target_pairs={{0,4},{4,0},{8,12},{12,8},{24,28},{28,24},{16,20},{20,16},{1,5},{5... | collective-permute-start | bytes 393224 | tf_op jit(solution)/shard_map/ppermute | solution.py:50
  353.3 10.2 %copy-start.12 = (bf16[4,1,128,128]{3,2,1,0:T(8,128)(2,1)S(1)}, bf16[4,1,128,128]{3,2,1,0:T(8,128)(2,1)}, u32[]{:S(2)}) copy-start(bf16[4,1,128,128]{3,2,1,0:T(8,128)(2,1)} %copy.144) | copy-start | bytes 393220
  353.3 11.2 %copy-start.13 = (bf16[4,1,128,128]{3,2,1,0:T(8,128)(2,1)S(1)}, bf16[4,1,128,128]{3,2,1,0:T(8,128)(2,1)}, u32[]{:S(2)}) copy-start(bf16[4,1,128,128]{3,2,1,0:T(8,128)(2,1)} %copy.146) | copy-start | bytes 393220
  361.0 26.2 %collective-permute-start.17 = (bf16[4,8,128,128]{3,2,0,1:T(8,128)(2,1)S(1)}, bf16[4,8,128,128]{3,2,0,1:T(8,128)(2,1)S(1)}, u32[]{:S(2)}, u32[]{:S(2)}) collective-permute-start(bf16[4,8,128,128]{3,2,0,1:T(8,128)(2,1)S(1)} %constant_dynamic-update-slice_fusion), channel_id=1, source_target_pairs={{0,2},{1,3},{2,0},{3,1},{4,6},{5,7},{6,4},{7,5},{8,10},{9,11},{10,... | collective-permute-start | bytes 3145736 | tf_op jit(solution)/shard_map/ppermute | solution.py:54
  365.5 42.2 %collective-permute-start.24 = (bf16[4,8,128,128]{3,2,1,0:T(8,128)(2,1)S(1)}, bf16[4,8,128,128]{3,2,1,0:T(8,128)(2,1)S(1)}, u32[]{:S(2)}, u32[]{:S(2)}) collective-permute-start(bf16[4,8,128,128]{3,2,1,0:T(8,128)(2,1)S(1)} %bitcast_dynamic-update-slice_fusion.7), channel_id=1, source_target_pairs={{0,2},{1,3},{2,0},{3,1},{4,6},{5,7},{6,4},{7,5},{8,10},{9,11},{10,... | collective-permute-start | bytes 3145736 | tf_op jit(solution)/shard_map/ppermute | solution.py:54
  388.6 23.1 %copy-start.16 = (s32[4]{0:T(128)S(1)}, s32[4]{0:T(128)}, u32[]{:S(2)}) copy-start(s32[4]{0:T(128)} %get-tuple-element.61) | copy-start | bytes 52
  388.6 24.4 %collective-permute-start.18 = (bf16[8,8,128,128]{3,2,0,1:T(8,128)(2,1)}, bf16[8,8,128,128]{3,2,0,1:T(8,128)(2,1)}, u32[]{:S(2)}, u32[]{:S(2)}) collective-permute-start(bf16[8,8,128,128]{3,2,0,1:T(8,128)(2,1)} %pad_maximum_fusion.5), channel_id=1, source_target_pairs={{0,1},{1,0},{2,3},{3,2},{4,5},{5,4},{6,7},{7,6},{8,9},{9,8},{10,11... | collective-permute-start | bytes 6291464 | tf_op jit(solution)/shard_map/ppermute | solution.py:58
  407.7 1.0 copy-start.4
  410.3 6.8 %collective-permute-start.25 = (bf16[8,8,128,128]{3,2,1,0:T(8,128)(2,1)}, bf16[8,8,128,128]{3,2,1,0:T(8,128)(2,1)}, u32[]{:S(2)}, u32[]{:S(2)}) collective-permute-start(bf16[8,8,128,128]{3,2,1,0:T(8,128)(2,1)} %pad_maximum_fusion.6), channel_id=1, source_target_pairs={{0,1},{1,0},{2,3},{3,2},{4,5},{5,4},{6,7},{7,6},{8,9},{9,8},{10,11... | collective-permute-start | bytes 6291464 | tf_op jit(solution)/shard_map/ppermute | solution.py:58
  410.3 37.1 %collective-permute-start.12 = (bf16[8,768,128]{2,1,0:T(8,128)(2,1)}, bf16[8,768,128]{2,1,0:T(8,128)(2,1)}, u32[]{:S(2)}, u32[]{:S(2)}) collective-permute-start(bf16[8,768,128]{2,1,0:T(8,128)(2,1)} %collective-permute-done.10.rest_6_), channel_id=1, source_target_pairs={{0,4},{4,0},{8,12},{12,8},{24,28},{28,24},{16,20},{20,16},{1,5},{5... | collective-permute-start | bytes 4718600 | tf_op jit(solution)/shard_map/ppermute | solution.py:50
  414.8 2.3 copy-start.5
  517.6 3.6 copy-start.1

commit v2 on v0

v2 whole, which is shorter than its diff:
```python
import functools

import jax
import jax.numpy as jnp
import numpy as np
from jax import lax
from jax.experimental import pallas as pl
from jax.experimental.pallas import tpu as pltpu
from jax.sharding import PartitionSpec as P

CORES = 2
RING = (0, 1, 3, 2)
HALVES = 2
HOME_CHUNKS = 1
PIECES = 2
EXTRA_ROWS = 16
VMEM = 56 * 1024 * 1024
F32 = jnp.float32
BF16 = jnp.bfloat16


class Layout:
    def __init__(self, mesh):
        self.n_pair = mesh.shape["pair"]
        self.n_aux = mesh.shape["aux"]
        self.nz = len(RING)
        self.nx = self.n_pair // self.nz
        self.ny = self.n_aux // CORES

    def pair_shift(self, s, t):
        return [
            (RING[r] * self.nx + x, RING[(r + s) % self.nz] * self.nx + (x + t) % self.nx)
            for r in range(self.nz)
            for x in range(self.nx)
        ]

    def y_shift(self, k, flip=0):
        return [
            (y * CORES + c, (y + k) % self.ny * CORES + (c ^ flip))
            for y in range(self.ny)
            for c in range(CORES)
        ]

    def core_swap(self):
        return [(a, a ^ 1) for a in range(self.n_aux)]

    def inverse(self, g):
        return (-g[0] % self.nz, -g[1] % self.nx)

    def elements(self):
        return [(s, t) for s in range(self.nz) for t in range(self.nx)]


def to_pair(x, lay, s, t):
    return lax.ppermute(x, "pair", lay.pair_shift(s % lay.nz, t % lay.nx))


def to_y(x, lay, k):
    return lax.ppermute(x, "aux", lay.y_shift(k))


def to_core(x, lay):
    return lax.ppermute(x, "aux", lay.core_swap())


def after(values, *done):
    return lax.optimization_barrier((tuple(values), done))[0]


WHOLE = pl.BlockSpec(memory_space=pltpu.VMEM)
SCALARS = pl.BlockSpec(memory_space=pltpu.SMEM)


def params():
    return pltpu.CompilerParams(vmem_limit_bytes=VMEM)


def cost(flops, moved):
    return pl.CostEstimate(flops=int(flops), bytes_accessed=int(moved), transcendentals=0)


def fit_kernel(places, starts, *rest):
    metrics, pieces, out = rest[:len(places)], rest[len(places):-1], rest[-1]
    w = out.shape[-1]
    total = None
    for metric, (source, start) in zip(metrics, places):
        depth = metric.shape[1]
        if start is None:
            piece = pieces[source][...]
        else:
            piece = pieces[source][pl.ds(pl.multiple_of(starts[start], depth), depth), :]
        term = jnp.dot(metric[...], piece, preferred_element_type=F32)
        total = term if total is None else total + term
    for i in range(out.shape[0]):
        out[i] = total[:, i * w:(i + 1) * w].astype(BF16)


def fit_more_kernel(places, so_far, *rest):
    del so_far
    fit_kernel(places, *rest)


def fit(metrics, places, starts, pieces, w, occ, part, so_far):
    rows = metrics[0].shape[0]
    wide = pieces[0].shape[1]
    depth = sum(metric.shape[1] for metric in metrics)
    tile = 256 if rows % 256 == 0 else 128
    given = [] if so_far is None else [so_far]
    return pl.pallas_call(
        functools.partial(fit_kernel if so_far is None else fit_more_kernel, places),
        grid=(rows // tile,),
        out_shape=jax.ShapeDtypeStruct((occ, rows, w), BF16),
        in_specs=[pl.BlockSpec(memory_space=pl.ANY)] * len(given)
        + [SCALARS]
        + [pl.BlockSpec((tile, metric.shape[1]), lambda q: (q, 0)) for metric in metrics]
        + [WHOLE] * len(pieces),
        out_specs=pl.BlockSpec((wide // w, tile, w), lambda q: (part, q, 0)),
        input_output_aliases={0: 0} if given else {},
        compiler_params=params(),
        cost_estimate=cost(2 * rows * depth * wide, 2 * (rows + wide) * depth),
        name="fit",
    )(*given, starts, *metrics, *pieces)


def spread(cat, blocks):
    w = blocks[0][0].shape[-1]
    for b, block in enumerate(blocks):
        at = 0
        for ref in block:
            n = ref.shape[0]
            cat[at:at + n, :, b * w:(b + 1) * w] = ref[...]
            at += n


def split(refs, counts):
    out, at = [], 0
    for n in counts:
        out.append(refs[at:at + n])
        at += n
    return out, refs[at:]


def products_kernel(n_blocks, n_both, n_chunks, table, own, *rest):
    blocks, chunks, (own_t, cat) = rest[:n_blocks], rest[n_blocks:n_blocks + n_chunks], rest[-2:]
    w = own_t.shape[1]
    spread(cat, [[ref] for ref in blocks])
    for i in range(own.shape[0]):
        own_t[i] = own[i].T
    for n, out in enumerate(chunks):
        share = out.shape[0]
        for c in range(share):
            i, j = table[0, n * share + c], table[1, n * share + c]
            first = jnp.dot(own_t[i], cat[j], preferred_element_type=F32)
            for e in range(n_blocks):
                out[c, e] = first[:, e * w:(e + 1) * w]
            if n_both > 0:
                second = jnp.dot(own_t[j], cat[i, :, :n_both * w], preferred_element_type=F32)
                for e in range(n_both):
                    out[c, n_blocks + e] = second[:, e * w:(e + 1) * w]


def products(table, n_chunks, own, blocks, n_both):
    slots = table.shape[1]
    occ, rows, w = own.shape
    entries = len(blocks) + n_both
    chunk = jax.ShapeDtypeStruct((slots // n_chunks, entries, w, w), F32)
    return pl.pallas_call(
        functools.partial(products_kernel, len(blocks), n_both, n_chunks),
        out_shape=(chunk,) * n_chunks,
        in_specs=[SCALARS] + [WHOLE] * (1 + len(blocks)),
        out_specs=(WHOLE,) * n_chunks,
        scratch_shapes=[pltpu.VMEM((occ, w, rows), BF16), pltpu.VMEM((occ, rows, len(blocks) * w), BF16)],
        compiler_params=params(),
        cost_estimate=cost(2 * slots * entries * w * w * rows, 4 * slots * entries * w * w),
        name="products",
    )(table, own, *blocks)


def amplitude_kernel(plan, n_terms, numbers, down, across, *rest):
    terms, weights, sent = rest[:n_terms], rest[n_terms], rest[n_terms + 1:]
    share = weights.shape[0]
    part = share // PIECES
    for s in range(share):
        left, right, live = numbers[0, s], numbers[1, s], numbers[2, s]
        for e, (block, flipped, plain, out, slot) in enumerate(plan):
            total = None
            for term in terms[s // part::PIECES]:
                value = term[s % part, e]
                total = value if total is None else total + value
            below = down[...] + across[block:block + 1, :] - left - right
            amp = jnp.where(live > 0, total / below, 0.0)
            weights[s, flipped] = amp.T.astype(BF16)
            if plain is not None:
                weights[s, plain] = amp.astype(BF16)
            if out is not None:
                sent[out][s, slot] = amp.astype(BF16)


def amplitudes(plan, numbers, down, across, terms, n_weights, sends):
    share, w = numbers.shape[1], terms[0].shape[-1]
    entries = len(plan)
    outs = [n_weights] + sends
    return pl.pallas_call(
        functools.partial(amplitude_kernel, plan, len(terms)),
        out_shape=tuple(jax.ShapeDtypeStruct((share, n, w, w), BF16) for n in outs),
        in_specs=[SCALARS] + [WHOLE] * (2 + len(terms)),
        out_specs=(WHOLE,) * len(outs),
        compiler_params=params(),
        cost_estimate=cost(share * entries * w * w * 10, share * entries * w * w * 8),
        name="amplitudes",
    )(numbers, down, across, *terms)


def gradient_kernel(where, counts, n_rounds, n_chunks, has_start, table, *rest):
    blocks, rest = split(rest, counts)
    rounds = [rest[g * n_chunks:(g + 1) * n_chunks] for g in range(n_rounds)]
    rest = rest[n_rounds * n_chunks:]
    if has_start:
        start, out, acc, cat = rest
        acc[...] = start[...]
    else:
        out, acc, cat = rest
        acc[...] = jnp.zeros_like(acc)
    w = out.shape[-1]
    spread(cat, blocks)
    share = rounds[0][0].shape[0]
    for chunk in range(n_chunks):

        for s in range(share):
            at = chunk * share + s
            i, j = table[0, at], table[1, at]
            for way, (l, r) in enumerate(((i, j), (j, i))):
                right = jnp.concatenate([rounds[g][chunk][s, e] for g, e in where[way]], axis=0)
                acc[l] += jnp.dot(cat[r], right, preferred_element_type=F32)
    out[...] = acc[...].astype(out.dtype)


def gradient(table, blocks, rounds, where, tile, first, tiles, start, kind):
    occ, rows, w = blocks[0][0].shape
    slots = table.shape[1]
    n_chunks = len(rounds[0])
    parts = [part for block in blocks for part in block]
    flat = [chunk for one in rounds for chunk in one]
    starts = [] if start is None else [start]
    return pl.pallas_call(
        functools.partial(
            gradient_kernel, where, [len(block) for block in blocks], len(rounds), n_chunks, start is not None
        ),
        grid=(tiles,),
        out_shape=jax.ShapeDtypeStruct((occ, tiles * tile, w), kind),
        in_specs=[SCALARS]
        + [pl.BlockSpec((part.shape[0], tile, w), lambda q: (0, q + first, 0)) for part in parts]
        + [WHOLE] * len(flat)
        + [pl.BlockSpec((occ, tile, w), lambda q: (0, q + first, 0))] * len(starts),
        out_specs=pl.BlockSpec((occ, tile, w), lambda q: (0, q, 0)),
        scratch_shapes=[pltpu.VMEM((occ, tile, w), F32), pltpu.VMEM((occ, tile, len(blocks) * w), BF16)],
        compiler_params=params(),
        cost_estimate=cost(4 * slots * tiles * tile * w * w * len(blocks), 2 * occ * tiles * tile * w * len(blocks)),
        name="gradient",
    )(table, *parts, *flat, *starts)


def arrange_kernel(given, out):
    u = given.shape[-1]
    for p in range(given.shape[0]):
        out[:, p * u:(p + 1) * u] = given[p].astype(F32)


def arrange(given):
    n, rows, u = given.shape
    tile = 128 if rows % 128 == 0 else rows
    return pl.pallas_call(
        arrange_kernel,
        grid=(rows // tile,),
        out_shape=jax.ShapeDtypeStruct((rows, n * u), F32),
        in_specs=[pl.BlockSpec((n, tile, u), lambda q: (0, q, 0))],
        out_specs=pl.BlockSpec((tile, n * u), lambda q: (q, 0)),
        compiler_params=params(),
        cost_estimate=cost(0, 6 * n * rows * u),
        name="arrange",
    )(given)


def gather_slots(x, lay):
    here = [x] + [to_y(x, lay, k) for k in range(1, lay.ny)]
    return here + [to_core(v, lay) for v in here]


def on_device(lay, integrals, metric, occ_energy, virt_energy, pair_table, pair_count):
    n_pair, n_aux, ny, nz, nx = lay.n_pair, lay.n_aux, lay.ny, lay.nz, lay.nx
    occ = occ_energy.shape[0]
    parts = n_pair // occ
    u = integrals.shape[1] // (n_pair * n_pair)
    w = parts * u
    slab = metric.shape[0]
    aux = lax.axis_index("aux")
    y, c = aux // CORES, aux % CORES
    pair = lax.axis_index("pair")
    z, x = pair // nx, pair % nx

    step = integrals.shape[1] // HALVES
    wide_d = step // (n_pair * u)
    rows = integrals.shape[0]

    def regroup(piece):
        got = lax.all_to_all(
            piece.reshape(piece.shape[0], wide_d, n_pair, u), "pair", split_axis=2, concat_axis=0, tiled=True
        )
        return got.reshape(slab // rows, piece.shape[0], wide_d * u)

    cap = pair_table.shape[0]
    slots = n_pair * cap
    listed = jnp.concatenate([pair_table.reshape(-1), pair_count]).astype(BF16)
    listed = jnp.pad(listed, (0, u - listed.shape[0]))
    listed = jnp.broadcast_to(listed, (EXTRA_ROWS, step // u, u)).reshape(EXTRA_ROWS, step)

    def slot_tables(listed):
        listed = listed.astype(jnp.int32)
        pairs = listed[:, :2 * cap].reshape(slots, 2)
        live = (jnp.arange(cap) < listed[:, 2 * cap:2 * cap + 1]).astype(jnp.int32).reshape(slots, 1)
        grouped = jnp.concatenate([pairs, live], axis=1).reshape(n_aux, share, 3)

        def ordered(sign):
            owners = jnp.stack([(y + sign * k) % ny * CORES + (c ^ cc) for cc in range(CORES) for k in range(ny)])
            return grouped[owners].reshape(slots, 3).T

        mine = lax.dynamic_index_in_dim(grouped, aux, 0, keepdims=False)
        numbers = jnp.stack([occ_energy[mine[:, 0]], occ_energy[mine[:, 1]], mine[:, 2].astype(F32)])
        return ordered(1), ordered(-1), numbers

    share = slots // n_aux
    ring_at = jnp.asarray(np.argsort(RING))[z]
    virt_of = virt_energy.reshape(parts, n_pair, u).transpose(1, 0, 2).reshape(n_pair, w)
    own_virt = virt_of[pair][:, None]

    def source(g):
        return jnp.asarray(RING)[(ring_at - g[0]) % nz] * nx + (x - g[1]) % nx

    across = {g: virt_of[source(g)] for g in lay.elements()}

    cut = slab // nx
    starts = jnp.stack([(x - t) % nx * cut for t in range(nx)])
    metrics, places = [], []

    def columns(k, cc):
        return ((y + k) % ny * CORES + (c ^ cc)) * slab

    metrics.append(lax.dynamic_slice_in_dim(metric, columns(0, 0), slab, 1).T)
    crossed = to_core(lax.dynamic_slice_in_dim(metric, columns(0, 1), slab, 1), lay)
    places += [(0, None), (ny, None)]
    parts_y = {}
    for k in range(1, ny):
        for cc in range(CORES):
            part = lax.dynamic_slice(metric, (x * cut, columns(k, cc)), (cut, slab))
            parts_y[k, cc] = part
    first, = after((jnp.concatenate([integrals[:, :step], listed], axis=0),), *parts_y.values())
    parts_y = {key: lax.ppermute(part, "aux", lay.y_shift(*key)) for key, part in parts_y.items()}
    first = regroup(first)
    scatter_table, gather_table, numbers = slot_tables(first[:, rows, :u])
    first = first[:, :rows].reshape(slab, -1)
    second, *arrived = after([integrals[:, step:], *parts_y.values()], first)
    second = regroup(second).reshape(slab, -1)
    swapped = []
    keys_y = list(parts_y)
    arrived = jnp.stack(arrived)
    for t in range(nx):
        if t > 0:
            arrived = to_pair(arrived, lay, 0, 1)
        swapped += [arrived[n] for n in range(len(keys_y))]
        places += [(cc * ny + k, t) for k, cc in keys_y]

    def from_aux(part):
        there = [part] + [to_y(part, lay, k) for k in range(1, ny)]
        return there + [to_core(v, lay) for v in there]

    there = from_aux(first)
    ready = after((second, crossed, scatter_table, gather_table, numbers, *across.values()), *there[:ny])
    second, crossed, scatter_table, gather_table, numbers = ready[:5]
    across = dict(zip(across, ready[5:]))
    metrics.append(crossed.T)
    metrics += [part.T for part in swapped]
    own = fit(metrics, tuple(places), starts, there, w, occ, 0, None)
    own = fit(metrics, tuple(places), starts, from_aux(second), w, occ, 1, own)

    block = {(0, 0): [own]}

    def ring(s, *done):
        here = block[s, 0][0]
        if s < nz - 1:
            if done:
                here, = after((here,), *done)
            block[s + 1, 0] = [to_pair(here, lay, 1, 0)]
            for t in range(1, nx):
                here = to_pair(here, lay, 0, 1)
                block[s, t] = [here]
            return [block[s + 1, 0][0]] + [block[s, t][0] for t in range(1, nx)]
        half = occ // HALVES
        here, other = after((here, block[s - 1, nx - 1][0]), *done)
        for t in range(1, nx - 1):
            here = to_pair(here, lay, 0, 1)
            block[s, t] = [here]
        block[s, nx - 1] = [to_pair(here[:half], lay, 0, 1), to_pair(other[half:], lay, 1, 0)]
        return block[s, nx - 1]

    firsts = [g for g in lay.elements() if g <= lay.inverse(g)]
    stages = [[] for _ in range(nz)]
    for s, t in firsts:
        stages[s if t == 0 else s + 1].append((s, t))
    last = nz - 1
    rounds, pending, place = [], [], ({}, {})

    def collect(values):
        for e, (g, way) in enumerate([key for _, keys in values for key in keys]):
            place[way][g] = (len(rounds), e)
        arrays = [v for v, _ in values]
        rounds.append(gather_slots(arrays[0] if len(arrays) == 1 else jnp.concatenate(arrays, axis=1), lay))

    def sums(n, *done):
        both = [g for g in stages[n] if g != lay.inverse(g) or n == last]
        stage = both + [g for g in stages[n] if g not in both]
        here, = after((own,), *done) if done else (own,)
        chunks = products(scatter_table, n_aux * PIECES, here, [block[g][0] for g in stage], len(both))
        got = [to_core(v, lay) for v in chunks[ny * PIECES:]]
        terms = [chunks[:PIECES], got[:PIECES]]
        for k in range(1, ny):
            there = slice(k * PIECES, (k + 1) * PIECES)
            terms.append([to_y(near + far, lay, k) for near, far in zip(chunks[there], got[there])])
        terms = [piece for term in terms for piece in term]
        return stage, both, terms

    def weigh(stage, both, terms):
        rows_of = jnp.stack([across[g] for g in stage])
        entries = [(b, 0) for b in range(len(stage))] + [(b, 1) for b in range(len(both))]
        keys = [(g, way) for g in stage for way in range(2 if g in both or g == (0, 0) else 1)]
        plan, sends, out_of = [], [], {}
        for b, way in entries:
            g = stage[b]
            flipped, plain, out, slot = keys.index((g, way)), None, None, None
            if g == (0, 0):
                plain = keys.index((g, 1))
            elif g not in both or lay.inverse(g) != g:
                if g not in out_of:
                    out_of[g] = len(sends)
                    sends.append(0)
                out = out_of[g]
                slot = sends[out]
                sends[out] += 1
            plan.append((b, flipped, plain, out, slot))
        weights, *sent = amplitudes(tuple(plan), numbers, own_virt, rows_of, terms, len(keys), sends)
        arrived = []
        for g, out in out_of.items():
            back = lay.inverse(g)
            value = to_pair(sent[out], lay, -g[0], -g[1])
            arrived.append((value, [(g, 1)] if back == g else [(back, 1), (back, 0)]))
        return (weights, keys), arrived

    def only(weights, which):
        values, keys = weights
        at = [e for e, (g, _) in enumerate(keys) if g in which]
        if len(at) == len(keys):
            return weights
        return values[:, at[0]:at[-1] + 1], [keys[e] for e in at]

    def part(which, tile, first, tiles, start, kind):
        used = sorted({place[way][g][0] for g in which for way in (0, 1)})
        where = tuple(tuple((used.index(place[way][g][0]), place[way][g][1]) for g in which) for way in (0, 1))
        return gradient(
            gather_table, [block[g] for g in which], [rounds[r] for r in used], where, tile, first, tiles, start, kind
        )

    moved = ring(0)
    weights0, _ = weigh(*sums(0))
    collect([weights0])
    moved = ring(1, *moved, *rounds[0])
    weights1, arrived1 = weigh(*sums(1))
    collect([weights1])
    moved = ring(2, *moved, *[v for v, _ in arrived1])
    stage2 = sums(2, weights1[0])
    collect(arrived1)
    weights2, arrived2 = weigh(*stage2)
    collect([only(weights2, stage2[1])])
    moved = ring(3, *moved, *rounds[1], *rounds[2], *[v for v, _ in arrived2])
    stage3 = sums(3, weights2[0])
    rest2 = [g for g in stage2[0] if g not in stage2[1]]
    collect(arrived2 + [only(weights2, rest2)])

    def there(g):
        return all(g in place[way] and place[way][g][0] <= 3 for way in (0, 1))

    early = [g for g in lay.elements() if there(g)]
    late = [g for g in lay.elements() if g not in early]
    total = part(early, slab // 2, 0, 2, None, F32)
    weights3, arrived3 = weigh(stage3[0], stage3[1], after(stage3[2], *moved, total))
    collect([weights3])
    if arrived3:
        collect(arrived3)
    tile = slab // HOME_CHUNKS
    home = []
    for q in range(HOME_CHUNKS):
        rows = part(late, tile, q, 1, total, BF16)
        rows = rows.reshape(occ, tile, parts, u).transpose(0, 2, 1, 3).reshape(n_pair, tile, u)
        rows = lax.all_to_all(rows, "pair", split_axis=0, concat_axis=0, tiled=True)
        home.append(rows)
    return arrange(home[0]) if len(home) == 1 else jnp.concatenate([arrange(rows) for rows in home], axis=0)


def solution(mesh):
    placed = (P(("aux", "pair"), None), P("aux", None), P(), P(), P("pair", None), P("pair"))
    return jax.shard_map(
        functools.partial(on_device, Layout(mesh)), mesh=mesh, in_specs=placed, out_specs=P("aux", "pair"), check_vma=False
    )
```

time: 974 us -> 363 us (0.37)
  waiting for transfers between devices: 803 us -> 124 us
  Pallas kernels: 0 us -> 79 us
  starting transfers between devices: 0.18 us -> 57.7 us
  matrix products: 40.3 us -> 0 us
  local copies, waits for them, and re-layouts: 53.4 us -> 37.3 us
  loops' own time: 11.6 us -> 0 us
    reduce_scatter x4 -> x0, waiting for transfers between devices: 586 us -> none  [the longest x1 405 us: on_device(): lax.psum_scatter(gradient.reshape(slab, occ_total * virt_total), 'pair',...]
    all_gather x3 -> x0, waiting for transfers between devices: 217 us -> none  [the longest x1 177 us: on_device(): gathered = lax.all_gather(fitted, 'pair', axis=1, tiled=True)]
    ppermute x0 -> x64, waiting for transfers between devices: none -> 105 us  [the longest x16 74.5 us: to_y(): return lax.ppermute(x, 'aux', lay.y_shift(k))]
    pallas_call x0 -> x13, Pallas kernels: none -> 79 us  [the longest x2 27 us: gradient(): pl.pallas_call(functools.partial(gradient_kernel, where, [len(block) for...]
    ppermute x0 -> x64, starting transfers between devices: none -> 46.2 us  [the longest x13 20.4 us: to_pair(): return lax.ppermute(x, 'pair', lay.pair_shift(s % lay.nz, t % lay.nx))]
    dot_general x7 -> x0, matrix products: 40.3 us -> none  [the longest x2 11.4 us: visit(): lax.dot_general(left, right, (((0,), (0,)), ((), ())), preferred_element_...]
    reshape x2 -> x6, local copies, waits for them, and re-layouts: 28.3 us -> 6.35 us  [the longest x1 2.47 us: regroup(): return got.reshape(slab // rows, piece.shape[0], wide_d * u)]
    all_to_all x0 -> x2, waiting for transfers between devices: none -> 18.6 us  [regroup(): lax.all_to_all(piece.reshape(piece.shape[0], wide_d, n_pair, u), 'pair',...]
  transfers between devices with their start and end apart: 7 -> 66, of which waited for: 7 -> 23; matrix products, arithmetic and copies ran while one was open for 1% -> 10% of each run, Pallas kernels for 0% -> 15%
where the time goes in v2:
time: 363 us; the launch traced here: 362 us
  waiting for transfers between devices  124 us (34%)
  Pallas kernels  79 us (22%)
  starting transfers between devices  57.7 us (16%)
  blocking collectives  45.6 us (13%)
  local copies, waits for them, and re-layouts  37.3 us (10%)
  other arithmetic  12 us (3%)
  between operations  6.38 us (2%)
    ppermute x16, waiting for transfers between devices, to_y(): return lax.ppermute(x, 'aux', lay.y_shift(k))  74.5 us
    all_to_all x1, blocking collectives, on_device(): rows = lax.all_to_all(rows, 'pair', split_axis=0, concat_axis=0, tiled=True)  45.6 us
    pallas_call x2, Pallas kernels, gradient(): pl.pallas_call(functools.partial(gradient_kernel, where, [len(block) for...  27 us
    ppermute x13, waiting for transfers between devices, to_pair(): return lax.ppermute(x, 'pair', lay.pair_shift(s % lay.nz, t % lay.nx))  24.8 us
    pallas_call x4, Pallas kernels, products(): pl.pallas_call(functools.partial(products_kernel, len(blocks), n_both, n_...  22.4 us
    ppermute x13, starting transfers between devices, to_pair(): return lax.ppermute(x, 'pair', lay.pair_shift(s % lay.nz, t % lay.nx))  20.4 us
    ppermute x16, starting transfers between devices, to_y(): return lax.ppermute(x, 'aux', lay.y_shift(k))  18.7 us
    all_to_all x2, waiting for transfers between devices, regroup(): lax.all_to_all(piece.reshape(piece.shape[0], wide_d, n_pair, u), 'pair',...  18.6 us
  transfers between devices with their start and end apart: 66, of which 23 were waited for; matrix products, arithmetic and copies ran while one was open for 10% of the time, Pallas kernels for 15%

profile of v2, /device:TPU:0, one launch (start us, length us, event | category | flops | bytes accessed | tf_op | source)
XLA Modules:
  0.0 362.0 jit_solution(12918073449295055578)
XLA Ops:
  0.0 1.3 fusion.14
  6.9 7.3 %all-to-all-start = ((bf16[112,4,8,128]{3,1,0,2:T(4,128)(2,1)}), bf16[112,4,8,128]{3,1,0,2:T(4,128)(2,1)}, u32[]{:S(2)}, u32[]{:S(2)}) async-start(bf16[112,4,8,128]{3,1,0,2:T(4,128)(2,1)} %copy.96), calls=%async_computation | async-start | bytes 1835008 | tf_op jit(solution)/shard_map/all_to_all | solution.py:306
  14.2 1.5 collective-permute-start
  15.7 1.8 constant_dynamic-slice_fusion.1
  17.5 1.5 copy.121
  27.2 1.5 fusion.13
  29.5 7.8 %all-to-all-done = bf16[112,4,8,128]{3,1,0,2:T(4,128)(2,1)} async-done(((bf16[112,4,8,128]{3,1,0,2:T(4,128)(2,1)}), bf16[112,4,8,128]{3,1,0,2:T(4,128)(2,1)}, u32[]{:S(2)}, u32[]{:S(2)}) %all-to-all-start) | async-done | bytes 917536 | tf_op jit(solution)/shard_map/all_to_all | solution.py:306
  37.3 2.5 reshape.410
  39.8 2.2 slice.68
  42.7 1.5 collective-permute-start.3
  45.6 4.2 %all-to-all-start.1 = ((bf16[96,4,8,128]{3,1,0,2:T(4,128)(2,1)}), bf16[96,4,8,128]{3,1,0,2:T(4,128)(2,1)}, u32[]{:S(2)}, u32[]{:S(2)}) async-start(bf16[96,4,8,128]{3,1,0,2:T(4,128)(2,1)} %copy.97), calls=%async_computation.1 | async-start | bytes 1572864 | tf_op jit(solution)/shard_map/all_to_all | solution.py:306
  51.0 1.9 collective-permute-start.4
  58.6 10.8 %all-to-all-done.1 = bf16[96,4,8,128]{3,1,0,2:T(4,128)(2,1)} async-done(((bf16[96,4,8,128]{3,1,0,2:T(4,128)(2,1)}), bf16[96,4,8,128]{3,1,0,2:T(4,128)(2,1)}, u32[]{:S(2)}, u32[]{:S(2)}) %all-to-all-start.1) | async-done | bytes 786464 | tf_op jit(solution)/shard_map/all_to_all | solution.py:306
  70.7 1.4 collective-permute-start.7
  72.6 16.0 %collective-permute-done.7.rest_8_ = bf16[768,512]{1,0:T(8,128)(2,1)} collective-permute-done((bf16[768,512]{1,0:T(8,128)(2,1)S(1)}, bf16[768,512]{1,0:T(8,128)(2,1)}, u32[]{:S(2)}, u32[]{:S(2)}) %collective-permute-start.7) | collective-permute-done | bytes 786464 | tf_op jit(solution)/shard_map/ppermute | solution.py:59
  88.6 1.4 copy.123
  90.7 2.4 slice_bitcast_fusion
  93.1 7.0 %fit.2.so_far = bf16[8,768,128]{2,1,0:T(8,128)(2,1)} custom-call(s32[2]{0:T(128)} %pad_add_fusion.3.starts.rest_0_, bf16[768,768]{1,0:T(8,128)(2,1)} %bitcast.83, bf16[768,768]{1,0:T(8,128)(2,1)} %bitcast.91, bf16[768,384]{1,0:T(8,128)(2,1)} %bitcast.86, bf16[768,384]{1,0:T(8,128)(2,1)} %bitcast.89, bf16[768,384]{1,0:T(8,128)(2,1)} %get-tuple-element.144.rest_4_.rest_5_, ...), custom_call_target="tpu_custom_call" | custom-call | flops 2415919104 | bytes 7864320 | tf_op jit(solution)/shard_map/fit/pallas_call | solution.py:109
  100.1 7.0 %fit.3.own.rest_0_ = bf16[8,768,128]{2,1,0:T(8,128)(2,1)} custom-call(bf16[8,768,128]{2,1,0:T(8,128)(2,1)} %fit.2.so_far, s32[2]{0:T(128)} %pad_add_fusion.3.starts.rest_0_, bf16[768,768]{1,0:T(8,128)(2,1)} %bitcast.84, bf16[768,768]{1,0:T(8,128)(2,1)} %bitcast.92, bf16[768,384]{1,0:T(8,128)(2,1)} %bitcast.87, ...), custom_call_target="tpu_custom_call", output_to_operand_aliasing={{}: (0, {})} | custom-call | flops 2415919104 | bytes 7864320 | tf_op jit(solution)/shard_map/fit/pallas_call | solution.py:109
  107.2 2.1 collective-permute-start.11
  109.3 4.1 %products.4 = (f32[2,1,128,128]{3,2,1,0:T(8,128)}, f32[2,1,128,128]{3,2,1,0:T(8,128)}, f32[2,1,128,128]{3,2,1,0:T(8,128)}, f32[2,1,128,128]{3,2,1,0:T(8,128)}, f...) custom-call(s32[3,16]{1,0:T(4,128)} %bitcast.100, ...), custom_call_target="tpu_custom_call" | custom-call | flops 402653184 | bytes 1048576 | tf_op jit(solution)/shard_map/products/pallas_call | solution.py:167
  116.1 1.6 collective-permute-start.17
  120.0 2.5 collective-permute-done.17.rest_5_
  122.5 2.3 collective-permute-done.15.rest_4_
  124.8 2.3 amplitudes.4.rest_5_
  127.1 1.5 collective-permute-start.18
  128.6 6.5 %collective-permute-done.18.rest_6_ = bf16[4,2,128,128]{3,2,1,0:T(8,128)(2,1)S(1)} collective-permute-done((bf16[4,2,128,128]{3,2,1,0:T(8,128)(2,1)}, bf16[4,2,128,128]{3,2,1,0:T(8,128)(2,1)S(1)}, u32[]{:S(2)}, u32[]{:S(2)}) %collective-permute-start.18) | collective-permute-done | bytes 262176 | tf_op jit(solution)/shard_map/ppermute | solution.py:59
  135.1 1.5 collective-permute-done.20.rest_8_
  136.6 8.5 %collective-permute-done.10.rest_0_.rest_2_ = bf16[8,768,128]{2,1,0:T(8,128)(2,1)S(1)} collective-permute-done((bf16[8,768,128]{2,1,0:T(8,128)(2,1)}, bf16[8,768,128]{2,1,0:T(8,128)(2,1)S(1)}, u32[]{:S(2)}, u32[]{:S(2)}) %collective-permute-start.10) | collective-permute-done | bytes 1572896 | tf_op jit(solution)/shard_map/ppermute | solution.py:55
  145.1 2.2 collective-permute-start.21
  147.4 1.7 collective-permute-start.22
  149.1 6.5 %products.5 = (f32[2,3,128,128]{3,2,1,0:T(8,128)}, f32[2,3,128,128]{3,2,1,0:T(8,128)}, f32[2,3,128,128]{3,2,1,0:T(8,128)}, f32[2,3,128,128]{3,2,1,0:T(8,128)}, f...) custom-call(s32[3,16]{1,0:T(4,128)} %bitcast.101, ...), custom_call_target="tpu_custom_call" | custom-call | flops 1207959552 | bytes 3145728 | tf_op jit(solution)/shard_map/products/pallas_call | solution.py:167
  156.2 1.3 collective-permute-done.27
  158.8 1.4 collective-permute-start.28
  162.6 8.2 %collective-permute-done.28.rest_5_ = f32[2,3,128,128]{3,2,1,0:T(8,128)S(1)} collective-permute-done((f32[2,3,128,128]{3,2,1,0:T(8,128)S(1)}, f32[2,3,128,128]{3,2,1,0:T(8,128)S(1)}, u32[]{:S(2)}, u32[]{:S(2)}) %collective-permute-start.28) | collective-permute-done | bytes 393248 | tf_op jit(solution)/shard_map/ppermute | solution.py:59
  170.8 7.9 %collective-permute-done.26.rest_4_ = f32[2,3,128,128]{3,2,1,0:T(8,128)S(1)} collective-permute-done((f32[2,3,128,128]{3,2,1,0:T(8,128)S(1)}, f32[2,3,128,128]{3,2,1,0:T(8,128)S(1)}, u32[]{:S(2)}, u32[]{:S(2)}) %collective-permute-start.26) | collective-permute-done | bytes 393248 | tf_op jit(solution)/shard_map/ppermute | solution.py:59
  179.4 3.0 amplitudes.5
  183.7 1.7 collective-permute-start.33
  185.4 3.4 collective-permute-done.30
  188.8 1.6 collective-permute-done.29
  192.0 6.5 %products.6 = (f32[2,3,128,128]{3,2,1,0:T(8,128)}, f32[2,3,128,128]{3,2,1,0:T(8,128)}, f32[2,3,128,128]{3,2,1,0:T(8,128)}, f32[2,3,128,128]{3,2,1,0:T(8,128)}, f...) custom-call(s32[3,16]{1,0:T(4,128)} %bitcast.102, ...), custom_call_target="tpu_custom_call" | custom-call | flops 1207959552 | bytes 3145728 | tf_op jit(solution)/shard_map/products/pallas_call | solution.py:167
  199.1 2.3 collective-permute-start.32
  202.7 1.4 collective-permute-start.44
  206.1 8.6 %collective-permute-done.44.rest_5_ = f32[2,3,128,128]{3,2,1,0:T(8,128)S(1)} collective-permute-done((f32[2,3,128,128]{3,2,1,0:T(8,128)S(1)}, f32[2,3,128,128]{3,2,1,0:T(8,128)S(1)}, u32[]{:S(2)}, u32[]{:S(2)}) %collective-permute-start.44) | collective-permute-done | bytes 393248 | tf_op jit(solution)/shard_map/ppermute | solution.py:59
  214.7 1.4 collective-permute-start.36
  216.1 7.1 %collective-permute-done.42.rest_4_ = f32[2,3,128,128]{3,2,1,0:T(8,128)S(1)} collective-permute-done((f32[2,3,128,128]{3,2,1,0:T(8,128)S(1)}, f32[2,3,128,128]{3,2,1,0:T(8,128)S(1)}, u32[]{:S(2)}, u32[]{:S(2)}) %collective-permute-start.42) | collective-permute-done | bytes 393248 | tf_op jit(solution)/shard_map/ppermute | solution.py:59
  223.9 3.0 amplitudes.6
  226.9 1.3 collective-permute-start.46
  228.2 2.8 collective-permute-done.36.rest_14_
  232.1 8.9 %collective-permute-done.46 = bf16[4,1,128,128]{3,2,1,0:T(8,128)(2,1)S(1)} collective-permute-done((bf16[4,1,128,128]{3,2,1,0:T(8,128)(2,1)}, bf16[4,1,128,128]{3,2,1,0:T(8,128)(2,1)S(1)}, u32[]{:S(2)}, u32[]{:S(2)}) %collective-permute-start.46) | collective-permute-done | bytes 131104 | tf_op jit(solution)/shard_map/ppermute | solution.py:55
  243.0 2.3 collective-permute-done.45
  245.3 1.4 collective-permute-start.58
  247.9 5.3 %products.7 = (f32[2,2,128,128]{3,2,1,0:T(8,128)}, f32[2,2,128,128]{3,2,1,0:T(8,128)}, f32[2,2,128,128]{3,2,1,0:T(8,128)}, f32[2,2,128,128]{3,2,1,0:T(8,128)}, f...) custom-call(s32[3,16]{1,0:T(4,128)} %bitcast.103, ...), custom_call_target="tpu_custom_call" | custom-call | flops 805306368 | bytes 2097152 | tf_op jit(solution)/shard_map/products/pallas_call | solution.py:167
  255.2 1.6 collective-permute-start.47
  256.8 4.5 %collective-permute-start.48 = (bf16[4,768,128]{2,1,0:T(8,128)(2,1)S(1)}, bf16[4,768,128]{2,1,0:T(8,128)(2,1)S(1)}, u32[]{:S(2)}, u32[]{:S(2)}) collective-permute-start(bf16[4,768,128]{2,1,0:T(8,128)(2,1)S(1)} %slice.57), channel_id=1, source_target_pairs={{0,8},{4,12},{8,24},{12,28},{24,16},{28,20},{16,0},{20,4},{1,9},{5... | collective-permute-start | bytes 2359304 | tf_op jit(solution)/shard_map/ppermute | solution.py:55
  263.0 4.9 %collective-permute-done.49.rest_5_ = bf16[4,4,128,128]{3,2,1,0:T(8,128)(2,1)S(1)} collective-permute-done((bf16[4,4,128,128]{3,2,1,0:T(8,128)(2,1)S(1)}, bf16[4,4,128,128]{3,2,1,0:T(8,128)(2,1)S(1)}, u32[]{:S(2)}, u32[]{:S(2)}) %collective-permute-start.49) | collective-permute-done | bytes 524320 | tf_op jit(solution)/shard_map/ppermute | solution.py:59
  268.5 1.4 collective-permute-start.55
  269.9 15.3 %gradient.2.rest_12_ = f32[8,768,128]{2,1,0:T(8,128)} custom-call(s32[3,16]{1,0:T(4,128)} %bitcast.106, bf16[8,768,128]{2,1,0:T(8,128)(2,1)} %fit.3.own.rest_0_, bf16[8,768,128]{2,1,0:T(8,128)(2,1)} %copy-done.5, bf16[8,768,128]{2,1,0:T(8,128)(2,1)} %copy-done.4, bf16[8,768,128]{2,1,0:T(8,128)(2,1)} %copy-done.6, bf16[8,768,128]{2,1,0:T(8,128)(2,1)} %copy-done.11, ...), custom_call_target="tpu_custom_call" | custom-call | flops 4026531840 | bytes 7864320 | tf_op jit(solution)/shard_map/gradient/pallas_call | solution.py:245
  286.6 2.5 amplitudes.7.rest_8_
  289.8 7.8 %collective-permute-done.61.rest_9_ = bf16[4,2,128,128]{3,2,1,0:T(8,128)(2,1)S(1)} collective-permute-done((bf16[4,2,128,128]{3,2,1,0:T(8,128)(2,1)}, bf16[4,2,128,128]{3,2,1,0:T(8,128)(2,1)S(1)}, u32[]{:S(2)}, u32[]{:S(2)}) %collective-permute-start.61) | collective-permute-done | bytes 262176 | tf_op jit(solution)/shard_map/ppermute | solution.py:59
  297.7 1.5 collective-permute-done.63.rest_11_
  299.9 11.6 %gradient.3 = bf16[8,768,128]{2,1,0:T(8,128)(2,1)} custom-call(s32[3,16]{1,0:T(4,128)} %bitcast.107, bf16[8,768,128]{2,1,0:T(8,128)(2,1)} %copy-done.7, bf16[8,768,128]{2,1,0:T(8,128)(2,1)} %copy-done.2, bf16[4,768,128]{2,1,0:T(8,128)(2,1)} %copy-done.18, bf16[4,768,128]{2,1,0:T(8,128)(2,1)} %copy-done.19, bf16[4,4,128,128]{3,2,1,0:T(8,128)(2,1)} %copy-done.14, ...), custom_call_target="tpu_custom_call" | custom-call | flops 2415919104 | bytes 4718592 | tf_op jit(solution)/shard_map/gradient/pallas_call | solution.py:245
  311.5 45.6 %all_to_all.35.given = bf16[8,768,128]{2,1,0:T(8,128)(2,1)} all-to-all(bf16[8,768,128]{2,1,0:T(8,128)(2,1)} %gradient.3), channel_id=1, replica_groups=mesh['pair'=8,'aux'=4] {'pair'}, dimensions={0} | all-to-all | bytes 3145728 | tf_op jit(solution)/shard_map/all_to_all | solution.py:502
  357.1 4.8 %arrange.1 = f32[768,1024]{1,0:T(8,128)} custom-call(bf16[8,768,128]{2,1,0:T(8,128)(2,1)} %all_to_all.35.given), custom_call_target="tpu_custom_call" | custom-call | bytes 4718592 | tf_op jit(solution)/shard_map/arrange/pallas_call | solution.py:272
  (284 shorter events, 49.0 us)
Async XLA Ops:
  6.9 30.4 %all-to-all-start = ((bf16[112,4,8,128]{3,1,0,2:T(4,128)(2,1)}), bf16[112,4,8,128]{3,1,0,2:T(4,128)(2,1)}, u32[]{:S(2)}, u32[]{:S(2)}) async-start(bf16[112,4,8,128]{3,1,0,2:T(4,128)(2,1)} %copy.96), calls=%async_computation | async-start | bytes 1835008 | tf_op jit(solution)/shard_map/all_to_all | solution.py:306
  14.2 30.0 %collective-permute-start = (bf16[384,768]{0,1:T(8,128)(2,1)}, bf16[384,768]{0,1:T(8,128)(2,1)S(1)}, u32[]{:S(2)}, u32[]{:S(2)}) collective-permute-start(bf16[384,768]{0,1:T(8,128)(2,1)} %copy.119), channel_id=1, source_target_pairs={{0,2},{1,3},{2,0},{3,1},{4,6},{5,7},{6,4},{7,5},{8,10},{9,11},{10,... | collective-permute-start | bytes 1769480 | tf_op jit(solution)/shard_map/ppermute | solution.py:357
  15.7 28.5 %collective-permute-start.1 = (bf16[384,768]{0,1:T(8,128)(2,1)}, bf16[384,768]{0,1:T(8,128)(2,1)S(1)}, u32[]{:S(2)}, u32[]{:S(2)}) collective-permute-start(bf16[384,768]{0,1:T(8,128)(2,1)} %copy.120), channel_id=1, source_target_pairs={{0,3},{1,2},{2,1},{3,0},{4,7},{5,6},{6,5},{7,4},{8,11},{9,10},{10,... | collective-permute-start | bytes 1769480 | tf_op jit(solution)/shard_map/ppermute | solution.py:357
  19.0 51.7 %collective-permute-start.2 = (bf16[768,768]{0,1:T(8,128)(2,1)}, bf16[768,768]{0,1:T(8,128)(2,1)S(1)}, u32[]{:S(2)}, u32[]{:S(2)}) collective-permute-start(bf16[768,768]{0,1:T(8,128)(2,1)} %copy.121), channel_id=1, source_target_pairs={{0,1},{1,0},{2,3},{3,2},{4,5},{5,4},{6,7},{7,6},{8,9},{9,8},{10,11... | collective-permute-start | bytes 3538952 | tf_op jit(solution)/shard_map/ppermute | solution.py:63
  42.7 28.0 %collective-permute-start.3 = (bf16[768,512]{1,0:T(8,128)(2,1)}, bf16[768,512]{1,0:T(8,128)(2,1)}, u32[]{:S(2)}, u32[]{:S(2)}) collective-permute-start(bf16[768,512]{1,0:T(8,128)(2,1)} %bitcast.3.rest_6_), channel_id=1, source_target_pairs={{0,2},{1,3},{2,0},{3,1},{4,6},{5,7},{6,4},{7,5},{8,10},{9,11},{10,... | collective-permute-start | bytes 2359304 | tf_op jit(solution)/shard_map/ppermute | solution.py:59
  45.6 23.8 %all-to-all-start.1 = ((bf16[96,4,8,128]{3,1,0,2:T(4,128)(2,1)}), bf16[96,4,8,128]{3,1,0,2:T(4,128)(2,1)}, u32[]{:S(2)}, u32[]{:S(2)}) async-start(bf16[96,4,8,128]{3,1,0,2:T(4,128)(2,1)} %copy.97), calls=%async_computation.1 | async-start | bytes 1572864 | tf_op jit(solution)/shard_map/all_to_all | solution.py:306
  51.0 39.7 %collective-permute-start.4 = (bf16[2,384,768]{1,2,0:T(8,128)(2,1)}, bf16[2,384,768]{1,2,0:T(8,128)(2,1)}, u32[]{:S(2)}, u32[]{:S(2)}) collective-permute-start(bf16[2,384,768]{1,2,0:T(8,128)(2,1)} %pad_maximum_fusion), channel_id=1, source_target_pairs={{0,4},{4,0},{8,12},{12,8},{24,28},{28,24},{16,20},{20,16},{1,5},{5... | collective-permute-start | bytes 3538952 | tf_op jit(solution)/shard_map/ppermute | solution.py:55
  70.7 17.9 %collective-permute-start.7 = (bf16[768,512]{1,0:T(8,128)(2,1)S(1)}, bf16[768,512]{1,0:T(8,128)(2,1)}, u32[]{:S(2)}, u32[]{:S(2)}) collective-permute-start(bf16[768,512]{1,0:T(8,128)(2,1)S(1)} %bitcast.97), channel_id=1, source_target_pairs={{0,2},{1,3},{2,0},{3,1},{4,6},{5,7},{6,4},{7,5},{8,10},{9,11},{10,... | collective-permute-start | bytes 2359304 | tf_op jit(solution)/shard_map/ppermute | solution.py:59
  72.1 21.0 %collective-permute-start.5 = (bf16[768,512]{1,0:T(8,128)(2,1)}, bf16[768,512]{1,0:T(8,128)(2,1)}, u32[]{:S(2)}, u32[]{:S(2)}) collective-permute-start(bf16[768,512]{1,0:T(8,128)(2,1)} %bitcast.3.rest_6_), channel_id=1, source_target_pairs={{0,1},{1,0},{2,3},{3,2},{4,5},{5,4},{6,7},{7,6},{8,9},{9,8},{10,11... | collective-permute-start | bytes 2359304 | tf_op jit(solution)/shard_map/ppermute | solution.py:63
  72.1 21.0 %collective-permute-start.6 = (bf16[768,512]{1,0:T(8,128)(2,1)}, bf16[768,512]{1,0:T(8,128)(2,1)}, u32[]{:S(2)}, u32[]{:S(2)}) collective-permute-start(bf16[768,512]{1,0:T(8,128)(2,1)} %collective-permute-done.3.rest_7_), channel_id=1, source_target_pairs={{0,1},{1,0},{2,3},{3,2},{4,5},{5,4},{6,7},{7,6},{8,9},{9,8},{10,11... | collective-permute-start | bytes 2359304 | tf_op jit(solution)/shard_map/ppermute | solution.py:63
  72.6 27.5 %collective-permute-start.8 = (bf16[768,512]{1,0:T(8,128)(2,1)S(1)}, bf16[768,512]{1,0:T(8,128)(2,1)}, u32[]{:S(2)}, u32[]{:S(2)}) collective-permute-start(bf16[768,512]{1,0:T(8,128)(2,1)S(1)} %bitcast.98), channel_id=1, source_target_pairs={{0,1},{1,0},{2,3},{3,2},{4,5},{5,4},{6,7},{7,6},{8,9},{9,8},{10,11... | collective-permute-start | bytes 2359304 | tf_op jit(solution)/shard_map/ppermute | solution.py:63
  88.6 11.5 %collective-permute-start.9 = (bf16[768,512]{1,0:T(8,128)(2,1)}, bf16[768,512]{1,0:T(8,128)(2,1)}, u32[]{:S(2)}, u32[]{:S(2)}) collective-permute-start(bf16[768,512]{1,0:T(8,128)(2,1)} %collective-permute-done.7.rest_8_), channel_id=1, source_target_pairs={{0,1},{1,0},{2,3},{3,2},{4,5},{5,4},{6,7},{7,6},{8,9},{9,8},{10,11... | collective-permute-start | bytes 2359304 | tf_op jit(solution)/shard_map/ppermute | solution.py:63
  107.1 38.0 %collective-permute-start.10 = (bf16[8,768,128]{2,1,0:T(8,128)(2,1)}, bf16[8,768,128]{2,1,0:T(8,128)(2,1)S(1)}, u32[]{:S(2)}, u32[]{:S(2)}) collective-permute-start(bf16[8,768,128]{2,1,0:T(8,128)(2,1)} %fit.3.own.rest_0_), channel_id=1, source_target_pairs={{0,8},{4,12},{8,24},{12,28},{24,16},{28,20},{16,0},{20,4},{1,9},{5... | collective-permute-start | bytes 4718600 | tf_op jit(solution)/shard_map/ppermute | solution.py:55
  107.2 37.9 %collective-permute-start.11 = (bf16[8,768,128]{2,1,0:T(8,128)(2,1)}, bf16[8,768,128]{2,1,0:T(8,128)(2,1)S(1)}, u32[]{:S(2)}, u32[]{:S(2)}) collective-permute-start(bf16[8,768,128]{2,1,0:T(8,128)(2,1)} %fit.3.own.rest_0_), channel_id=1, source_target_pairs={{0,4},{4,0},{8,12},{12,8},{24,28},{28,24},{16,20},{20,16},{1,5},{5... | collective-permute-start | bytes 4718600 | tf_op jit(solution)/shard_map/ppermute | solution.py:55
  113.4 1.6 collective-permute-start.16
  113.6 2.5 collective-permute-start.14
  113.9 4.7 %collective-permute-start.12 = (f32[2,1,128,128]{3,2,1,0:T(8,128)}, f32[2,1,128,128]{3,2,1,0:T(8,128)S(1)}, u32[]{:S(2)}, u32[]{:S(2)}) collective-permute-start(f32[2,1,128,128]{3,2,1,0:T(8,128)} %get-tuple-element.82), channel_id=1, source_target_pairs={{0,1},{1,0},{2,3},{3,2},{4,5},{5,4},{6,7},{7,6},{8,9},{9,8},{10,11... | collective-permute-start | bytes 393224 | tf_op jit(solution)/shard_map/ppermute | solution.py:63
  115.0 5.0 %collective-permute-start.13 = (f32[2,1,128,128]{3,2,1,0:T(8,128)}, f32[2,1,128,128]{3,2,1,0:T(8,128)}, u32[]{:S(2)}, u32[]{:S(2)}) collective-permute-start(f32[2,1,128,128]{3,2,1,0:T(8,128)} %get-tuple-element.83), channel_id=1, source_target_pairs={{0,1},{1,0},{2,3},{3,2},{4,5},{5,4},{6,7},{7,6},{8,9},{9,8},{10,11... | collective-permute-start | bytes 393224 | tf_op jit(solution)/shard_map/ppermute | solution.py:63
  116.1 6.4 %collective-permute-start.17 = (f32[2,1,128,128]{3,2,1,0:T(8,128)S(1)}, f32[2,1,128,128]{3,2,1,0:T(8,128)}, u32[]{:S(2)}, u32[]{:S(2)}) collective-permute-start(f32[2,1,128,128]{3,2,1,0:T(8,128)S(1)} %add.273), channel_id=1, source_target_pairs={{0,2},{1,3},{2,0},{3,1},{4,6},{5,7},{6,4},{7,5},{8,10},{9,11},{10,... | collective-permute-start | bytes 393224 | tf_op jit(solution)/shard_map/ppermute | solution.py:59
  118.7 6.2 %collective-permute-start.15 = (f32[2,1,128,128]{3,2,1,0:T(8,128)S(1)}, f32[2,1,128,128]{3,2,1,0:T(8,128)}, u32[]{:S(2)}, u32[]{:S(2)}) collective-permute-start(f32[2,1,128,128]{3,2,1,0:T(8,128)S(1)} %add.272), channel_id=1, source_target_pairs={{0,2},{1,3},{2,0},{3,1},{4,6},{5,7},{6,4},{7,5},{8,10},{9,11},{10,... | collective-permute-start | bytes 393224 | tf_op jit(solution)/shard_map/ppermute | solution.py:59
  127.1 8.0 %collective-permute-start.18 = (bf16[4,2,128,128]{3,2,1,0:T(8,128)(2,1)}, bf16[4,2,128,128]{3,2,1,0:T(8,128)(2,1)S(1)}, u32[]{:S(2)}, u32[]{:S(2)}) collective-permute-start(bf16[4,2,128,128]{3,2,1,0:T(8,128)(2,1)} %amplitudes.4.rest_5_), channel_id=1, source_target_pairs={{0,2},{1,3},{2,0},{3,1},{4,6},{5,7},{6,4},{7,5},{8,10},{9,11},{10,... | collective-permute-start | bytes 786440 | tf_op jit(solution)/shard_map/ppermute | solution.py:59
  128.6 6.5 %collective-permute-start.19 = (bf16[4,2,128,128]{3,2,1,0:T(8,128)(2,1)}, bf16[4,2,128,128]{3,2,1,0:T(8,128)(2,1)S(1)}, u32[]{:S(2)}, u32[]{:S(2)}) collective-permute-start(bf16[4,2,128,128]{3,2,1,0:T(8,128)(2,1)} %amplitudes.4.rest_5_), channel_id=1, source_target_pairs={{0,1},{1,0},{2,3},{3,2},{4,5},{5,4},{6,7},{7,6},{8,9},{9,8},{10,11... | collective-permute-start | bytes 786440 | tf_op jit(solution)/shard_map/ppermute | solution.py:63
  145.1 45.3 %collective-permute-start.21 = (bf16[8,768,128]{2,1,0:T(8,128)(2,1)S(1)}, bf16[8,768,128]{2,1,0:T(8,128)(2,1)S(1)}, u32[]{:S(2)}, u32[]{:S(2)}) collective-permute-start(bf16[8,768,128]{2,1,0:T(8,128)(2,1)S(1)} %collective-permute-done.10.rest_0_.rest_2_), channel_id=1, source_target_pairs={{0,8},{4,12},{8,24},{12,28},{24,16},{28,20},{16,0},{20,4},{1,9},{5... | collective-permute-start | bytes 4718600 | tf_op jit(solution)/shard_map/ppermute | solution.py:55
  147.4 43.1 %collective-permute-start.22 = (bf16[8,768,128]{2,1,0:T(8,128)(2,1)S(1)}, bf16[8,768,128]{2,1,0:T(8,128)(2,1)S(1)}, u32[]{:S(2)}, u32[]{:S(2)}) collective-permute-start(bf16[8,768,128]{2,1,0:T(8,128)(2,1)S(1)} %collective-permute-done.10.rest_0_.rest_2_), channel_id=1, source_target_pairs={{0,4},{4,0},{8,12},{12,8},{24,28},{28,24},{16,20},{20,16},{1,5},{5... | collective-permute-start | bytes 4718600 | tf_op jit(solution)/shard_map/ppermute | solution.py:55
  155.6 2.0 collective-permute-start.27
  155.7 3.1 collective-permute-start.25
  156.2 5.2 %collective-permute-start.23 = (f32[2,3,128,128]{3,2,1,0:T(8,128)}, f32[2,3,128,128]{3,2,1,0:T(8,128)S(1)}, u32[]{:S(2)}, u32[]{:S(2)}) collective-permute-start(f32[2,3,128,128]{3,2,1,0:T(8,128)} %get-tuple-element.93), channel_id=1, source_target_pairs={{0,1},{1,0},{2,3},{3,2},{4,5},{5,4},{6,7},{7,6},{8,9},{9,8},{10,11... | collective-permute-start | bytes 1179656 | tf_op jit(solution)/shard_map/ppermute | solution.py:63
  157.6 5.0 %collective-permute-start.24 = (f32[2,3,128,128]{3,2,1,0:T(8,128)}, f32[2,3,128,128]{3,2,1,0:T(8,128)S(1)}, u32[]{:S(2)}, u32[]{:S(2)}) collective-permute-start(f32[2,3,128,128]{3,2,1,0:T(8,128)} %get-tuple-element.94), channel_id=1, source_target_pairs={{0,1},{1,0},{2,3},{3,2},{4,5},{5,4},{6,7},{7,6},{8,9},{9,8},{10,11... | collective-permute-start | bytes 1179656 | tf_op jit(solution)/shard_map/ppermute | solution.py:63
  158.8 12.0 %collective-permute-start.28 = (f32[2,3,128,128]{3,2,1,0:T(8,128)S(1)}, f32[2,3,128,128]{3,2,1,0:T(8,128)S(1)}, u32[]{:S(2)}, u32[]{:S(2)}) collective-permute-start(f32[2,3,128,128]{3,2,1,0:T(8,128)S(1)} %add.275), channel_id=1, source_target_pairs={{0,2},{1,3},{2,0},{3,1},{4,6},{5,7},{6,4},{7,5},{8,10},{9,11},{10,... | collective-permute-start | bytes 1179656 | tf_op jit(solution)/shard_map/ppermute | solution.py:59
  161.3 17.4 %collective-permute-start.26 = (f32[2,3,128,128]{3,2,1,0:T(8,128)S(1)}, f32[2,3,128,128]{3,2,1,0:T(8,128)S(1)}, u32[]{:S(2)}, u32[]{:S(2)}) collective-permute-start(f32[2,3,128,128]{3,2,1,0:T(8,128)S(1)} %add.274), channel_id=1, source_target_pairs={{0,2},{1,3},{2,0},{3,1},{4,6},{5,7},{6,4},{7,5},{8,10},{9,11},{10,... | collective-permute-start | bytes 1179656 | tf_op jit(solution)/shard_map/ppermute | solution.py:59
  182.5 8.0 %collective-permute-start.29 = (bf16[4,2,128,128]{3,2,1,0:T(8,128)(2,1)}, bf16[4,2,128,128]{3,2,1,0:T(8,128)(2,1)S(1)}, u32[]{:S(2)}, u32[]{:S(2)}) collective-permute-start(bf16[4,2,128,128]{3,2,1,0:T(8,128)(2,1)} %get-tuple-element.99), channel_id=1, source_target_pairs={{0,16},{4,20},{8,0},{12,4},{24,8},{28,12},{16,24},{20,28},{1,17},{... | collective-permute-start | bytes 786440 | tf_op jit(solution)/shard_map/ppermute | solution.py:55
  183.7 5.2 %collective-permute-start.30 = (bf16[4,1,128,128]{3,2,1,0:T(8,128)(2,1)}, bf16[4,1,128,128]{3,2,1,0:T(8,128)(2,1)S(1)}, u32[]{:S(2)}, u32[]{:S(2)}) collective-permute-start(bf16[4,1,128,128]{3,2,1,0:T(8,128)(2,1)} %get-tuple-element.100), channel_id=1, source_target_pairs={{0,4},{4,0},{8,12},{12,8},{24,28},{28,24},{16,20},{20,16},{1,5},{5... | collective-permute-start | bytes 393224 | tf_op jit(solution)/shard_map/ppermute | solution.py:55
  183.7 15.4 %collective-permute-start.33 = (bf16[4,3,128,128]{3,2,1,0:T(8,128)(2,1)}, bf16[4,3,128,128]{3,2,1,0:T(8,128)(2,1)S(1)}, u32[]{:S(2)}, u32[]{:S(2)}) collective-permute-start(bf16[4,3,128,128]{3,2,1,0:T(8,128)(2,1)} %get-tuple-element.102.rest_9_), channel_id=1, source_target_pairs={{0,2},{1,3},{2,0},{3,1},{4,6},{5,7},{6,4},{7,5},{8,10},{9,11},{10,... | collective-permute-start | bytes 1179656 | tf_op jit(solution)/shard_map/ppermute | solution.py:59
  190.4 56.3 %collective-permute-start.31 = (bf16[8,768,128]{2,1,0:T(8,128)(2,1)S(1)}, bf16[8,768,128]{2,1,0:T(8,128)(2,1)S(1)}, u32[]{:S(2)}, u32[]{:S(2)}) collective-permute-start(bf16[8,768,128]{2,1,0:T(8,128)(2,1)S(1)} %collective-permute-done.21.rest_1_.rest_0_), channel_id=1, source_target_pairs={{0,4},{4,0},{8,12},{12,8},{24,28},{28,24},{16,20},{20,16},{1,5},{5... | collective-permute-start | bytes 4718600 | tf_op jit(solution)/shard_map/ppermute | solution.py:55
  198.5 2.9 collective-permute-start.43
  198.5 4.1 %collective-permute-start.41 = (f32[2,3,128,128]{3,2,1,0:T(8,128)}, f32[2,3,128,128]{3,2,1,0:T(8,128)S(1)}, u32[]{:S(2)}, u32[]{:S(2)}) collective-permute-start(f32[2,3,128,128]{3,2,1,0:T(8,128)} %get-tuple-element.111), channel_id=1, source_target_pairs={{0,1},{1,0},{2,3},{3,2},{4,5},{5,4},{6,7},{7,6},{8,9},{9,8},{10,11... | collective-permute-start | bytes 1179656 | tf_op jit(solution)/shard_map/ppermute | solution.py:63
  199.0 6.1 %collective-permute-start.39 = (f32[2,3,128,128]{3,2,1,0:T(8,128)}, f32[2,3,128,128]{3,2,1,0:T(8,128)S(1)}, u32[]{:S(2)}, u32[]{:S(2)}) collective-permute-start(f32[2,3,128,128]{3,2,1,0:T(8,128)} %get-tuple-element.108), channel_id=1, source_target_pairs={{0,1},{1,0},{2,3},{3,2},{4,5},{5,4},{6,7},{7,6},{8,9},{9,8},{10,11... | collective-permute-start | bytes 1179656 | tf_op jit(solution)/shard_map/ppermute | solution.py:63
  199.1 54.8 %collective-permute-start.32 = (bf16[8,768,128]{2,1,0:T(8,128)(2,1)}, bf16[8,768,128]{2,1,0:T(8,128)(2,1)S(1)}, u32[]{:S(2)}, u32[]{:S(2)}) collective-permute-start(bf16[8,768,128]{2,1,0:T(8,128)(2,1)} %copy-done.7), channel_id=1, source_target_pairs={{0,8},{4,12},{8,24},{12,28},{24,16},{28,20},{16,0},{20,4},{1,9},{5... | collective-permute-start | bytes 4718600 | tf_op jit(solution)/shard_map/ppermute | solution.py:55
  201.4 4.5 %collective-permute-start.40 = (f32[2,3,128,128]{3,2,1,0:T(8,128)}, f32[2,3,128,128]{3,2,1,0:T(8,128)S(1)}, u32[]{:S(2)}, u32[]{:S(2)}) collective-permute-start(f32[2,3,128,128]{3,2,1,0:T(8,128)} %get-tuple-element.109), channel_id=1, source_target_pairs={{0,1},{1,0},{2,3},{3,2},{4,5},{5,4},{6,7},{7,6},{8,9},{9,8},{10,11... | collective-permute-start | bytes 1179656 | tf_op jit(solution)/shard_map/ppermute | solution.py:63
  202.7 12.0 %collective-permute-start.44 = (f32[2,3,128,128]{3,2,1,0:T(8,128)S(1)}, f32[2,3,128,128]{3,2,1,0:T(8,128)S(1)}, u32[]{:S(2)}, u32[]{:S(2)}) collective-permute-start(f32[2,3,128,128]{3,2,1,0:T(8,128)S(1)} %add.277), channel_id=1, source_target_pairs={{0,2},{1,3},{2,0},{3,1},{4,6},{5,7},{6,4},{7,5},{8,10},{9,11},{10,... | collective-permute-start | bytes 1179656 | tf_op jit(solution)/shard_map/ppermute | solution.py:59
  205.2 17.9 %collective-permute-start.42 = (f32[2,3,128,128]{3,2,1,0:T(8,128)S(1)}, f32[2,3,128,128]{3,2,1,0:T(8,128)S(1)}, u32[]{:S(2)}, u32[]{:S(2)}) collective-permute-start(f32[2,3,128,128]{3,2,1,0:T(8,128)S(1)} %add.276), channel_id=1, source_target_pairs={{0,2},{1,3},{2,0},{3,1},{4,6},{5,7},{6,4},{7,5},{8,10},{9,11},{10,... | collective-permute-start | bytes 1179656 | tf_op jit(solution)/shard_map/ppermute | solution.py:59
  206.0 20.9 %collective-permute-start.34 = (bf16[4,3,128,128]{3,2,1,0:T(8,128)(2,1)S(1)}, bf16[4,3,128,128]{3,2,1,0:T(8,128)(2,1)S(1)}, u32[]{:S(2)}, u32[]{:S(2)}) collective-permute-start(bf16[4,3,128,128]{3,2,1,0:T(8,128)(2,1)S(1)} %copy-done.31), channel_id=1, source_target_pairs={{0,1},{1,0},{2,3},{3,2},{4,5},{5,4},{6,7},{7,6},{8,9},{9,8},{10,11... | collective-permute-start | bytes 1179656 | tf_op jit(solution)/shard_map/ppermute | solution.py:63
  214.7 16.3 %collective-permute-start.36 = (bf16[4,3,128,128]{3,2,1,0:T(8,128)(2,1)S(1)}, bf16[4,3,128,128]{3,2,1,0:T(8,128)(2,1)S(1)}, u32[]{:S(2)}, u32[]{:S(2)}) collective-permute-start(bf16[4,3,128,128]{3,2,1,0:T(8,128)(2,1)S(1)} %constant_dynamic-update-slice_fusion.rest_13_), channel_id=1, source_target_pairs={{0,2},{1,3},{2,0},{3,1},{4,6},{5,7},{6,4},{7,5},{8,10},{9,11},{10,... | collective-permute-start | bytes 1179656 | tf_op jit(solution)/shard_map/ppermute | solution.py:59
  223.1 8.9 %collective-permute-start.37 = (bf16[4,3,128,128]{3,2,1,0:T(8,128)(2,1)S(1)}, bf16[4,3,128,128]{3,2,1,0:T(8,128)(2,1)}, u32[]{:S(2)}, u32[]{:S(2)}) collective-permute-start(bf16[4,3,128,128]{3,2,1,0:T(8,128)(2,1)S(1)} %constant_dynamic-update-slice_fusion.rest_13_), channel_id=1, source_target_pairs={{0,1},{1,0},{2,3},{3,2},{4,5},{5,4},{6,7},{7,6},{8,9},{9,8},{10,11... | collective-permute-start | bytes 1179656 | tf_op jit(solution)/shard_map/ppermute | solution.py:63
  226.9 14.1 %collective-permute-start.46 = (bf16[4,1,128,128]{3,2,1,0:T(8,128)(2,1)}, bf16[4,1,128,128]{3,2,1,0:T(8,128)(2,1)S(1)}, u32[]{:S(2)}, u32[]{:S(2)}) collective-permute-start(bf16[4,1,128,128]{3,2,1,0:T(8,128)(2,1)} %get-tuple-element.115), channel_id=1, source_target_pairs={{0,24},{4,28},{8,16},{12,20},{24,0},{28,4},{16,8},{20,12},{1,25},{... | collective-permute-start | bytes 393224 | tf_op jit(solution)/shard_map/ppermute | solution.py:55
  231.0 14.3 %collective-permute-start.45 = (bf16[4,2,128,128]{3,2,1,0:T(8,128)(2,1)}, bf16[4,2,128,128]{3,2,1,0:T(8,128)(2,1)S(1)}, u32[]{:S(2)}, u32[]{:S(2)}) collective-permute-start(bf16[4,2,128,128]{3,2,1,0:T(8,128)(2,1)} %get-tuple-element.114), channel_id=1, source_target_pairs={{0,20},{4,16},{8,4},{12,0},{24,12},{28,8},{16,28},{20,24},{1,21},{... | collective-permute-start | bytes 786440 | tf_op jit(solution)/shard_map/ppermute | solution.py:55
  232.1 21.2 %collective-permute-start.35 = (bf16[4,3,128,128]{3,2,1,0:T(8,128)(2,1)S(1)}, bf16[4,3,128,128]{3,2,1,0:T(8,128)(2,1)S(1)}, u32[]{:S(2)}, u32[]{:S(2)}) collective-permute-start(bf16[4,3,128,128]{3,2,1,0:T(8,128)(2,1)S(1)} %collective-permute-done.33.rest_10_), channel_id=1, source_target_pairs={{0,1},{1,0},{2,3},{3,2},{4,5},{5,4},{6,7},{7,6},{8,9},{9,8},{10,11... | collective-permute-start | bytes 1179656 | tf_op jit(solution)/shard_map/ppermute | solution.py:63
  241.0 12.4 %collective-permute-start.38 = (bf16[4,3,128,128]{3,2,1,0:T(8,128)(2,1)S(1)}, bf16[4,3,128,128]{3,2,1,0:T(8,128)(2,1)S(1)}, u32[]{:S(2)}, u32[]{:S(2)}) collective-permute-start(bf16[4,3,128,128]{3,2,1,0:T(8,128)(2,1)S(1)} %collective-permute-done.36.rest_14_), channel_id=1, source_target_pairs={{0,1},{1,0},{2,3},{3,2},{4,5},{5,4},{6,7},{7,6},{8,9},{9,8},{10,11... | collective-permute-start | bytes 1179656 | tf_op jit(solution)/shard_map/ppermute | solution.py:63
  245.3 9.8 %collective-permute-start.58 = (bf16[4,2,128,128]{3,2,1,0:T(8,128)(2,1)S(1)}, bf16[4,2,128,128]{3,2,1,0:T(8,128)(2,1)S(1)}, u32[]{:S(2)}, u32[]{:S(2)}) collective-permute-start(bf16[4,2,128,128]{3,2,1,0:T(8,128)(2,1)S(1)} %slice.59.rest_17_), channel_id=1, source_target_pairs={{0,2},{1,3},{2,0},{3,1},{4,6},{5,7},{6,4},{7,5},{8,10},{9,11},{10,... | collective-permute-start | bytes 786440 | tf_op jit(solution)/shard_map/ppermute | solution.py:59
  246.7 10.1 %collective-permute-start.59 = (bf16[4,2,128,128]{3,2,1,0:T(8,128)(2,1)S(1)}, bf16[4,2,128,128]{3,2,1,0:T(8,128)(2,1)S(1)}, u32[]{:S(2)}, u32[]{:S(2)}) collective-permute-start(bf16[4,2,128,128]{3,2,1,0:T(8,128)(2,1)S(1)} %slice.59.rest_17_), channel_id=1, source_target_pairs={{0,1},{1,0},{2,3},{3,2},{4,5},{5,4},{6,7},{7,6},{8,9},{9,8},{10,11... | collective-permute-start | bytes 786440 | tf_op jit(solution)/shard_map/ppermute | solution.py:63
  253.3 8.0 %collective-permute-start.56 = (f32[2,2,128,128]{3,2,1,0:T(8,128)}, f32[2,2,128,128]{3,2,1,0:T(8,128)S(1)}, u32[]{:S(2)}, u32[]{:S(2)}) collective-permute-start(f32[2,2,128,128]{3,2,1,0:T(8,128)} %get-tuple-element.128), channel_id=1, source_target_pairs={{0,1},{1,0},{2,3},{3,2},{4,5},{5,4},{6,7},{7,6},{8,9},{9,8},{10,11... | collective-permute-start | bytes 786440 | tf_op jit(solution)/shard_map/ppermute | solution.py:63
  253.4 7.9 %collective-permute-start.54 = (f32[2,2,128,128]{3,2,1,0:T(8,128)}, f32[2,2,128,128]{3,2,1,0:T(8,128)S(1)}, u32[]{:S(2)}, u32[]{:S(2)}) collective-permute-start(f32[2,2,128,128]{3,2,1,0:T(8,128)} %get-tuple-element.126), channel_id=1, source_target_pairs={{0,1},{1,0},{2,3},{3,2},{4,5},{5,4},{6,7},{7,6},{8,9},{9,8},{10,11... | collective-permute-start | bytes 786440 | tf_op jit(solution)/shard_map/ppermute | solution.py:63
  253.9 13.9 %collective-permute-start.49 = (bf16[4,4,128,128]{3,2,1,0:T(8,128)(2,1)S(1)}, bf16[4,4,128,128]{3,2,1,0:T(8,128)(2,1)S(1)}, u32[]{:S(2)}, u32[]{:S(2)}) collective-permute-start(bf16[4,4,128,128]{3,2,1,0:T(8,128)(2,1)S(1)} %pad_maximum_fusion.2.rest_4_), channel_id=1, source_target_pairs={{0,2},{1,3},{2,0},{3,1},{4,6},{5,7},{6,4},{7,5},{8,10},{9,11},{10,... | collective-permute-start | bytes 1572872 | tf_op jit(solution)/shard_map/ppermute | solution.py:59
  255.2 30.8 %collective-permute-start.47 = (bf16[4,768,128]{2,1,0:T(8,128)(2,1)S(1)}, bf16[4,768,128]{2,1,0:T(8,128)(2,1)S(1)}, u32[]{:S(2)}, u32[]{:S(2)}) collective-permute-start(bf16[4,768,128]{2,1,0:T(8,128)(2,1)S(1)} %slice.56), channel_id=1, source_target_pairs={{0,4},{4,0},{8,12},{12,8},{24,28},{28,24},{16,20},{20,16},{1,5},{5... | collective-permute-start | bytes 2359304 | tf_op jit(solution)/shard_map/ppermute | solution.py:55
  256.8 29.2 %collective-permute-start.48 = (bf16[4,768,128]{2,1,0:T(8,128)(2,1)S(1)}, bf16[4,768,128]{2,1,0:T(8,128)(2,1)S(1)}, u32[]{:S(2)}, u32[]{:S(2)}) collective-permute-start(bf16[4,768,128]{2,1,0:T(8,128)(2,1)S(1)} %slice.57), channel_id=1, source_target_pairs={{0,8},{4,12},{8,24},{12,28},{24,16},{28,20},{16,0},{20,4},{1,9},{5... | collective-permute-start | bytes 2359304 | tf_op jit(solution)/shard_map/ppermute | solution.py:55
  261.3 1.5 collective-permute-start.60
  261.3 7.2 %collective-permute-start.52 = (f32[2,2,128,128]{3,2,1,0:T(8,128)S(1)}, f32[2,2,128,128]{3,2,1,0:T(8,128)S(1)}, u32[]{:S(2)}, u32[]{:S(2)}) collective-permute-start(f32[2,2,128,128]{3,2,1,0:T(8,128)S(1)} %copy-done.60), channel_id=1, source_target_pairs={{0,1},{1,0},{2,3},{3,2},{4,5},{5,4},{6,7},{7,6},{8,9},{9,8},{10,11... | collective-permute-start | bytes 786440 | tf_op jit(solution)/shard_map/ppermute | solution.py:63
  262.8 22.4 %collective-permute-start.53 = (f32[2,2,128,128]{3,2,1,0:T(8,128)S(1)}, f32[2,2,128,128]{3,2,1,0:T(8,128)S(1)}, u32[]{:S(2)}, u32[]{:S(2)}) collective-permute-start(f32[2,2,128,128]{3,2,1,0:T(8,128)S(1)} %copy-done.59), channel_id=1, source_target_pairs={{0,1},{1,0},{2,3},{3,2},{4,5},{5,4},{6,7},{7,6},{8,9},{9,8},{10,11... | collective-permute-start | bytes 786440 | tf_op jit(solution)/shard_map/ppermute | solution.py:63
  267.9 17.5 %collective-permute-start.57 = (f32[2,2,128,128]{3,2,1,0:T(8,128)S(1)}, f32[2,2,128,128]{3,2,1,0:T(8,128)S(1)}, u32[]{:S(2)}, u32[]{:S(2)}) collective-permute-start(f32[2,2,128,128]{3,2,1,0:T(8,128)S(1)} %add.279), channel_id=1, source_target_pairs={{0,2},{1,3},{2,0},{3,1},{4,6},{5,7},{6,4},{7,5},{8,10},{9,11},{10,... | collective-permute-start | bytes 786440 | tf_op jit(solution)/shard_map/ppermute | solution.py:59
  268.5 17.4 %collective-permute-start.55 = (f32[2,2,128,128]{3,2,1,0:T(8,128)S(1)}, f32[2,2,128,128]{3,2,1,0:T(8,128)S(1)}, u32[]{:S(2)}, u32[]{:S(2)}) collective-permute-start(f32[2,2,128,128]{3,2,1,0:T(8,128)S(1)} %add.278), channel_id=1, source_target_pairs={{0,2},{1,3},{2,0},{3,1},{4,6},{5,7},{6,4},{7,5},{8,10},{9,11},{10,... | collective-permute-start | bytes 786440 | tf_op jit(solution)/shard_map/ppermute | solution.py:59
  285.3 12.4 %collective-permute-start.50 = (bf16[4,4,128,128]{3,2,1,0:T(8,128)(2,1)S(1)}, bf16[4,4,128,128]{3,2,1,0:T(8,128)(2,1)S(1)}, u32[]{:S(2)}, u32[]{:S(2)}) collective-permute-start(bf16[4,4,128,128]{3,2,1,0:T(8,128)(2,1)S(1)} %pad_maximum_fusion.2.rest_4_), channel_id=1, source_target_pairs={{0,1},{1,0},{2,3},{3,2},{4,5},{5,4},{6,7},{7,6},{8,9},{9,8},{10,11... | collective-permute-start | bytes 1572872 | tf_op jit(solution)/shard_map/ppermute | solution.py:63
  285.4 12.3 %collective-permute-start.51 = (bf16[4,4,128,128]{3,2,1,0:T(8,128)(2,1)S(1)}, bf16[4,4,128,128]{3,2,1,0:T(8,128)(2,1)S(1)}, u32[]{:S(2)}, u32[]{:S(2)}) collective-permute-start(bf16[4,4,128,128]{3,2,1,0:T(8,128)(2,1)S(1)} %collective-permute-done.49.rest_5_), channel_id=1, source_target_pairs={{0,1},{1,0},{2,3},{3,2},{4,5},{5,4},{6,7},{7,6},{8,9},{9,8},{10,11... | collective-permute-start | bytes 1572872 | tf_op jit(solution)/shard_map/ppermute | solution.py:63
  289.2 8.5 %collective-permute-start.61 = (bf16[4,2,128,128]{3,2,1,0:T(8,128)(2,1)}, bf16[4,2,128,128]{3,2,1,0:T(8,128)(2,1)S(1)}, u32[]{:S(2)}, u32[]{:S(2)}) collective-permute-start(bf16[4,2,128,128]{3,2,1,0:T(8,128)(2,1)} %amplitudes.7.rest_8_), channel_id=1, source_target_pairs={{0,2},{1,3},{2,0},{3,1},{4,6},{5,7},{6,4},{7,5},{8,10},{9,11},{10,... | collective-permute-start | bytes 786440 | tf_op jit(solution)/shard_map/ppermute | solution.py:59
  289.8 7.8 %collective-permute-start.62 = (bf16[4,2,128,128]{3,2,1,0:T(8,128)(2,1)}, bf16[4,2,128,128]{3,2,1,0:T(8,128)(2,1)S(1)}, u32[]{:S(2)}, u32[]{:S(2)}) collective-permute-start(bf16[4,2,128,128]{3,2,1,0:T(8,128)(2,1)} %amplitudes.7.rest_8_), channel_id=1, source_target_pairs={{0,1},{1,0},{2,3},{3,2},{4,5},{5,4},{6,7},{7,6},{8,9},{9,8},{10,11... | collective-permute-start | bytes 786440 | tf_op jit(solution)/shard_map/ppermute | solution.py:63
  (64 other events, 698.1 us)

commit v3 on v2

--- a/solution.py
+++ b/solution.py
@@ -11,7 +11,6 @@
 CORES = 2
 RING = (0, 1, 3, 2)
 HALVES = 2
-HOME_CHUNKS = 1
 PIECES = 2
 EXTRA_ROWS = 16
 VMEM = 56 * 1024 * 1024
@@ -64,7 +63,7 @@
 
 
 def after(values, *done):
-    return lax.optimization_barrier((tuple(values), done))[0]
+    return lax.optimization_barrier((tuple(values), tuple(done)))[0]
 
 
 WHOLE = pl.BlockSpec(memory_space=pltpu.VMEM)
@@ -140,10 +139,12 @@
     return out, refs[at:]
 
 
-def products_kernel(n_blocks, n_both, n_chunks, table, own, *rest):
-    blocks, chunks, (own_t, cat) = rest[:n_blocks], rest[n_blocks:n_blocks + n_chunks], rest[-2:]
+def products_kernel(counts, n_both, n_chunks, table, own, *rest):
+    blocks, rest = split(rest, counts)
+    chunks, (own_t, cat) = rest[:n_chunks], rest[-2:]
+    n_blocks = len(blocks)
     w = own_t.shape[1]
-    spread(cat, [[ref] for ref in blocks])
+    spread(cat, blocks)
     for i in range(own.shape[0]):
         own_t[i] = own[i].T
     for n, out in enumerate(chunks):
@@ -163,17 +164,18 @@
     slots = table.shape[1]
     occ, rows, w = own.shape
     entries = len(blocks) + n_both
+    parts = [part for block in blocks for part in block]
     chunk = jax.ShapeDtypeStruct((slots // n_chunks, entries, w, w), F32)
     return pl.pallas_call(
-        functools.partial(products_kernel, len(blocks), n_both, n_chunks),
+        functools.partial(products_kernel, [len(block) for block in blocks], n_both, n_chunks),
         out_shape=(chunk,) * n_chunks,
-        in_specs=[SCALARS] + [WHOLE] * (1 + len(blocks)),
+        in_specs=[SCALARS] + [WHOLE] * (1 + len(parts)),
         out_specs=(WHOLE,) * n_chunks,
         scratch_shapes=[pltpu.VMEM((occ, w, rows), BF16), pltpu.VMEM((occ, rows, len(blocks) * w), BF16)],
         compiler_params=params(),
         cost_estimate=cost(2 * slots * entries * w * w * rows, 4 * slots * entries * w * w),
         name="products",
-    )(table, own, *blocks)
+    )(table, own, *parts)
 
 
 def amplitude_kernel(plan, n_terms, numbers, down, across, *rest):
@@ -268,7 +270,7 @@
 
 def arrange(given):
     n, rows, u = given.shape
-    tile = 128 if rows % 128 == 0 else rows
+    tile = rows // 2
     return pl.pallas_call(
         arrange_kernel,
         grid=(rows // tile,),
@@ -302,11 +304,12 @@
     wide_d = step // (n_pair * u)
     rows = integrals.shape[0]
 
+    def by_owner(piece):
+        piece = piece.reshape(piece.shape[0], wide_d, n_pair, u).transpose(2, 0, 1, 3)
+        return piece.reshape(n_pair, piece.shape[1], wide_d * u)
+
     def regroup(piece):
-        got = lax.all_to_all(
-            piece.reshape(piece.shape[0], wide_d, n_pair, u), "pair", split_axis=2, concat_axis=0, tiled=True
-        )
-        return got.reshape(slab // rows, piece.shape[0], wide_d * u)
+        return lax.all_to_all(piece, "pair", split_axis=0, concat_axis=0, tiled=True)
 
     cap = pair_table.shape[0]
     slots = n_pair * cap
@@ -348,26 +351,28 @@
     metrics.append(lax.dynamic_slice_in_dim(metric, columns(0, 0), slab, 1).T)
     crossed = to_core(lax.dynamic_slice_in_dim(metric, columns(0, 1), slab, 1), lay)
     places += [(0, None), (ny, None)]
-    parts_y = {}
-    for k in range(1, ny):
-        for cc in range(CORES):
-            part = lax.dynamic_slice(metric, (x * cut, columns(k, cc)), (cut, slab))
-            parts_y[k, cc] = part
-    first, = after((jnp.concatenate([integrals[:, :step], listed], axis=0),), *parts_y.values())
-    parts_y = {key: lax.ppermute(part, "aux", lay.y_shift(*key)) for key, part in parts_y.items()}
-    first = regroup(first)
+    parts_y = [
+        lax.dynamic_slice(metric, (x * cut, (y + k) % ny * CORES * slab), (cut, CORES * slab)) for k in range(1, ny)
+    ]
+    first = by_owner(jnp.concatenate([integrals[:, :step], listed], axis=0))
+    parts_y = [to_y(part, lay, k) for k, part in enumerate(parts_y, 1)]
+    raw = first = regroup(first)
     scatter_table, gather_table, numbers = slot_tables(first[:, rows, :u])
     first = first[:, :rows].reshape(slab, -1)
-    second, *arrived = after([integrals[:, step:], *parts_y.values()], first)
+    second, = after([by_owner(integrals[:, step:])], raw)
     second = regroup(second).reshape(slab, -1)
-    swapped = []
-    keys_y = list(parts_y)
+    first, *arrived = after([first, *parts_y])
     arrived = jnp.stack(arrived)
     for t in range(nx):
         if t > 0:
             arrived = to_pair(arrived, lay, 0, 1)
-        swapped += [arrived[n] for n in range(len(keys_y))]
-        places += [(cc * ny + k, t) for k, cc in keys_y]
+        for cc in range(CORES):
+            here = lax.dynamic_slice_in_dim(arrived, (c ^ cc) * slab, slab, 2)
+            if cc == 1:
+                here = to_core(here, lay)
+            swapped = [here[k - 1] for k in range(1, ny)]
+            metrics += [part.T for part in swapped]
+            places += [(cc * ny + k, t) for k in range(1, ny)]
 
     def from_aux(part):
         there = [part] + [to_y(part, lay, k) for k in range(1, ny)]
@@ -377,30 +382,38 @@
     ready = after((second, crossed, scatter_table, gather_table, numbers, *across.values()), *there[:ny])
     second, crossed, scatter_table, gather_table, numbers = ready[:5]
     across = dict(zip(across, ready[5:]))
-    metrics.append(crossed.T)
-    metrics += [part.T for part in swapped]
+    metrics.insert(1, crossed.T)
     own = fit(metrics, tuple(places), starts, there, w, occ, 0, None)
     own = fit(metrics, tuple(places), starts, from_aux(second), w, occ, 1, own)
 
     block = {(0, 0): [own]}
 
-    def ring(s, *done):
-        here = block[s, 0][0]
-        if s < nz - 1:
-            if done:
-                here, = after((here,), *done)
-            block[s + 1, 0] = [to_pair(here, lay, 1, 0)]
-            for t in range(1, nx):
-                here = to_pair(here, lay, 0, 1)
-                block[s, t] = [here]
-            return [block[s + 1, 0][0]] + [block[s, t][0] for t in range(1, nx)]
-        half = occ // HALVES
-        here, other = after((here, block[s - 1, nx - 1][0]), *done)
-        for t in range(1, nx - 1):
+    half = occ // HALVES
+
+    def along(here, s, t_first, t_end, out):
+        for t in range(t_first, t_end):
             here = to_pair(here, lay, 0, 1)
             block[s, t] = [here]
-        block[s, nx - 1] = [to_pair(here[:half], lay, 0, 1), to_pair(other[half:], lay, 1, 0)]
-        return block[s, nx - 1]
+            out.append(here)
+        return here
+
+    def both_ways(s, done):
+        here, other = block[s, 0][0], block[s - 1, nx - 1][-1]
+        moved = []
+        here, other = after((here, other), *done)
+        here = along(here, s, 1, nx - 1, moved)
+        block[s, nx - 1] = [to_pair(here[:half], lay, 0, 1), to_pair(other[-half:], lay, 1, 0)]
+        return moved + block[s, nx - 1]
+
+    def ring(s, x_too, *done):
+        here = block[s, 0][0]
+        if done:
+            here, = after((here,), *done)
+        block[s + 1, 0] = [to_pair(here, lay, 1, 0)]
+        moved = [block[s + 1, 0][0]]
+        if x_too:
+            along(here, s, 1, nx, moved)
+        return moved
 
     firsts = [g for g in lay.elements() if g <= lay.inverse(g)]
     stages = [[] for _ in range(nz)]
@@ -415,18 +428,22 @@
         arrays = [v for v, _ in values]
         rounds.append(gather_slots(arrays[0] if len(arrays) == 1 else jnp.concatenate(arrays, axis=1), lay))
 
-    def sums(n, *done):
+    def sums(n, done=(), hold=()):
         both = [g for g in stages[n] if g != lay.inverse(g) or n == last]
         stage = both + [g for g in stages[n] if g not in both]
         here, = after((own,), *done) if done else (own,)
-        chunks = products(scatter_table, n_aux * PIECES, here, [block[g][0] for g in stage], len(both))
+        chunks = products(scatter_table, n_aux * PIECES, here, [block[g] for g in stage], len(both))
         got = [to_core(v, lay) for v in chunks[ny * PIECES:]]
-        terms = [chunks[:PIECES], got[:PIECES]]
+        terms, sends = [chunks[:PIECES], got[:PIECES]], []
         for k in range(1, ny):
             there = slice(k * PIECES, (k + 1) * PIECES)
-            terms.append([to_y(near + far, lay, k) for near, far in zip(chunks[there], got[there])])
+            going = [near + far for near, far in zip(chunks[there], got[there])]
+            if hold:
+                going = after(going, *hold)
+            sends += going
+            terms.append([to_y(value, lay, k) for value in going])
         terms = [piece for term in terms for piece in term]
-        return stage, both, terms
+        return (stage, both, terms), sends
 
     def weigh(stage, both, terms):
         rows_of = jnp.stack([across[g] for g in stage])
@@ -447,12 +464,24 @@
                 sends[out] += 1
             plan.append((b, flipped, plain, out, slot))
         weights, *sent = amplitudes(tuple(plan), numbers, own_virt, rows_of, terms, len(keys), sends)
+        return (weights, keys), [(sent[out], g) for g, out in out_of.items()]
+
+    def exchange(sent, *done):
         arrived = []
-        for g, out in out_of.items():
+        for value, g in sent:
+            if done:
+                value, = after((value,), *done)
             back = lay.inverse(g)
-            value = to_pair(sent[out], lay, -g[0], -g[1])
+            value = to_pair(value, lay, -g[0], -g[1])
             arrived.append((value, [(g, 1)] if back == g else [(back, 1), (back, 0)]))
-        return (weights, keys), arrived
+        return arrived
+
+    def part(which, tile, first, tiles, start, kind):
+        used = sorted({place[way][g][0] for g in which for way in (0, 1)})
+        where = tuple(tuple((used.index(place[way][g][0]), place[way][g][1]) for g in which) for way in (0, 1))
+        return gradient(
+            gather_table, [block[g] for g in which], [rounds[r] for r in used], where, tile, first, tiles, start, kind
+        )
 
     def only(weights, which):
         values, keys = weights
@@ -461,47 +490,40 @@
             return weights
         return values[:, at[0]:at[-1] + 1], [keys[e] for e in at]
 
-    def part(which, tile, first, tiles, start, kind):
-        used = sorted({place[way][g][0] for g in which for way in (0, 1)})
-        where = tuple(tuple((used.index(place[way][g][0]), place[way][g][1]) for g in which) for way in (0, 1))
-        return gradient(
-            gather_table, [block[g] for g in which], [rounds[r] for r in used], where, tile, first, tiles, start, kind
-        )
-
-    moved = ring(0)
-    weights0, _ = weigh(*sums(0))
+    moved = ring(0, True)
+    stage0, _ = sums(0)
+    weights0, _ = weigh(*stage0)
     collect([weights0])
-    moved = ring(1, *moved, *rounds[0])
-    weights1, arrived1 = weigh(*sums(1))
+    moved = ring(1, True, *moved, *rounds[0])
+    stage1, _ = sums(1)
+    weights1, sent1 = weigh(*stage1)
     collect([weights1])
-    moved = ring(2, *moved, *[v for v, _ in arrived1])
-    stage2 = sums(2, weights1[0])
+    arrived1 = exchange(sent1)
+    moved = ring(2, True, *moved, *[v for v, _ in arrived1])
+    stage2, _ = sums(2, [weights1[0]])
     collect(arrived1)
-    weights2, arrived2 = weigh(*stage2)
+    weights2, sent2 = weigh(*stage2)
+    arrived2 = exchange(sent2)
     collect([only(weights2, stage2[1])])
-    moved = ring(3, *moved, *rounds[1], *rounds[2], *[v for v, _ in arrived2])
-    stage3 = sums(3, weights2[0])
+    stage3, sends3 = sums(3, [weights2[0]])
+    moved = both_ways(3, [*moved, *rounds[1], *rounds[2], *[v for v, _ in arrived2], *sends3])
     rest2 = [g for g in stage2[0] if g not in stage2[1]]
+    arrived2 = [(after((v,), *stage3[2])[0], keys) for v, keys in arrived2]
     collect(arrived2 + [only(weights2, rest2)])
 
-    def there(g):
-        return all(g in place[way] and place[way][g][0] <= 3 for way in (0, 1))
-
-    early = [g for g in lay.elements() if there(g)]
+    def known(g, n):
+        return all(g in place[way] and place[way][g][0] < n for way in (0, 1))
+
+    early = [g for g in lay.elements() if known(g, 4)]
     late = [g for g in lay.elements() if g not in early]
     total = part(early, slab // 2, 0, 2, None, F32)
-    weights3, arrived3 = weigh(stage3[0], stage3[1], after(stage3[2], *moved, total))
+    weights3, sent3 = weigh(stage3[0], stage3[1], after(stage3[2], total, *moved))
     collect([weights3])
-    if arrived3:
-        collect(arrived3)
-    tile = slab // HOME_CHUNKS
-    home = []
-    for q in range(HOME_CHUNKS):
-        rows = part(late, tile, q, 1, total, BF16)
-        rows = rows.reshape(occ, tile, parts, u).transpose(0, 2, 1, 3).reshape(n_pair, tile, u)
-        rows = lax.all_to_all(rows, "pair", split_axis=0, concat_axis=0, tiled=True)
-        home.append(rows)
-    return arrange(home[0]) if len(home) == 1 else jnp.concatenate([arrange(rows) for rows in home], axis=0)
+    if sent3:
+        collect(exchange(sent3))
+    rows = part(late, slab // 2, 0, 2, total, BF16)
+    rows = rows.reshape(occ, slab, parts, u).transpose(0, 2, 1, 3).reshape(n_pair, slab, u)
+    return arrange(lax.all_to_all(rows, "pair", split_axis=0, concat_axis=0, tiled=True))
 
 
 def solution(mesh):

time: 363 us -> 349 us (0.961)
  local copies, waits for them, and re-layouts: 37.3 us -> 31.7 us
  waiting for transfers between devices: 124 us -> 119 us
    all_to_all x2, waiting for transfers between devices: 18.6 us -> 7.27 us  [regroup(): lax.all_to_all(piece, 'pair', split_axis=0, concat_axis=0, tiled=True)]
    ppermute x13, waiting for transfers between devices: 24.8 us -> 30.1 us  [to_pair(): return lax.ppermute(x, 'pair', lay.pair_shift(s % lay.nz, t % lay.nx))]
    dynamic_slice x1 -> x4, local copies, waits for them, and re-layouts: 1.33 us -> 5.85 us  [the longest x2 4.58 us: on_device(): here = lax.dynamic_slice_in_dim(arrived, (c ^ cc) * slab, slab, 2)]
    ppermute x16 -> x17, starting transfers between devices: 18.7 us -> 20.4 us  [to_y(): return lax.ppermute(x, 'aux', lay.y_shift(k))]
    ppermute x16 -> x17, waiting for transfers between devices: 74.5 us -> 76.2 us  [to_y(): return lax.ppermute(x, 'aux', lay.y_shift(k))]
    unnamed x133 -> x121, local copies, waits for them, and re-layouts: 12 us -> 12.1 us
  transfers between devices with their start and end apart: 66 -> 67, of which waited for: 23 -> 25; matrix products, arithmetic and copies ran while one was open for 10% -> 10% of each run, Pallas kernels for 15% -> 16%
where the time goes in v3:
time: 349 us; the launch traced here: 348 us
  waiting for transfers between devices  119 us (34%)
  Pallas kernels  76.2 us (22%)
  starting transfers between devices  58.9 us (17%)
  blocking collectives  42.5 us (12%)
  local copies, waits for them, and re-layouts  31.7 us (9%)
  other arithmetic  13 us (4%)
  between operations  6.3 us (2%)
    ppermute x17, waiting for transfers between devices, to_y(): return lax.ppermute(x, 'aux', lay.y_shift(k))  76.2 us
    all_to_all x1, blocking collectives, on_device(): lax.all_to_all(rows, 'pair', split_axis=0, concat_axis=0, tiled=True)  42.5 us
    ppermute x13, waiting for transfers between devices, to_pair(): return lax.ppermute(x, 'pair', lay.pair_shift(s % lay.nz, t % lay.nx))  30.1 us
    pallas_call x2, Pallas kernels, gradient(): pl.pallas_call(functools.partial(gradient_kernel, where, [len(block) for...  25.7 us
    pallas_call x4, Pallas kernels, products(): pl.pallas_call(functools.partial(products_kernel, [len(block) for block i...  22.2 us
    ppermute x13, starting transfers between devices, to_pair(): return lax.ppermute(x, 'pair', lay.pair_shift(s % lay.nz, t % lay.nx))  21.7 us
    ppermute x17, starting transfers between devices, to_y(): return lax.ppermute(x, 'aux', lay.y_shift(k))  20.4 us
    pallas_call x2, Pallas kernels, fit(): pl.pallas_call(functools.partial(fit_kernel if so_far is None else fit_mo...  14 us
  transfers between devices with their start and end apart: 67, of which 25 were waited for; matrix products, arithmetic and copies ran while one was open for 10% of the time, Pallas kernels for 16%

profile of v3, /device:TPU:0, one launch (start us, length us, event | category | flops | bytes accessed | tf_op | source)
XLA Modules:
  0.0 347.6 jit_solution(17744208234262833498)
XLA Ops:
  0.0 2.4 slice_bitcast_fusion
  5.7 7.3 %all-to-all-start = ((bf16[8,112,512]{2,1,0:T(8,128)(2,1)}), bf16[8,112,512]{2,1,0:T(8,128)(2,1)}, u32[]{:S(2)}, u32[]{:S(2)}) async-start(bf16[8,112,512]{2,1,0:T(8,128)(2,1)} %reshape.422), calls=%async_computation | async-start | bytes 1835008 | tf_op jit(solution)/shard_map/all_to_all | solution.py:312
  14.2 1.4 copy.90
  15.6 1.5 collective-permute-start.1
  17.1 1.8 constant_dynamic-slice_fusion.2
  18.9 1.5 copy.89
  28.8 7.3 %all-to-all-done = bf16[8,112,512]{2,1,0:T(8,128)(2,1)} async-done(((bf16[8,112,512]{2,1,0:T(8,128)(2,1)}), bf16[8,112,512]{2,1,0:T(8,128)(2,1)}, u32[]{:S(2)}, u32[]{:S(2)}) %all-to-all-start) | async-done | bytes 917536 | tf_op jit(solution)/shard_map/all_to_all | solution.py:312
  36.1 4.2 %all-to-all-start.1 = ((bf16[8,96,512]{2,1,0:T(8,128)(2,1)}), bf16[8,96,512]{2,1,0:T(8,128)(2,1)}, u32[]{:S(2)}, u32[]{:S(2)}) async-start(bf16[8,96,512]{2,1,0:T(8,128)(2,1)} %reshape.420), calls=%async_computation.1 | async-start | bytes 1572864 | tf_op jit(solution)/shard_map/all_to_all | solution.py:312
  43.3 1.7 collective-permute-start.4
  45.1 1.5 collective-permute-start.2
  52.8 9.9 %collective-permute-done.2.rest_7_ = bf16[768,512]{1,0:T(8,128)(2,1)} collective-permute-done((bf16[768,512]{1,0:T(8,128)(2,1)S(1)}, bf16[768,512]{1,0:T(8,128)(2,1)}, u32[]{:S(2)}, u32[]{:S(2)}) %collective-permute-start.2) | collective-permute-done | bytes 786464 | tf_op jit(solution)/shard_map/ppermute | solution.py:58
  62.7 1.5 collective-permute-start.8
  64.2 2.2 dynamic-slice_bitcast_fusion.1
  66.9 9.7 %collective-permute-done.4 = bf16[1,384,1536]{1,2,0:T(8,128)(2,1)} collective-permute-done((bf16[1,384,1536]{1,2,0:T(8,128)(2,1)}, bf16[1,384,1536]{1,2,0:T(8,128)(2,1)}, u32[]{:S(2)}, u32[]{:S(2)}) %collective-permute-start.4) | collective-permute-done | bytes 1179680 | tf_op jit(solution)/shard_map/ppermute | solution.py:54
  76.7 2.4 constant_dynamic-slice_fusion.1
  79.6 1.4 copy.91
  82.5 7.0 %fit.2.so_far = bf16[8,768,128]{2,1,0:T(8,128)(2,1)} custom-call(s32[2]{0:T(128)} %pad_add_fusion.3.starts.rest_0_, bf16[768,768]{1,0:T(8,128)(2,1)} %bitcast.76, bf16[768,768]{1,0:T(8,128)(2,1)} %bitcast.78, bf16[768,384]{1,0:T(8,128)(2,1)} %get-tuple-element.146.rest_2_.rest_3_, bf16[768,384]{1,0:T(8,128)(2,1)} %bitcast.37.rest_3_.rest_4_, ...), custom_call_target="tpu_custom_call" | custom-call | flops 2415919104 | bytes 7864320 | tf_op jit(solution)/shard_map/fit/pallas_call | solution.py:108
  89.6 7.0 %fit.3.own.rest_0_ = bf16[8,768,128]{2,1,0:T(8,128)(2,1)} custom-call(bf16[8,768,128]{2,1,0:T(8,128)(2,1)} %fit.2.so_far, s32[2]{0:T(128)} %pad_add_fusion.3.starts.rest_0_, bf16[768,768]{1,0:T(8,128)(2,1)} %bitcast.77, bf16[768,768]{1,0:T(8,128)(2,1)} %bitcast.79, ...), custom_call_target="tpu_custom_call", output_to_operand_aliasing={{}: (0, {})} | custom-call | flops 2415919104 | bytes 7864320 | tf_op jit(solution)/shard_map/fit/pallas_call | solution.py:108
  96.6 1.5 collective-permute-start.11
  98.6 4.1 %products.4 = (f32[2,1,128,128]{3,2,1,0:T(8,128)}, f32[2,1,128,128]{3,2,1,0:T(8,128)}, f32[2,1,128,128]{3,2,1,0:T(8,128)}, f32[2,1,128,128]{3,2,1,0:T(8,128)}, f...) custom-call(s32[3,16]{1,0:T(4,128)} %bitcast.87, ...), custom_call_target="tpu_custom_call" | custom-call | flops 402653184 | bytes 1048576 | tf_op jit(solution)/shard_map/products/pallas_call | solution.py:169
  105.3 1.6 collective-permute-start.18
  109.2 2.6 collective-permute-done.18.rest_5_
  111.8 2.3 collective-permute-done.16.rest_4_
  114.1 2.2 amplitudes.4.rest_5_
  116.3 1.5 collective-permute-start.19
  117.8 6.5 %collective-permute-done.19.rest_6_ = bf16[4,2,128,128]{3,2,1,0:T(8,128)(2,1)S(1)} collective-permute-done((bf16[4,2,128,128]{3,2,1,0:T(8,128)(2,1)}, bf16[4,2,128,128]{3,2,1,0:T(8,128)(2,1)S(1)}, u32[]{:S(2)}, u32[]{:S(2)}) %collective-permute-start.19) | collective-permute-done | bytes 262176 | tf_op jit(solution)/shard_map/ppermute | solution.py:58
  124.4 1.5 collective-permute-done.21.rest_8_
  125.9 8.6 %collective-permute-done.11.rest_0_.rest_2_ = bf16[8,768,128]{2,1,0:T(8,128)(2,1)S(1)} collective-permute-done((bf16[8,768,128]{2,1,0:T(8,128)(2,1)}, bf16[8,768,128]{2,1,0:T(8,128)(2,1)S(1)}, u32[]{:S(2)}, u32[]{:S(2)}) %collective-permute-start.11) | collective-permute-done | bytes 1572896 | tf_op jit(solution)/shard_map/ppermute | solution.py:54
  134.8 2.4 collective-permute-start.22
  137.7 6.5 %products.5 = (f32[2,3,128,128]{3,2,1,0:T(8,128)}, f32[2,3,128,128]{3,2,1,0:T(8,128)}, f32[2,3,128,128]{3,2,1,0:T(8,128)}, f32[2,3,128,128]{3,2,1,0:T(8,128)}, f...) custom-call(s32[3,16]{1,0:T(4,128)} %bitcast.88, ...), custom_call_target="tpu_custom_call" | custom-call | flops 1207959552 | bytes 3145728 | tf_op jit(solution)/shard_map/products/pallas_call | solution.py:169
  147.4 1.6 collective-permute-start.29
  151.3 8.2 %collective-permute-done.29.rest_5_ = f32[2,3,128,128]{3,2,1,0:T(8,128)S(1)} collective-permute-done((f32[2,3,128,128]{3,2,1,0:T(8,128)S(1)}, f32[2,3,128,128]{3,2,1,0:T(8,128)S(1)}, u32[]{:S(2)}, u32[]{:S(2)}) %collective-permute-start.29) | collective-permute-done | bytes 393248 | tf_op jit(solution)/shard_map/ppermute | solution.py:58
  159.4 7.9 %collective-permute-done.27.rest_4_ = f32[2,3,128,128]{3,2,1,0:T(8,128)S(1)} collective-permute-done((f32[2,3,128,128]{3,2,1,0:T(8,128)S(1)}, f32[2,3,128,128]{3,2,1,0:T(8,128)S(1)}, u32[]{:S(2)}, u32[]{:S(2)}) %collective-permute-start.27) | collective-permute-done | bytes 393248 | tf_op jit(solution)/shard_map/ppermute | solution.py:58
  168.0 3.0 amplitudes.5
  173.1 4.0 %collective-permute-done.31 = bf16[4,1,128,128]{3,2,1,0:T(8,128)(2,1)S(1)} collective-permute-done((bf16[4,1,128,128]{3,2,1,0:T(8,128)(2,1)}, bf16[4,1,128,128]{3,2,1,0:T(8,128)(2,1)S(1)}, u32[]{:S(2)}, u32[]{:S(2)}) %collective-permute-start.31) | collective-permute-done | bytes 131104 | tf_op jit(solution)/shard_map/ppermute | solution.py:54
  177.1 2.0 collective-permute-done.30
  179.0 1.5 collective-permute-start.32
  180.6 1.5 collective-permute-start.34
  182.7 6.5 %products.6 = (f32[2,3,128,128]{3,2,1,0:T(8,128)}, f32[2,3,128,128]{3,2,1,0:T(8,128)}, f32[2,3,128,128]{3,2,1,0:T(8,128)}, f32[2,3,128,128]{3,2,1,0:T(8,128)}, f...) custom-call(s32[3,16]{1,0:T(4,128)} %bitcast.89, ...), custom_call_target="tpu_custom_call" | custom-call | flops 1207959552 | bytes 3145728 | tf_op jit(solution)/shard_map/products/pallas_call | solution.py:169
  189.7 3.1 collective-permute-done.34.rest_10_
  192.8 2.3 collective-permute-start.33
  195.2 3.4 collective-permute-done.37.rest_14_
  200.2 1.6 collective-permute-start.45
  203.5 8.7 %collective-permute-done.45.rest_5_ = f32[2,3,128,128]{3,2,1,0:T(8,128)S(1)} collective-permute-done((f32[2,3,128,128]{3,2,1,0:T(8,128)S(1)}, f32[2,3,128,128]{3,2,1,0:T(8,128)S(1)}, u32[]{:S(2)}, u32[]{:S(2)}) %collective-permute-start.45) | collective-permute-done | bytes 393248 | tf_op jit(solution)/shard_map/ppermute | solution.py:58
  212.2 7.5 %collective-permute-done.43.rest_4_ = f32[2,3,128,128]{3,2,1,0:T(8,128)S(1)} collective-permute-done((f32[2,3,128,128]{3,2,1,0:T(8,128)S(1)}, f32[2,3,128,128]{3,2,1,0:T(8,128)S(1)}, u32[]{:S(2)}, u32[]{:S(2)}) %collective-permute-start.43) | collective-permute-done | bytes 393248 | tf_op jit(solution)/shard_map/ppermute | solution.py:58
  221.0 3.0 amplitudes.6
  224.0 5.2 %products.7 = (f32[2,2,128,128]{3,2,1,0:T(8,128)}, f32[2,2,128,128]{3,2,1,0:T(8,128)}, f32[2,2,128,128]{3,2,1,0:T(8,128)}, f32[2,2,128,128]{3,2,1,0:T(8,128)}, f...) custom-call(s32[3,16]{1,0:T(4,128)} %bitcast.90, ...), custom_call_target="tpu_custom_call" | custom-call | flops 805306368 | bytes 2097152 | tf_op jit(solution)/shard_map/products/pallas_call | solution.py:169
  229.8 1.7 collective-permute-start.46
  231.6 1.6 collective-permute-start.59
  233.2 3.0 collective-permute-start.47
  238.3 5.5 %collective-permute-done.47 = bf16[4,1,128,128]{3,2,1,0:T(8,128)(2,1)S(1)} collective-permute-done((bf16[4,1,128,128]{3,2,1,0:T(8,128)(2,1)S(1)}, bf16[4,1,128,128]{3,2,1,0:T(8,128)(2,1)S(1)}, u32[]{:S(2)}, u32[]{:S(2)}) %collective-permute-start.47) | collective-permute-done | bytes 131104 | tf_op jit(solution)/shard_map/ppermute | solution.py:54
  243.9 1.6 collective-permute-start.55
  246.6 1.5 collective-permute-start.50
  248.1 2.9 collective-permute-start.51
  251.1 1.9 collective-permute-done.55.rest_5_
  253.1 5.2 %collective-permute-done.54.rest_4_ = f32[2,2,128,128]{3,2,1,0:T(8,128)S(1)} collective-permute-done((f32[2,2,128,128]{3,2,1,0:T(8,128)S(1)}, f32[2,2,128,128]{3,2,1,0:T(8,128)S(1)}, u32[]{:S(2)}, u32[]{:S(2)}) %collective-permute-start.54) | collective-permute-done | bytes 262176 | tf_op jit(solution)/shard_map/ppermute | solution.py:58
  258.3 1.6 collective-permute-start.56
  261.3 15.3 %gradient.2.rest_12_ = f32[8,768,128]{2,1,0:T(8,128)} custom-call(s32[3,16]{1,0:T(4,128)} %bitcast.95, bf16[8,768,128]{2,1,0:T(8,128)(2,1)} %fit.3.own.rest_0_, bf16[8,768,128]{2,1,0:T(8,128)(2,1)} %copy-done.5, bf16[8,768,128]{2,1,0:T(8,128)(2,1)} %copy-done.4, bf16[8,768,128]{2,1,0:T(8,128)(2,1)} %copy-done.6, bf16[8,768,128]{2,1,0:T(8,128)(2,1)} %copy-done.9, ...), custom_call_target="tpu_custom_call" | custom-call | flops 4026531840 | bytes 7864320 | tf_op jit(solution)/shard_map/gradient/pallas_call | solution.py:247
  276.8 3.1 amplitudes.7.rest_8_
  280.9 7.9 %collective-permute-done.62.rest_9_ = bf16[4,2,128,128]{3,2,1,0:T(8,128)(2,1)S(1)} collective-permute-done((bf16[4,2,128,128]{3,2,1,0:T(8,128)(2,1)}, bf16[4,2,128,128]{3,2,1,0:T(8,128)(2,1)S(1)}, u32[]{:S(2)}, u32[]{:S(2)}) %collective-permute-start.62) | collective-permute-done | bytes 262176 | tf_op jit(solution)/shard_map/ppermute | solution.py:58
  288.8 1.5 collective-permute-done.64.rest_11_
  291.8 10.3 %gradient.3 = bf16[8,768,128]{2,1,0:T(8,128)(2,1)} custom-call(s32[3,16]{1,0:T(4,128)} %bitcast.96, bf16[8,768,128]{2,1,0:T(8,128)(2,1)} %copy-done.7, bf16[8,768,128]{2,1,0:T(8,128)(2,1)} %copy-done.2, bf16[4,768,128]{2,1,0:T(8,128)(2,1)} %copy-done.16, bf16[4,768,128]{2,1,0:T(8,128)(2,1)} %copy-done.17, bf16[4,4,128,128]{3,2,1,0:T(8,128)(2,1)} %copy-done.13, ...), custom_call_target="tpu_custom_call" | custom-call | flops 2415919104 | bytes 4718592 | tf_op jit(solution)/shard_map/gradient/pallas_call | solution.py:247
  302.2 42.5 %all_to_all.15.given = bf16[8,768,128]{2,1,0:T(8,128)(2,1)} all-to-all(bf16[8,768,128]{2,1,0:T(8,128)(2,1)} %gradient.3), channel_id=1, replica_groups=mesh['pair'=8,'aux'=4] {'pair'}, dimensions={0} | all-to-all | bytes 3145728 | tf_op jit(solution)/shard_map/all_to_all | solution.py:526
  344.7 3.0 arrange.1
  (271 shorter events, 47.3 us)
Async XLA Ops:
  5.7 30.4 %all-to-all-start = ((bf16[8,112,512]{2,1,0:T(8,128)(2,1)}), bf16[8,112,512]{2,1,0:T(8,128)(2,1)}, u32[]{:S(2)}, u32[]{:S(2)}) async-start(bf16[8,112,512]{2,1,0:T(8,128)(2,1)} %reshape.422), calls=%async_computation | async-start | bytes 1835008 | tf_op jit(solution)/shard_map/all_to_all | solution.py:312
  15.6 27.7 %collective-permute-start.1 = (bf16[384,1536]{0,1:T(8,128)(2,1)}, bf16[384,1536]{0,1:T(8,128)(2,1)}, u32[]{:S(2)}, u32[]{:S(2)}) collective-permute-start(bf16[384,1536]{0,1:T(8,128)(2,1)} %copy.90), channel_id=1, source_target_pairs={{0,2},{1,3},{2,0},{3,1},{4,6},{5,7},{6,4},{7,5},{8,10},{9,11},{10,... | collective-permute-start | bytes 3538952 | tf_op jit(solution)/shard_map/ppermute | solution.py:58
  20.4 32.5 %collective-permute-start = (bf16[768,768]{0,1:T(8,128)(2,1)}, bf16[768,768]{0,1:T(8,128)(2,1)S(1)}, u32[]{:S(2)}, u32[]{:S(2)}) collective-permute-start(bf16[768,768]{0,1:T(8,128)(2,1)} %copy.89), channel_id=1, source_target_pairs={{0,1},{1,0},{2,3},{3,2},{4,5},{5,4},{6,7},{7,6},{8,9},{9,8},{10,11... | collective-permute-start | bytes 3538952 | tf_op jit(solution)/shard_map/ppermute | solution.py:62
  36.1 26.6 %all-to-all-start.1 = ((bf16[8,96,512]{2,1,0:T(8,128)(2,1)}), bf16[8,96,512]{2,1,0:T(8,128)(2,1)}, u32[]{:S(2)}, u32[]{:S(2)}) async-start(bf16[8,96,512]{2,1,0:T(8,128)(2,1)} %reshape.420), calls=%async_computation.1 | async-start | bytes 1572864 | tf_op jit(solution)/shard_map/all_to_all | solution.py:312
  43.3 33.3 %collective-permute-start.4 = (bf16[1,384,1536]{1,2,0:T(8,128)(2,1)}, bf16[1,384,1536]{1,2,0:T(8,128)(2,1)}, u32[]{:S(2)}, u32[]{:S(2)}) collective-permute-start(bf16[1,384,1536]{1,2,0:T(8,128)(2,1)} %bitcast.38), channel_id=1, source_target_pairs={{0,4},{4,0},{8,12},{12,8},{24,28},{28,24},{16,20},{20,16},{1,5},{5... | collective-permute-start | bytes 3538952 | tf_op jit(solution)/shard_map/ppermute | solution.py:54
  45.1 17.6 %collective-permute-start.2 = (bf16[768,512]{1,0:T(8,128)(2,1)S(1)}, bf16[768,512]{1,0:T(8,128)(2,1)}, u32[]{:S(2)}, u32[]{:S(2)}) collective-permute-start(bf16[768,512]{1,0:T(8,128)(2,1)S(1)} %bitcast.80), channel_id=1, source_target_pairs={{0,2},{1,3},{2,0},{3,1},{4,6},{5,7},{6,4},{7,5},{8,10},{9,11},{10,... | collective-permute-start | bytes 2359304 | tf_op jit(solution)/shard_map/ppermute | solution.py:58
  62.7 16.9 %collective-permute-start.8 = (bf16[768,512]{1,0:T(8,128)(2,1)}, bf16[768,512]{1,0:T(8,128)(2,1)}, u32[]{:S(2)}, u32[]{:S(2)}) collective-permute-start(bf16[768,512]{1,0:T(8,128)(2,1)} %bitcast.2.rest_7_), channel_id=1, source_target_pairs={{0,2},{1,3},{2,0},{3,1},{4,6},{5,7},{6,4},{7,5},{8,10},{9,11},{10,... | collective-permute-start | bytes 2359304 | tf_op jit(solution)/shard_map/ppermute | solution.py:58
  66.4 12.6 %collective-permute-start.3 = (bf16[1,384,768]{1,2,0:T(8,128)(2,1)S(1)}, bf16[1,384,768]{1,2,0:T(8,128)(2,1)}, u32[]{:S(2)}, u32[]{:S(2)}) collective-permute-start(bf16[1,384,768]{1,2,0:T(8,128)(2,1)S(1)} %get-tuple-element.145), channel_id=1, source_target_pairs={{0,1},{1,0},{2,3},{3,2},{4,5},{5,4},{6,7},{7,6},{8,9},{9,8},{10,11... | collective-permute-start | bytes 1769480 | tf_op jit(solution)/shard_map/ppermute | solution.py:62
  66.4 15.3 %collective-permute-start.6 = (bf16[768,512]{1,0:T(8,128)(2,1)S(1)}, bf16[768,512]{1,0:T(8,128)(2,1)}, u32[]{:S(2)}, u32[]{:S(2)}) collective-permute-start(bf16[768,512]{1,0:T(8,128)(2,1)S(1)} %bitcast.81), channel_id=1, source_target_pairs={{0,1},{1,0},{2,3},{3,2},{4,5},{5,4},{6,7},{7,6},{8,9},{9,8},{10,11... | collective-permute-start | bytes 2359304 | tf_op jit(solution)/shard_map/ppermute | solution.py:62
  66.9 14.8 %collective-permute-start.7 = (bf16[768,512]{1,0:T(8,128)(2,1)}, bf16[768,512]{1,0:T(8,128)(2,1)}, u32[]{:S(2)}, u32[]{:S(2)}) collective-permute-start(bf16[768,512]{1,0:T(8,128)(2,1)} %collective-permute-done.2.rest_7_), channel_id=1, source_target_pairs={{0,1},{1,0},{2,3},{3,2},{4,5},{5,4},{6,7},{7,6},{8,9},{9,8},{10,11... | collective-permute-start | bytes 2359304 | tf_op jit(solution)/shard_map/ppermute | solution.py:62
  79.1 2.7 collective-permute-start.5
  79.1 10.5 %collective-permute-start.9 = (bf16[768,512]{1,0:T(8,128)(2,1)}, bf16[768,512]{1,0:T(8,128)(2,1)}, u32[]{:S(2)}, u32[]{:S(2)}) collective-permute-start(bf16[768,512]{1,0:T(8,128)(2,1)} %bitcast.2.rest_7_), channel_id=1, source_target_pairs={{0,1},{1,0},{2,3},{3,2},{4,5},{5,4},{6,7},{7,6},{8,9},{9,8},{10,11... | collective-permute-start | bytes 2359304 | tf_op jit(solution)/shard_map/ppermute | solution.py:62
  79.6 10.0 %collective-permute-start.10 = (bf16[768,512]{1,0:T(8,128)(2,1)}, bf16[768,512]{1,0:T(8,128)(2,1)}, u32[]{:S(2)}, u32[]{:S(2)}) collective-permute-start(bf16[768,512]{1,0:T(8,128)(2,1)} %collective-permute-done.8.rest_8_), channel_id=1, source_target_pairs={{0,1},{1,0},{2,3},{3,2},{4,5},{5,4},{6,7},{7,6},{8,9},{9,8},{10,11... | collective-permute-start | bytes 2359304 | tf_op jit(solution)/shard_map/ppermute | solution.py:62
  96.6 37.9 %collective-permute-start.11 = (bf16[8,768,128]{2,1,0:T(8,128)(2,1)}, bf16[8,768,128]{2,1,0:T(8,128)(2,1)S(1)}, u32[]{:S(2)}, u32[]{:S(2)}) collective-permute-start(bf16[8,768,128]{2,1,0:T(8,128)(2,1)} %fit.3.own.rest_0_), channel_id=1, source_target_pairs={{0,8},{4,12},{8,24},{12,28},{24,16},{28,20},{16,0},{20,4},{1,9},{5... | collective-permute-start | bytes 4718600 | tf_op jit(solution)/shard_map/ppermute | solution.py:54
  98.1 36.7 %collective-permute-start.12 = (bf16[8,768,128]{2,1,0:T(8,128)(2,1)}, bf16[8,768,128]{2,1,0:T(8,128)(2,1)S(1)}, u32[]{:S(2)}, u32[]{:S(2)}) collective-permute-start(bf16[8,768,128]{2,1,0:T(8,128)(2,1)} %fit.3.own.rest_0_), channel_id=1, source_target_pairs={{0,4},{4,0},{8,12},{12,8},{24,28},{28,24},{16,20},{20,16},{1,5},{5... | collective-permute-start | bytes 4718600 | tf_op jit(solution)/shard_map/ppermute | solution.py:54
  102.7 2.6 collective-permute-start.15
  103.2 4.7 %collective-permute-start.13 = (f32[2,1,128,128]{3,2,1,0:T(8,128)}, f32[2,1,128,128]{3,2,1,0:T(8,128)S(1)}, u32[]{:S(2)}, u32[]{:S(2)}) collective-permute-start(f32[2,1,128,128]{3,2,1,0:T(8,128)} %get-tuple-element.82), channel_id=1, source_target_pairs={{0,1},{1,0},{2,3},{3,2},{4,5},{5,4},{6,7},{7,6},{8,9},{9,8},{10,11... | collective-permute-start | bytes 393224 | tf_op jit(solution)/shard_map/ppermute | solution.py:62
  104.2 4.9 %collective-permute-start.14 = (f32[2,1,128,128]{3,2,1,0:T(8,128)}, f32[2,1,128,128]{3,2,1,0:T(8,128)}, u32[]{:S(2)}, u32[]{:S(2)}) collective-permute-start(f32[2,1,128,128]{3,2,1,0:T(8,128)} %get-tuple-element.83), channel_id=1, source_target_pairs={{0,1},{1,0},{2,3},{3,2},{4,5},{5,4},{6,7},{7,6},{8,9},{9,8},{10,11... | collective-permute-start | bytes 393224 | tf_op jit(solution)/shard_map/ppermute | solution.py:62
  105.3 6.4 %collective-permute-start.18 = (f32[2,1,128,128]{3,2,1,0:T(8,128)S(1)}, f32[2,1,128,128]{3,2,1,0:T(8,128)}, u32[]{:S(2)}, u32[]{:S(2)}) collective-permute-start(f32[2,1,128,128]{3,2,1,0:T(8,128)S(1)} %add.274), channel_id=1, source_target_pairs={{0,2},{1,3},{2,0},{3,1},{4,6},{5,7},{6,4},{7,5},{8,10},{9,11},{10,... | collective-permute-start | bytes 393224 | tf_op jit(solution)/shard_map/ppermute | solution.py:58
  107.9 6.2 %collective-permute-start.16 = (f32[2,1,128,128]{3,2,1,0:T(8,128)S(1)}, f32[2,1,128,128]{3,2,1,0:T(8,128)}, u32[]{:S(2)}, u32[]{:S(2)}) collective-permute-start(f32[2,1,128,128]{3,2,1,0:T(8,128)S(1)} %add.273), channel_id=1, source_target_pairs={{0,2},{1,3},{2,0},{3,1},{4,6},{5,7},{6,4},{7,5},{8,10},{9,11},{10,... | collective-permute-start | bytes 393224 | tf_op jit(solution)/shard_map/ppermute | solution.py:58
  116.3 8.0 %collective-permute-start.19 = (bf16[4,2,128,128]{3,2,1,0:T(8,128)(2,1)}, bf16[4,2,128,128]{3,2,1,0:T(8,128)(2,1)S(1)}, u32[]{:S(2)}, u32[]{:S(2)}) collective-permute-start(bf16[4,2,128,128]{3,2,1,0:T(8,128)(2,1)} %amplitudes.4.rest_5_), channel_id=1, source_target_pairs={{0,2},{1,3},{2,0},{3,1},{4,6},{5,7},{6,4},{7,5},{8,10},{9,11},{10,... | collective-permute-start | bytes 786440 | tf_op jit(solution)/shard_map/ppermute | solution.py:58
  117.8 6.5 %collective-permute-start.20 = (bf16[4,2,128,128]{3,2,1,0:T(8,128)(2,1)}, bf16[4,2,128,128]{3,2,1,0:T(8,128)(2,1)S(1)}, u32[]{:S(2)}, u32[]{:S(2)}) collective-permute-start(bf16[4,2,128,128]{3,2,1,0:T(8,128)(2,1)} %amplitudes.4.rest_5_), channel_id=1, source_target_pairs={{0,1},{1,0},{2,3},{3,2},{4,5},{5,4},{6,7},{7,6},{8,9},{9,8},{10,11... | collective-permute-start | bytes 786440 | tf_op jit(solution)/shard_map/ppermute | solution.py:62
  134.8 44.3 %collective-permute-start.22 = (bf16[8,768,128]{2,1,0:T(8,128)(2,1)S(1)}, bf16[8,768,128]{2,1,0:T(8,128)(2,1)S(1)}, u32[]{:S(2)}, u32[]{:S(2)}) collective-permute-start(bf16[8,768,128]{2,1,0:T(8,128)(2,1)S(1)} %collective-permute-done.11.rest_0_.rest_2_), channel_id=1, source_target_pairs={{0,8},{4,12},{8,24},{12,28},{24,16},{28,20},{16,0},{20,4},{1,9},{5... | collective-permute-start | bytes 4718600 | tf_op jit(solution)/shard_map/ppermute | solution.py:54
  137.1 41.9 %collective-permute-start.23 = (bf16[8,768,128]{2,1,0:T(8,128)(2,1)S(1)}, bf16[8,768,128]{2,1,0:T(8,128)(2,1)S(1)}, u32[]{:S(2)}, u32[]{:S(2)}) collective-permute-start(bf16[8,768,128]{2,1,0:T(8,128)(2,1)S(1)} %collective-permute-done.11.rest_0_.rest_2_), channel_id=1, source_target_pairs={{0,4},{4,0},{8,12},{12,8},{24,28},{28,24},{16,20},{20,16},{1,5},{5... | collective-permute-start | bytes 4718600 | tf_op jit(solution)/shard_map/ppermute | solution.py:54
  144.2 2.0 collective-permute-start.28
  144.3 3.1 collective-permute-start.26
  144.8 5.3 %collective-permute-start.24 = (f32[2,3,128,128]{3,2,1,0:T(8,128)}, f32[2,3,128,128]{3,2,1,0:T(8,128)S(1)}, u32[]{:S(2)}, u32[]{:S(2)}) collective-permute-start(f32[2,3,128,128]{3,2,1,0:T(8,128)} %get-tuple-element.93), channel_id=1, source_target_pairs={{0,1},{1,0},{2,3},{3,2},{4,5},{5,4},{6,7},{7,6},{8,9},{9,8},{10,11... | collective-permute-start | bytes 1179656 | tf_op jit(solution)/shard_map/ppermute | solution.py:62
  146.2 5.1 %collective-permute-start.25 = (f32[2,3,128,128]{3,2,1,0:T(8,128)}, f32[2,3,128,128]{3,2,1,0:T(8,128)S(1)}, u32[]{:S(2)}, u32[]{:S(2)}) collective-permute-start(f32[2,3,128,128]{3,2,1,0:T(8,128)} %get-tuple-element.94), channel_id=1, source_target_pairs={{0,1},{1,0},{2,3},{3,2},{4,5},{5,4},{6,7},{7,6},{8,9},{9,8},{10,11... | collective-permute-start | bytes 1179656 | tf_op jit(solution)/shard_map/ppermute | solution.py:62
  147.4 12.0 %collective-permute-start.29 = (f32[2,3,128,128]{3,2,1,0:T(8,128)S(1)}, f32[2,3,128,128]{3,2,1,0:T(8,128)S(1)}, u32[]{:S(2)}, u32[]{:S(2)}) collective-permute-start(f32[2,3,128,128]{3,2,1,0:T(8,128)S(1)} %add.276), channel_id=1, source_target_pairs={{0,2},{1,3},{2,0},{3,1},{4,6},{5,7},{6,4},{7,5},{8,10},{9,11},{10,... | collective-permute-start | bytes 1179656 | tf_op jit(solution)/shard_map/ppermute | solution.py:58
  150.1 17.2 %collective-permute-start.27 = (f32[2,3,128,128]{3,2,1,0:T(8,128)S(1)}, f32[2,3,128,128]{3,2,1,0:T(8,128)S(1)}, u32[]{:S(2)}, u32[]{:S(2)}) collective-permute-start(f32[2,3,128,128]{3,2,1,0:T(8,128)S(1)} %add.275), channel_id=1, source_target_pairs={{0,2},{1,3},{2,0},{3,1},{4,6},{5,7},{6,4},{7,5},{8,10},{9,11},{10,... | collective-permute-start | bytes 1179656 | tf_op jit(solution)/shard_map/ppermute | solution.py:58
  171.0 8.0 %collective-permute-start.30 = (bf16[4,2,128,128]{3,2,1,0:T(8,128)(2,1)}, bf16[4,2,128,128]{3,2,1,0:T(8,128)(2,1)S(1)}, u32[]{:S(2)}, u32[]{:S(2)}) collective-permute-start(bf16[4,2,128,128]{3,2,1,0:T(8,128)(2,1)} %get-tuple-element.99), channel_id=1, source_target_pairs={{0,16},{4,20},{8,0},{12,4},{24,8},{28,12},{16,24},{20,28},{1,17},{... | collective-permute-start | bytes 786440 | tf_op jit(solution)/shard_map/ppermute | solution.py:54
  171.9 5.2 %collective-permute-start.31 = (bf16[4,1,128,128]{3,2,1,0:T(8,128)(2,1)}, bf16[4,1,128,128]{3,2,1,0:T(8,128)(2,1)S(1)}, u32[]{:S(2)}, u32[]{:S(2)}) collective-permute-start(bf16[4,1,128,128]{3,2,1,0:T(8,128)(2,1)} %get-tuple-element.100), channel_id=1, source_target_pairs={{0,4},{4,0},{8,12},{12,8},{24,28},{28,24},{16,20},{20,16},{1,5},{5... | collective-permute-start | bytes 393224 | tf_op jit(solution)/shard_map/ppermute | solution.py:54
  179.0 40.7 %collective-permute-start.32 = (bf16[8,768,128]{2,1,0:T(8,128)(2,1)S(1)}, bf16[8,768,128]{2,1,0:T(8,128)(2,1)S(1)}, u32[]{:S(2)}, u32[]{:S(2)}) collective-permute-start(bf16[8,768,128]{2,1,0:T(8,128)(2,1)S(1)} %collective-permute-done.22.rest_1_.rest_0_), channel_id=1, source_target_pairs={{0,4},{4,0},{8,12},{12,8},{24,28},{28,24},{16,20},{20,16},{1,5},{5... | collective-permute-start | bytes 4718600 | tf_op jit(solution)/shard_map/ppermute | solution.py:54
  180.6 12.3 %collective-permute-start.34 = (bf16[4,3,128,128]{3,2,1,0:T(8,128)(2,1)}, bf16[4,3,128,128]{3,2,1,0:T(8,128)(2,1)S(1)}, u32[]{:S(2)}, u32[]{:S(2)}) collective-permute-start(bf16[4,3,128,128]{3,2,1,0:T(8,128)(2,1)} %get-tuple-element.102.rest_9_), channel_id=1, source_target_pairs={{0,2},{1,3},{2,0},{3,1},{4,6},{5,7},{6,4},{7,5},{8,10},{9,11},{10,... | collective-permute-start | bytes 1179656 | tf_op jit(solution)/shard_map/ppermute | solution.py:58
  182.2 16.4 %collective-permute-start.37 = (bf16[4,3,128,128]{3,2,1,0:T(8,128)(2,1)S(1)}, bf16[4,3,128,128]{3,2,1,0:T(8,128)(2,1)S(1)}, u32[]{:S(2)}, u32[]{:S(2)}) collective-permute-start(bf16[4,3,128,128]{3,2,1,0:T(8,128)(2,1)S(1)} %constant_dynamic-update-slice_fusion.rest_13_), channel_id=1, source_target_pairs={{0,2},{1,3},{2,0},{3,1},{4,6},{5,7},{6,4},{7,5},{8,10},{9,11},{10,... | collective-permute-start | bytes 1179656 | tf_op jit(solution)/shard_map/ppermute | solution.py:58
  189.2 9.4 %collective-permute-start.44 = (f32[2,3,128,128]{3,2,1,0:T(8,128)}, f32[2,3,128,128]{3,2,1,0:T(8,128)S(1)}, u32[]{:S(2)}, u32[]{:S(2)}) collective-permute-start(f32[2,3,128,128]{3,2,1,0:T(8,128)} %get-tuple-element.113), channel_id=1, source_target_pairs={{0,1},{1,0},{2,3},{3,2},{4,5},{5,4},{6,7},{7,6},{8,9},{9,8},{10,11... | collective-permute-start | bytes 1179656 | tf_op jit(solution)/shard_map/ppermute | solution.py:62
  189.2 11.0 %collective-permute-start.42 = (f32[2,3,128,128]{3,2,1,0:T(8,128)}, f32[2,3,128,128]{3,2,1,0:T(8,128)S(1)}, u32[]{:S(2)}, u32[]{:S(2)}) collective-permute-start(f32[2,3,128,128]{3,2,1,0:T(8,128)} %get-tuple-element.111), channel_id=1, source_target_pairs={{0,1},{1,0},{2,3},{3,2},{4,5},{5,4},{6,7},{7,6},{8,9},{9,8},{10,11... | collective-permute-start | bytes 1179656 | tf_op jit(solution)/shard_map/ppermute | solution.py:62
  192.8 52.6 %collective-permute-start.33 = (bf16[8,768,128]{2,1,0:T(8,128)(2,1)}, bf16[8,768,128]{2,1,0:T(8,128)(2,1)S(1)}, u32[]{:S(2)}, u32[]{:S(2)}) collective-permute-start(bf16[8,768,128]{2,1,0:T(8,128)(2,1)} %copy-done.7), channel_id=1, source_target_pairs={{0,8},{4,12},{8,24},{12,28},{24,16},{28,20},{16,0},{20,4},{1,9},{5... | collective-permute-start | bytes 4718600 | tf_op jit(solution)/shard_map/ppermute | solution.py:54
  198.6 4.2 %collective-permute-start.40 = (f32[2,3,128,128]{3,2,1,0:T(8,128)}, f32[2,3,128,128]{3,2,1,0:T(8,128)S(1)}, u32[]{:S(2)}, u32[]{:S(2)}) collective-permute-start(f32[2,3,128,128]{3,2,1,0:T(8,128)} %get-tuple-element.108), channel_id=1, source_target_pairs={{0,1},{1,0},{2,3},{3,2},{4,5},{5,4},{6,7},{7,6},{8,9},{9,8},{10,11... | collective-permute-start | bytes 1179656 | tf_op jit(solution)/shard_map/ppermute | solution.py:62
  198.6 4.8 %collective-permute-start.41 = (f32[2,3,128,128]{3,2,1,0:T(8,128)}, f32[2,3,128,128]{3,2,1,0:T(8,128)S(1)}, u32[]{:S(2)}, u32[]{:S(2)}) collective-permute-start(f32[2,3,128,128]{3,2,1,0:T(8,128)} %get-tuple-element.109), channel_id=1, source_target_pairs={{0,1},{1,0},{2,3},{3,2},{4,5},{5,4},{6,7},{7,6},{8,9},{9,8},{10,11... | collective-permute-start | bytes 1179656 | tf_op jit(solution)/shard_map/ppermute | solution.py:62
  200.2 12.0 %collective-permute-start.45 = (f32[2,3,128,128]{3,2,1,0:T(8,128)S(1)}, f32[2,3,128,128]{3,2,1,0:T(8,128)S(1)}, u32[]{:S(2)}, u32[]{:S(2)}) collective-permute-start(f32[2,3,128,128]{3,2,1,0:T(8,128)S(1)} %add.278), channel_id=1, source_target_pairs={{0,2},{1,3},{2,0},{3,1},{4,6},{5,7},{6,4},{7,5},{8,10},{9,11},{10,... | collective-permute-start | bytes 1179656 | tf_op jit(solution)/shard_map/ppermute | solution.py:58
  202.9 16.9 %collective-permute-start.43 = (f32[2,3,128,128]{3,2,1,0:T(8,128)S(1)}, f32[2,3,128,128]{3,2,1,0:T(8,128)S(1)}, u32[]{:S(2)}, u32[]{:S(2)}) collective-permute-start(f32[2,3,128,128]{3,2,1,0:T(8,128)S(1)} %add.277), channel_id=1, source_target_pairs={{0,2},{1,3},{2,0},{3,1},{4,6},{5,7},{6,4},{7,5},{8,10},{9,11},{10,... | collective-permute-start | bytes 1179656 | tf_op jit(solution)/shard_map/ppermute | solution.py:58
  203.4 25.8 %collective-permute-start.35 = (bf16[4,3,128,128]{3,2,1,0:T(8,128)(2,1)S(1)}, bf16[4,3,128,128]{3,2,1,0:T(8,128)(2,1)S(1)}, u32[]{:S(2)}, u32[]{:S(2)}) collective-permute-start(bf16[4,3,128,128]{3,2,1,0:T(8,128)(2,1)S(1)} %copy-done.30), channel_id=1, source_target_pairs={{0,1},{1,0},{2,3},{3,2},{4,5},{5,4},{6,7},{7,6},{8,9},{9,8},{10,11... | collective-permute-start | bytes 1179656 | tf_op jit(solution)/shard_map/ppermute | solution.py:62
  212.2 17.2 %collective-permute-start.38 = (bf16[4,3,128,128]{3,2,1,0:T(8,128)(2,1)S(1)}, bf16[4,3,128,128]{3,2,1,0:T(8,128)(2,1)}, u32[]{:S(2)}, u32[]{:S(2)}) collective-permute-start(bf16[4,3,128,128]{3,2,1,0:T(8,128)(2,1)S(1)} %constant_dynamic-update-slice_fusion.rest_13_), channel_id=1, source_target_pairs={{0,1},{1,0},{2,3},{3,2},{4,5},{5,4},{6,7},{7,6},{8,9},{9,8},{10,11... | collective-permute-start | bytes 1179656 | tf_op jit(solution)/shard_map/ppermute | solution.py:62
  219.8 10.0 %collective-permute-start.36 = (bf16[4,3,128,128]{3,2,1,0:T(8,128)(2,1)S(1)}, bf16[4,3,128,128]{3,2,1,0:T(8,128)(2,1)}, u32[]{:S(2)}, u32[]{:S(2)}) collective-permute-start(bf16[4,3,128,128]{3,2,1,0:T(8,128)(2,1)S(1)} %collective-permute-done.34.rest_10_), channel_id=1, source_target_pairs={{0,1},{1,0},{2,3},{3,2},{4,5},{5,4},{6,7},{7,6},{8,9},{9,8},{10,11... | collective-permute-start | bytes 1179656 | tf_op jit(solution)/shard_map/ppermute | solution.py:62
  219.8 11.8 %collective-permute-start.39 = (bf16[4,3,128,128]{3,2,1,0:T(8,128)(2,1)S(1)}, bf16[4,3,128,128]{3,2,1,0:T(8,128)(2,1)S(1)}, u32[]{:S(2)}, u32[]{:S(2)}) collective-permute-start(bf16[4,3,128,128]{3,2,1,0:T(8,128)(2,1)S(1)} %collective-permute-done.37.rest_14_), channel_id=1, source_target_pairs={{0,1},{1,0},{2,3},{3,2},{4,5},{5,4},{6,7},{7,6},{8,9},{9,8},{10,11... | collective-permute-start | bytes 1179656 | tf_op jit(solution)/shard_map/ppermute | solution.py:62
  229.2 4.0 %collective-permute-start.49 = (f32[2,2,128,128]{3,2,1,0:T(8,128)}, f32[2,2,128,128]{3,2,1,0:T(8,128)S(1)}, u32[]{:S(2)}, u32[]{:S(2)}) collective-permute-start(f32[2,2,128,128]{3,2,1,0:T(8,128)} %get-tuple-element.121), channel_id=1, source_target_pairs={{0,1},{1,0},{2,3},{3,2},{4,5},{5,4},{6,7},{7,6},{8,9},{9,8},{10,11... | collective-permute-start | bytes 786440 | tf_op jit(solution)/shard_map/ppermute | solution.py:62
  229.4 3.8 %collective-permute-start.48 = (f32[2,2,128,128]{3,2,1,0:T(8,128)}, f32[2,2,128,128]{3,2,1,0:T(8,128)S(1)}, u32[]{:S(2)}, u32[]{:S(2)}) collective-permute-start(f32[2,2,128,128]{3,2,1,0:T(8,128)} %get-tuple-element.119), channel_id=1, source_target_pairs={{0,1},{1,0},{2,3},{3,2},{4,5},{5,4},{6,7},{7,6},{8,9},{9,8},{10,11... | collective-permute-start | bytes 786440 | tf_op jit(solution)/shard_map/ppermute | solution.py:62
  229.8 14.1 %collective-permute-start.46 = (bf16[4,2,128,128]{3,2,1,0:T(8,128)(2,1)S(1)}, bf16[4,2,128,128]{3,2,1,0:T(8,128)(2,1)S(1)}, u32[]{:S(2)}, u32[]{:S(2)}) collective-permute-start(bf16[4,2,128,128]{3,2,1,0:T(8,128)(2,1)S(1)} %copy-done.54), channel_id=1, source_target_pairs={{0,20},{4,16},{8,4},{12,0},{24,12},{28,8},{16,28},{20,24},{1,21},{... | collective-permute-start | bytes 786440 | tf_op jit(solution)/shard_map/ppermute | solution.py:54
  231.6 15.0 %collective-permute-start.59 = (bf16[4,2,128,128]{3,2,1,0:T(8,128)(2,1)S(1)}, bf16[4,2,128,128]{3,2,1,0:T(8,128)(2,1)S(1)}, u32[]{:S(2)}, u32[]{:S(2)}) collective-permute-start(bf16[4,2,128,128]{3,2,1,0:T(8,128)(2,1)S(1)} %slice.51.rest_17_), channel_id=1, source_target_pairs={{0,2},{1,3},{2,0},{3,1},{4,6},{5,7},{6,4},{7,5},{8,10},{9,11},{10,... | collective-permute-start | bytes 786440 | tf_op jit(solution)/shard_map/ppermute | solution.py:58
  233.2 14.9 %collective-permute-start.52 = (f32[2,2,128,128]{3,2,1,0:T(8,128)}, f32[2,2,128,128]{3,2,1,0:T(8,128)S(1)}, u32[]{:S(2)}, u32[]{:S(2)}) collective-permute-start(f32[2,2,128,128]{3,2,1,0:T(8,128)} %get-tuple-element.126), channel_id=1, source_target_pairs={{0,1},{1,0},{2,3},{3,2},{4,5},{5,4},{6,7},{7,6},{8,9},{9,8},{10,11... | collective-permute-start | bytes 786440 | tf_op jit(solution)/shard_map/ppermute | solution.py:62
  233.2 10.7 %collective-permute-start.47 = (bf16[4,1,128,128]{3,2,1,0:T(8,128)(2,1)S(1)}, bf16[4,1,128,128]{3,2,1,0:T(8,128)(2,1)S(1)}, u32[]{:S(2)}, u32[]{:S(2)}) collective-permute-start(bf16[4,1,128,128]{3,2,1,0:T(8,128)(2,1)S(1)} %copy-done.55), channel_id=1, source_target_pairs={{0,24},{4,28},{8,16},{12,20},{24,0},{28,4},{16,8},{20,12},{1,25},{... | collective-permute-start | bytes 393224 | tf_op jit(solution)/shard_map/ppermute | solution.py:54
  243.9 7.2 %collective-permute-start.53 = (f32[2,2,128,128]{3,2,1,0:T(8,128)S(1)}, f32[2,2,128,128]{3,2,1,0:T(8,128)S(1)}, u32[]{:S(2)}, u32[]{:S(2)}) collective-permute-start(f32[2,2,128,128]{3,2,1,0:T(8,128)S(1)} %copy-done.53), channel_id=1, source_target_pairs={{0,1},{1,0},{2,3},{3,2},{4,5},{5,4},{6,7},{7,6},{8,9},{9,8},{10,11... | collective-permute-start | bytes 786440 | tf_op jit(solution)/shard_map/ppermute | solution.py:62
  243.9 9.2 %collective-permute-start.55 = (f32[2,2,128,128]{3,2,1,0:T(8,128)S(1)}, f32[2,2,128,128]{3,2,1,0:T(8,128)S(1)}, u32[]{:S(2)}, u32[]{:S(2)}) collective-permute-start(f32[2,2,128,128]{3,2,1,0:T(8,128)S(1)} %add.280), channel_id=1, source_target_pairs={{0,2},{1,3},{2,0},{3,1},{4,6},{5,7},{6,4},{7,5},{8,10},{9,11},{10,... | collective-permute-start | bytes 786440 | tf_op jit(solution)/shard_map/ppermute | solution.py:58
  245.5 12.7 %collective-permute-start.54 = (f32[2,2,128,128]{3,2,1,0:T(8,128)S(1)}, f32[2,2,128,128]{3,2,1,0:T(8,128)S(1)}, u32[]{:S(2)}, u32[]{:S(2)}) collective-permute-start(f32[2,2,128,128]{3,2,1,0:T(8,128)S(1)} %add.279), channel_id=1, source_target_pairs={{0,2},{1,3},{2,0},{3,1},{4,6},{5,7},{6,4},{7,5},{8,10},{9,11},{10,... | collective-permute-start | bytes 786440 | tf_op jit(solution)/shard_map/ppermute | solution.py:58
  246.6 30.1 %collective-permute-start.50 = (bf16[4,768,128]{2,1,0:T(8,128)(2,1)S(1)}, bf16[4,768,128]{2,1,0:T(8,128)(2,1)S(1)}, u32[]{:S(2)}, u32[]{:S(2)}) collective-permute-start(bf16[4,768,128]{2,1,0:T(8,128)(2,1)S(1)} %slice.48), channel_id=1, source_target_pairs={{0,4},{4,0},{8,12},{12,8},{24,28},{28,24},{16,20},{20,16},{1,5},{5... | collective-permute-start | bytes 2359304 | tf_op jit(solution)/shard_map/ppermute | solution.py:54
  248.1 28.7 %collective-permute-start.51 = (bf16[4,768,128]{2,1,0:T(8,128)(2,1)S(1)}, bf16[4,768,128]{2,1,0:T(8,128)(2,1)S(1)}, u32[]{:S(2)}, u32[]{:S(2)}) collective-permute-start(bf16[4,768,128]{2,1,0:T(8,128)(2,1)S(1)} %slice.49), channel_id=1, source_target_pairs={{0,8},{4,12},{8,24},{12,28},{24,16},{28,20},{16,0},{20,4},{1,9},{5... | collective-permute-start | bytes 2359304 | tf_op jit(solution)/shard_map/ppermute | solution.py:54
  251.1 8.8 %collective-permute-start.60 = (bf16[4,2,128,128]{3,2,1,0:T(8,128)(2,1)S(1)}, bf16[4,2,128,128]{3,2,1,0:T(8,128)(2,1)S(1)}, u32[]{:S(2)}, u32[]{:S(2)}) collective-permute-start(bf16[4,2,128,128]{3,2,1,0:T(8,128)(2,1)S(1)} %slice.51.rest_17_), channel_id=1, source_target_pairs={{0,1},{1,0},{2,3},{3,2},{4,5},{5,4},{6,7},{7,6},{8,9},{9,8},{10,11... | collective-permute-start | bytes 786440 | tf_op jit(solution)/shard_map/ppermute | solution.py:62
  253.1 6.8 %collective-permute-start.61 = (bf16[4,2,128,128]{3,2,1,0:T(8,128)(2,1)S(1)}, bf16[4,2,128,128]{3,2,1,0:T(8,128)(2,1)S(1)}, u32[]{:S(2)}, u32[]{:S(2)}) collective-permute-start(bf16[4,2,128,128]{3,2,1,0:T(8,128)(2,1)S(1)} %collective-permute-done.59.rest_18_), channel_id=1, source_target_pairs={{0,1},{1,0},{2,3},{3,2},{4,5},{5,4},{6,7},{7,6},{8,9},{9,8},{10,11... | collective-permute-start | bytes 786440 | tf_op jit(solution)/shard_map/ppermute | solution.py:62
  258.3 22.1 %collective-permute-start.56 = (bf16[4,4,128,128]{3,2,1,0:T(8,128)(2,1)S(1)}, bf16[4,4,128,128]{3,2,1,0:T(8,128)(2,1)S(1)}, u32[]{:S(2)}, u32[]{:S(2)}) collective-permute-start(bf16[4,4,128,128]{3,2,1,0:T(8,128)(2,1)S(1)} %pad_maximum_fusion.rest_4_), channel_id=1, source_target_pairs={{0,2},{1,3},{2,0},{3,1},{4,6},{5,7},{6,4},{7,5},{8,10},{9,11},{10,... | collective-permute-start | bytes 1572872 | tf_op jit(solution)/shard_map/ppermute | solution.py:58
  276.7 12.1 %collective-permute-start.57 = (bf16[4,4,128,128]{3,2,1,0:T(8,128)(2,1)S(1)}, bf16[4,4,128,128]{3,2,1,0:T(8,128)(2,1)S(1)}, u32[]{:S(2)}, u32[]{:S(2)}) collective-permute-start(bf16[4,4,128,128]{3,2,1,0:T(8,128)(2,1)S(1)} %pad_maximum_fusion.rest_4_), channel_id=1, source_target_pairs={{0,1},{1,0},{2,3},{3,2},{4,5},{5,4},{6,7},{7,6},{8,9},{9,8},{10,11... | collective-permute-start | bytes 1572872 | tf_op jit(solution)/shard_map/ppermute | solution.py:62
  279.9 8.9 %collective-permute-start.62 = (bf16[4,2,128,128]{3,2,1,0:T(8,128)(2,1)}, bf16[4,2,128,128]{3,2,1,0:T(8,128)(2,1)S(1)}, u32[]{:S(2)}, u32[]{:S(2)}) collective-permute-start(bf16[4,2,128,128]{3,2,1,0:T(8,128)(2,1)} %amplitudes.7.rest_8_), channel_id=1, source_target_pairs={{0,2},{1,3},{2,0},{3,1},{4,6},{5,7},{6,4},{7,5},{8,10},{9,11},{10,... | collective-permute-start | bytes 786440 | tf_op jit(solution)/shard_map/ppermute | solution.py:58
  280.4 9.9 %collective-permute-start.58 = (bf16[4,4,128,128]{3,2,1,0:T(8,128)(2,1)S(1)}, bf16[4,4,128,128]{3,2,1,0:T(8,128)(2,1)S(1)}, u32[]{:S(2)}, u32[]{:S(2)}) collective-permute-start(bf16[4,4,128,128]{3,2,1,0:T(8,128)(2,1)S(1)} %collective-permute-done.56.rest_5_), channel_id=1, source_target_pairs={{0,1},{1,0},{2,3},{3,2},{4,5},{5,4},{6,7},{7,6},{8,9},{9,8},{10,11... | collective-permute-start | bytes 1572872 | tf_op jit(solution)/shard_map/ppermute | solution.py:62
  280.6 8.2 %collective-permute-start.63 = (bf16[4,2,128,128]{3,2,1,0:T(8,128)(2,1)}, bf16[4,2,128,128]{3,2,1,0:T(8,128)(2,1)S(1)}, u32[]{:S(2)}, u32[]{:S(2)}) collective-permute-start(bf16[4,2,128,128]{3,2,1,0:T(8,128)(2,1)} %amplitudes.7.rest_8_), channel_id=1, source_target_pairs={{0,1},{1,0},{2,3},{3,2},{4,5},{5,4},{6,7},{7,6},{8,9},{9,8},{10,11... | collective-permute-start | bytes 786440 | tf_op jit(solution)/shard_map/ppermute | solution.py:62
  (61 other events, 707.8 us)
